TPU v7x, 512 devices: a whole 4x8x8 slice. The times are simulated.
512 devices in a mesh: dp: 32 (over y, x), ctx: 16 (over z, core).
Axes of the slice: x: 4, y: 8, z: 8, core: 2. Of those that a mesh axis runs over, the one named last changes fastest.
Arguments:
- tokens: bfloat16 [65536, 2048], P(('dp', 'ctx')), parts along dimension 0, may hold values from -64 to 64
- query_weight: bfloat16 [2048, 2048], P(None, 'ctx'), may hold values from -0.125 to 0.125
- key_matrix: bfloat16 [2048, 256], replicated, may hold values from -0.125 to 0.125
- value_matrix: bfloat16 [2048, 256], replicated, may hold values from -0.125 to 0.125
- doc_lengths: int32 [512], P('dp'), parts along dimension 0, may hold values from 64 to 512, as said below
Outputs:
- attended: bfloat16 [65536, 2048], P(('dp', 'ctx')), parts along dimension 0
There are 32 independent parts, one for each index of `dp`. A program takes and returns all parts, laid end to end along the dimension named above; an argument that names none is the same for every part. Nothing has to cross between parts.
Inputs may be any that keep to these rules, and one draw needn't show every extreme that they name: `doc_lengths`: lengths of the 16 documents packed in order into the 2048 tokens of a group; they sum to 2048 and the longest has exactly 512 tokens.
All inputs are finite; a program needn't handle non-finite values.
Results may differ from a plain program's by a relative error of at most 0.011.
Values may be sent and summed in bfloat16 or wider, within the bound.
No kernel may reach another device: no remote copies, remote signals or barrier semaphores. Data moves between devices by JAX's collectives and lax.ppermute only.
A program may use at most 64 MiB of HBM per device.

v0:
```python
import math

import jax
import jax.numpy as jnp
from jax import lax
from jax.sharding import PartitionSpec as P

QUERY_HEADS = 16
KEY_VALUE_HEADS = 2
HEAD_SIZE = 128


NEG = -1e30


def from_behind(value, axis, steps):
    count = lax.axis_size(axis)
    leading, last = (max(0, -steps), min(count, count - steps))
    return lax.ppermute(value, axis, [(source, source + steps) for source in range(leading, last)])


def doc_range(ends, first, token_amount):
    positions = first + jnp.arange(token_amount, dtype=jnp.int32)
    return jnp.sum((positions[:, None] >= ends[None, :]).astype(jnp.int32), axis=1)


def attend(carry, query_fourfold, query_docs, key_block, value_block, key_docs):
    scale = 1.0 / math.sqrt(query_fourfold.shape[-1])

    def work(state):
        highest, summed, mixed = state
        scores = (
            jnp.einsum(
                "qkgd,mkd->kgqm", query_fourfold, key_block, preferred_element_type=jnp.float32
            )
            * scale
        )
        allowed = (query_docs[:, None] == key_docs[None, :])[None, None]
        scores = jnp.where(allowed, scores, NEG)
        new_high = jnp.maximum(highest, jnp.max(scores, axis=-1))
        weights = jnp.where(allowed, jnp.exp(scores - new_high[..., None]), 0.0)
        keep = jnp.exp(highest - new_high)
        summed = summed * keep + jnp.sum(weights, axis=-1)
        mixed = mixed * keep[..., None] + jnp.einsum(
            "kgqm,mkd->kgqd",
            weights.astype(jnp.bfloat16),
            value_block,
            preferred_element_type=jnp.float32,
        )
        return (new_high, summed, mixed)

    touch = jnp.logical_and(query_docs[0] <= key_docs[-1], key_docs[0] <= query_docs[-1])
    return lax.cond(touch, work, lambda state: state, carry)


def sweep_keys(carry, query_fourfold, query_docs, key_rows, value_rows, ends, start, present):
    token_amount = key_rows.shape[0]
    kv_heads = key_rows.shape[1]
    stride = math.gcd(token_amount, 512)
    pieces = token_amount // stride
    key_blocks = key_rows.reshape(pieces, stride, kv_heads, HEAD_SIZE)
    value_blocks = value_rows.reshape(pieces, stride, kv_heads, HEAD_SIZE)

    def step(state, items):
        key_block, value_block, number = items
        key_docs = jnp.where(present, doc_range(ends, start + number * stride, stride), -1)
        return (attend(state, query_fourfold, query_docs, key_block, value_block, key_docs), None)

    carry, unused = lax.scan(
        step, carry, (key_blocks, value_blocks, jnp.arange(pieces, dtype=jnp.int32))
    )
    return carry


def initial_state(kv_heads, head_group, token_rows):
    return (
        jnp.full((kv_heads, head_group, token_rows), NEG, jnp.float32),
        jnp.zeros((kv_heads, head_group, token_rows), jnp.float32),
        jnp.zeros((kv_heads, head_group, token_rows, HEAD_SIZE), jnp.float32),
    )


def finish(state, token_rows):
    highest, summed, mixed = state
    result = (mixed / summed[..., None]).astype(jnp.bfloat16)
    return jnp.transpose(result, (2, 0, 1, 3)).reshape(
        token_rows, result.shape[0] * result.shape[1] * HEAD_SIZE
    )


def body(tokens, query_weight, key_matrix, value_matrix, doc_lengths):
    token_rows = tokens.shape[0]
    count = lax.axis_size("ctx")
    index = lax.axis_index("ctx")
    head_group = QUERY_HEADS // KEY_VALUE_HEADS
    ends = jnp.cumsum(doc_lengths)
    query_matrix = jnp.dot(
        tokens,
        lax.all_gather(query_weight, "ctx", axis=1, tiled=True),
        preferred_element_type=jnp.float32,
    ).astype(jnp.bfloat16)
    key_rows = jnp.dot(tokens, key_matrix, preferred_element_type=jnp.float32).astype(jnp.bfloat16)
    value_rows = jnp.dot(tokens, value_matrix, preferred_element_type=jnp.float32).astype(
        jnp.bfloat16
    )
    query_fourfold = query_matrix.reshape(token_rows, KEY_VALUE_HEADS, head_group, HEAD_SIZE)
    query_docs = doc_range(ends, index * token_rows, token_rows)
    stacked = jnp.stack([key_rows, value_rows])
    state = initial_state(KEY_VALUE_HEADS, head_group, token_rows)
    state = sweep_keys(
        state,
        query_fourfold,
        query_docs,
        key_rows.reshape(token_rows, KEY_VALUE_HEADS, HEAD_SIZE),
        value_rows.reshape(token_rows, KEY_VALUE_HEADS, HEAD_SIZE),
        ends,
        index * token_rows,
        True,
    )
    reach = count // 4
    distances = []
    for offset in range(1, reach + 1):
        distances.append(offset)
        distances.append(-offset)
    for offset in distances:
        arrived = from_behind(stacked, "ctx", offset)
        source = index - offset
        present = jnp.logical_and(source >= 0, source < count)
        state = sweep_keys(
            state,
            query_fourfold,
            query_docs,
            arrived[0].reshape(token_rows, KEY_VALUE_HEADS, HEAD_SIZE),
            arrived[1].reshape(token_rows, KEY_VALUE_HEADS, HEAD_SIZE),
            ends,
            source * token_rows,
            present,
        )
    attended = finish(state, token_rows)
    return attended


def solution(mesh):
    in_specs = (P(("dp", "ctx"), None), P(None, "ctx"), P(), P(), P("dp"))
    out_specs = P(("dp", "ctx"), None)
    return jax.shard_map(body, mesh=mesh, in_specs=in_specs, out_specs=out_specs, check_vma=False)
```

profile of v0, /device:TPU:127, one launch (start us, length us, event | category | flops | bytes accessed | tf_op | source)
XLA Modules:
  0.0 118.5 jit_solution(12996614212056619913)
XLA Ops:
  6.5 0.7 all-gather.2.cloned.1.call-update
  7.3 0.5 copy-done
  7.8 1.3 %convolution_convert_fusion.2 = bf16[128,256]{1,0:T(8,128)(2,1)S(1)} fusion(bf16[128,2048]{1,0:T(8,128)(2,1)} %param.23, bf16[2048,256]{1,0:T(8,128)(2,1)S(1)} %copy-done), kind=kOutput, calls=%fused_computation.152 | convolution fusion | flops 134250496 | bytes 1638400 | tf_op jit(solution)/shard_map/dot_general | solution.py:102
  9.1 1.7 %convolution_convert_fusion.1 = bf16[128,256]{1,0:T(8,128)(2,1)S(1)} fusion(bf16[128,2048]{1,0:T(8,128)(2,1)} %param.23, bf16[2048,256]{1,0:T(8,128)(2,1)} %param.26), kind=kOutput, calls=%fused_computation.151 | convolution fusion | flops 134250496 | bytes 1638400 | tf_op jit(solution)/shard_map/dot_general | solution.py:103
  10.8 0.7 pad_maximum_fusion
  11.5 1.3 %collective-permute-start.7 = (bf16[2,128,256]{2,1,0:T(8,128)(2,1)}, bf16[2,128,256]{2,1,0:T(8,128)(2,1)}, u32[]{:S(2)}, u32[]{:S(2)}) collective-permute-start(bf16[2,128,256]{2,1,0:T(8,128)(2,1)} %pad_maximum_fusion), channel_id=1, source_target_pairs={{4,0},{5,1},{6,2},{7,3},{8,4},{9,5},{10,6},{11,7},{12,8},{13,9},{1... | collective-permute-start | bytes 393224 | tf_op jit(solution)/shard_map/ppermute | solution.py:19
  12.8 7.1 %collective-permute-start.6 = (bf16[2,128,256]{2,1,0:T(8,128)(2,1)}, bf16[2,128,256]{2,1,0:T(8,128)(2,1)}, u32[]{:S(2)}, u32[]{:S(2)}) collective-permute-start(bf16[2,128,256]{2,1,0:T(8,128)(2,1)} %pad_maximum_fusion), channel_id=1, source_target_pairs={{0,4},{1,5},{2,6},{3,7},{4,8},{5,9},{6,10},{7,11},{8,12},{9,13},{1... | collective-permute-start | bytes 393224 | tf_op jit(solution)/shard_map/ppermute | solution.py:19
  19.9 2.1 %collective-permute-start.5 = (bf16[2,128,256]{2,1,0:T(8,128)(2,1)}, bf16[2,128,256]{2,1,0:T(8,128)(2,1)S(1)}, u32[]{:S(2)}, u32[]{:S(2)}) collective-permute-start(bf16[2,128,256]{2,1,0:T(8,128)(2,1)} %pad_maximum_fusion), channel_id=1, source_target_pairs={{3,0},{4,1},{5,2},{6,3},{7,4},{8,5},{9,6},{10,7},{11,8},{12,9},{13... | collective-permute-start | bytes 393224 | tf_op jit(solution)/shard_map/ppermute | solution.py:19
  22.0 6.1 %collective-permute-start.4 = (bf16[2,128,256]{2,1,0:T(8,128)(2,1)}, bf16[2,128,256]{2,1,0:T(8,128)(2,1)S(1)}, u32[]{:S(2)}, u32[]{:S(2)}) collective-permute-start(bf16[2,128,256]{2,1,0:T(8,128)(2,1)} %pad_maximum_fusion), channel_id=1, source_target_pairs={{0,3},{1,4},{2,5},{3,6},{4,7},{5,8},{6,9},{7,10},{8,11},{9,12},{10... | collective-permute-start | bytes 393224 | tf_op jit(solution)/shard_map/ppermute | solution.py:19
  28.1 2.2 %collective-permute-start.3 = (bf16[2,128,256]{2,1,0:T(8,128)(2,1)}, bf16[2,128,256]{2,1,0:T(8,128)(2,1)S(1)}, u32[]{:S(2)}, u32[]{:S(2)}) collective-permute-start(bf16[2,128,256]{2,1,0:T(8,128)(2,1)} %pad_maximum_fusion), channel_id=1, source_target_pairs={{2,0},{3,1},{4,2},{5,3},{6,4},{7,5},{8,6},{9,7},{10,8},{11,9},{12,... | collective-permute-start | bytes 393224 | tf_op jit(solution)/shard_map/ppermute | solution.py:19
  30.4 0.7 copy.93
  31.1 0.1 reduce
  31.5 0.6 fusion.125
  32.2 0.6 fusion.126
  32.8 0.6 fusion.127
  33.4 0.6 fusion.128
  34.0 0.7 fusion.123
  34.7 0.7 fusion.130
  35.4 0.6 fusion.124
  43.8 0.6 fusion.129
  58.5 4.0 %collective-permute-start.2 = (bf16[2,128,256]{2,1,0:T(8,128)(2,1)}, bf16[2,128,256]{2,1,0:T(8,128)(2,1)S(1)}, u32[]{:S(2)}, u32[]{:S(2)}) collective-permute-start(bf16[2,128,256]{2,1,0:T(8,128)(2,1)} %pad_maximum_fusion), channel_id=1, source_target_pairs={{0,2},{1,3},{2,4},{3,5},{4,6},{5,7},{6,8},{7,9},{8,10},{9,11},{10,... | collective-permute-start | bytes 393224 | tf_op jit(solution)/shard_map/ppermute | solution.py:19
  62.6 1.9 %collective-permute-start.1 = (bf16[2,128,256]{2,1,0:T(8,128)(2,1)}, bf16[2,128,256]{2,1,0:T(8,128)(2,1)}, u32[]{:S(2)}, u32[]{:S(2)}) collective-permute-start(bf16[2,128,256]{2,1,0:T(8,128)(2,1)} %pad_maximum_fusion), channel_id=1, source_target_pairs={{1,0},{2,1},{3,2},{4,3},{5,4},{6,5},{7,6},{8,7},{9,8},{10,9},{11,1... | collective-permute-start | bytes 393224 | tf_op jit(solution)/shard_map/ppermute | solution.py:19
  64.6 3.6 %collective-permute-start = (bf16[2,128,256]{2,1,0:T(8,128)(2,1)}, bf16[2,128,256]{2,1,0:T(8,128)(2,1)}, u32[]{:S(2)}, u32[]{:S(2)}) collective-permute-start(bf16[2,128,256]{2,1,0:T(8,128)(2,1)} %pad_maximum_fusion), channel_id=1, source_target_pairs={{0,1},{1,2},{2,3},{3,4},{4,5},{5,6},{6,7},{7,8},{8,9},{9,10},{10,1... | collective-permute-start | bytes 393224 | tf_op jit(solution)/shard_map/ppermute | solution.py:19
  68.4 3.2 %collective-permute-done.1 = bf16[2,128,256]{2,1,0:T(8,128)(2,1)} collective-permute-done((bf16[2,128,256]{2,1,0:T(8,128)(2,1)}, bf16[2,128,256]{2,1,0:T(8,128)(2,1)}, u32[]{:S(2)}, u32[]{:S(2)}) %collective-permute-start.1) | collective-permute-done | bytes 131104 | tf_op jit(solution)/shard_map/ppermute | solution.py:19
  71.6 0.9 fusion.121
  72.5 1.5 %fusion.122 = (bf16[1,128,256]{2,1,0:T(8,128)(2,1)S(1)}, bf16[1,128,256]{2,1,0:T(8,128)(2,1)}) fusion(bf16[2,128,256]{2,1,0:T(8,128)(2,1)} %collective-permute-done), kind=kLoop, calls=%fused_computation.199 | loop fusion | bytes 262144 | tf_op jit(solution)/shard_map/slice | solution.py:134
  74.0 0.9 squeeze.170
  74.9 16.8 %all-gather.2.cloned.1.call-done = bf16[2048,2048]{1,0:T(8,128)(2,1)} async-done(((bf16[2048,128]{1,0:T(8,128)(2,1)}), bf16[2048,2048]{1,0:T(8,128)(2,1)}) %all-gather.2.cloned.1.call-update) | async-done | bytes 8388624 | tf_op jit(solution)/shard_map/all_gather | solution.py:99
  91.7 4.6 %fusion.104 = bf16[16,8,16,128]{3,1,2,0:T(8,128)(2,1)S(1)} fusion(bf16[128,2048]{1,0:T(8,128)(2,1)S(1)} %copy-done.1, bf16[2048,2048]{1,0:T(8,128)(2,1)} %all-gather.2.cloned.1.call-done), kind=kOutput, calls=%fused_computation.150 | convolution fusion | flops 1074003968 | bytes 9437184 | tf_op jit(solution)/shard_map/dot_general | solution.py:97
  96.3 0.1 copy.183
  96.5 2.1 %conditional.9 = ((f32[2,8,128]{2,1,0:T(8,128)S(1)}, f32[2,8,128]{2,1,0:T(8,128)S(1)}, f32[2,8,128,128]{3,2,1,0:T(8,128)S(1)})) conditional(s32[]{:T(128)} %bitcast.40, (f32[2,8,128]{2,1,0:T(8,128)S(1)}, f32[2,8,128]{2,1,0:T(8,128)S(1)}, f32[2,8,128,128]{3,2,1,0:T(8,128)S(1)}) %tuple.84, (s32[128]{0:T(128)}, bf16[128,2,128]{2,1,0:T(2,128)(2,1)S(1)}, ...), branch_computations={%region_10.11_spmd, %region_11.14_spmd} | conditional | flops 137121792 | bytes 6095392 | solution.py:53
  96.5 0.8 broadcast_compare_fusion
  97.3 0.3 fusion.106
  97.6 0.2 fusion.3
  97.8 0.7 convolution_add_fusion
  98.6 2.0 %conditional.10 = ((f32[2,8,128]{2,1,0:T(8,128)S(1)}, f32[2,8,128]{2,1,0:T(8,128)S(1)}, f32[2,8,128,128]{3,2,1,0:T(8,128)S(1)})) conditional(s32[]{:T(128)} %bitcast.39, (f32[2,8,128]{2,1,0:T(8,128)S(1)}, f32[2,8,128]{2,1,0:T(8,128)S(1)}, f32[2,8,128,128]{3,2,1,0:T(8,128)S(1)}) %get-tuple-element.984, (s32[128]{0:T(128)}, s32[128]{0:T(128)}, ...), branch_computations={%region_14.15_spmd, %region_15.18_spmd} | conditional | flops 137121792 | bytes 6095904 | solution.py:53
  98.6 0.8 broadcast_compare_fusion.1
  99.4 0.3 fusion.107
  99.7 0.2 fusion.15
  99.9 0.7 convolution_add_fusion.1
  100.6 2.0 %conditional.11 = ((f32[2,8,128]{2,1,0:T(8,128)S(1)}, f32[2,8,128]{2,1,0:T(8,128)S(1)}, f32[2,8,128,128]{3,2,1,0:T(8,128)S(1)})) conditional(s32[]{:T(128)} %bitcast.38, (f32[2,8,128]{2,1,0:T(8,128)S(1)}, f32[2,8,128]{2,1,0:T(8,128)S(1)}, f32[2,8,128,128]{3,2,1,0:T(8,128)S(1)}) %get-tuple-element.985, (s32[128]{0:T(128)}, s32[128]{0:T(128)}, ...), branch_computations={%region_18.19_spmd, %region_19.22_spmd} | conditional | flops 137121792 | bytes 6095904 | solution.py:53
  100.6 0.7 broadcast_compare_fusion.2
  101.4 0.3 fusion.108
  101.7 0.2 fusion.27
  101.9 0.7 convolution_add_fusion.2
  102.7 2.0 %conditional.13 = ((f32[2,8,128]{2,1,0:T(8,128)S(1)}, f32[2,8,128]{2,1,0:T(8,128)S(1)}, f32[2,8,128,128]{3,2,1,0:T(8,128)S(1)})) conditional(s32[]{:T(128)} %bitcast.36, (f32[2,8,128]{2,1,0:T(8,128)S(1)}, f32[2,8,128]{2,1,0:T(8,128)S(1)}, f32[2,8,128,128]{3,2,1,0:T(8,128)S(1)}) %get-tuple-element.987, (s32[128]{0:T(128)}, s32[128]{0:T(128)S(1)}, ...), branch_computations={%region_26.27_spmd, %region_27.30_spmd} | conditional | flops 137121792 | bytes 6095904 | solution.py:53
  102.7 0.7 broadcast_compare_fusion.4
  103.4 0.3 fusion.110
  103.8 0.2 fusion.51
  104.0 0.7 convolution_add_fusion.4
  104.7 2.2 %conditional.15 = ((f32[2,8,128]{2,1,0:T(8,128)S(1)}, f32[2,8,128]{2,1,0:T(8,128)S(1)}, f32[2,8,128,128]{3,2,1,0:T(8,128)S(1)})) conditional(s32[]{:T(128)} %bitcast.34, (f32[2,8,128]{2,1,0:T(8,128)S(1)}, f32[2,8,128]{2,1,0:T(8,128)S(1)}, f32[2,8,128,128]{3,2,1,0:T(8,128)S(1)}) %get-tuple-element.989, (s32[128]{0:T(128)}, s32[128]{0:T(128)S(1)}, ...), branch_computations={%region_34.35_spmd, %region_35.38_spmd} | conditional | flops 137121792 | bytes 6095904 | solution.py:53
  104.9 0.7 broadcast_compare_fusion.6
  105.6 0.3 fusion.112
  106.0 0.2 fusion.75
  106.2 0.7 convolution_add_fusion.6
  107.0 3.1 %conditional.17 = ((f32[2,8,128]{2,1,0:T(8,128)S(1)}, f32[2,8,128,128]{3,2,1,0:T(8,128)S(1)})) conditional(s32[]{:T(128)} %bitcast.32, (f32[2,8,128]{2,1,0:T(8,128)S(1)}, f32[2,8,128,128]{3,2,1,0:T(8,128)S(1)}) %tuple.93, (s32[128]{0:T(128)}, s32[128]{0:T(128)S(1)}, bf16[2,128,256]{2,1,0:T(8,128)(2,1)}, bf16[128,2,8,128]{3,2,1,0:T(8,128)(2,1)S(1)}, ...), branch_computations={%region_42.43_spmd, %region_43.46_spmd} | conditional | flops 137121792 | bytes 6603800 | solution.py:53
  107.0 0.7 broadcast_compare_fusion.8
  107.7 1.0 copy.117
  108.7 0.4 fusion.116
  109.1 0.2 fusion.97
  109.4 0.7 convolution_add_fusion.8
  110.0 0.3 fusion.105
  110.4 0.3 copy.119
  110.8 0.9 copy.264
  (98 shorter events, 0.9 us)
Async XLA Ops:
  6.5 1.2 %copy-start = (bf16[2048,256]{1,0:T(8,128)(2,1)S(1)}, bf16[2048,256]{1,0:T(8,128)(2,1)}, u32[]{:S(2)}) copy-start(bf16[2048,256]{1,0:T(8,128)(2,1)} %param.25) | copy-start | bytes 3145732
  6.5 85.2 %copy-start.1 = (bf16[128,2048]{1,0:T(8,128)(2,1)S(1)}, bf16[128,2048]{1,0:T(8,128)(2,1)}, u32[]{:S(2)}) copy-start(bf16[128,2048]{1,0:T(8,128)(2,1)} %param.23) | copy-start | bytes 1572868
  6.5 85.2 %all-gather.2.cloned.1.call-start = ((), (), s32[]{:S(2)}) async-start(), calls=%async_computation | async-start | bytes 8912896 | tf_op jit(solution)/shard_map/all_gather | solution.py:99
  11.5 95.5 %collective-permute-start.7 = (bf16[2,128,256]{2,1,0:T(8,128)(2,1)}, bf16[2,128,256]{2,1,0:T(8,128)(2,1)}, u32[]{:S(2)}, u32[]{:S(2)}) collective-permute-start(bf16[2,128,256]{2,1,0:T(8,128)(2,1)} %pad_maximum_fusion), channel_id=1, source_target_pairs={{4,0},{5,1},{6,2},{7,3},{8,4},{9,5},{10,6},{11,7},{12,8},{13,9},{1... | collective-permute-start | bytes 393224 | tf_op jit(solution)/shard_map/ppermute | solution.py:19
  12.8 94.1 %collective-permute-start.6 = (bf16[2,128,256]{2,1,0:T(8,128)(2,1)}, bf16[2,128,256]{2,1,0:T(8,128)(2,1)}, u32[]{:S(2)}, u32[]{:S(2)}) collective-permute-start(bf16[2,128,256]{2,1,0:T(8,128)(2,1)} %pad_maximum_fusion), channel_id=1, source_target_pairs={{0,4},{1,5},{2,6},{3,7},{4,8},{5,9},{6,10},{7,11},{8,12},{9,13},{1... | collective-permute-start | bytes 393224 | tf_op jit(solution)/shard_map/ppermute | solution.py:19
  19.9 38.6 %collective-permute-start.5 = (bf16[2,128,256]{2,1,0:T(8,128)(2,1)}, bf16[2,128,256]{2,1,0:T(8,128)(2,1)S(1)}, u32[]{:S(2)}, u32[]{:S(2)}) collective-permute-start(bf16[2,128,256]{2,1,0:T(8,128)(2,1)} %pad_maximum_fusion), channel_id=1, source_target_pairs={{3,0},{4,1},{5,2},{6,3},{7,4},{8,5},{9,6},{10,7},{11,8},{12,9},{13... | collective-permute-start | bytes 393224 | tf_op jit(solution)/shard_map/ppermute | solution.py:19
  22.0 40.6 %collective-permute-start.4 = (bf16[2,128,256]{2,1,0:T(8,128)(2,1)}, bf16[2,128,256]{2,1,0:T(8,128)(2,1)S(1)}, u32[]{:S(2)}, u32[]{:S(2)}) collective-permute-start(bf16[2,128,256]{2,1,0:T(8,128)(2,1)} %pad_maximum_fusion), channel_id=1, source_target_pairs={{0,3},{1,4},{2,5},{3,6},{4,7},{5,8},{6,9},{7,10},{8,11},{9,12},{10... | collective-permute-start | bytes 393224 | tf_op jit(solution)/shard_map/ppermute | solution.py:19
  28.1 36.5 %collective-permute-start.3 = (bf16[2,128,256]{2,1,0:T(8,128)(2,1)}, bf16[2,128,256]{2,1,0:T(8,128)(2,1)S(1)}, u32[]{:S(2)}, u32[]{:S(2)}) collective-permute-start(bf16[2,128,256]{2,1,0:T(8,128)(2,1)} %pad_maximum_fusion), channel_id=1, source_target_pairs={{2,0},{3,1},{4,2},{5,3},{6,4},{7,5},{8,6},{9,7},{10,8},{11,9},{12,... | collective-permute-start | bytes 393224 | tf_op jit(solution)/shard_map/ppermute | solution.py:19
  31.5 3.9 %copy-start.2 = (s32[128]{0:T(128)}, s32[128]{0:T(128)S(1)}, u32[]{:S(2)}) copy-start(s32[128]{0:T(128)S(1)} %get-tuple-element.853) | copy-start | bytes 1540
  31.5 1.2 %copy-start.7 = (s32[128]{0:T(128)}, s32[128]{0:T(128)S(1)}, u32[]{:S(2)}) copy-start(s32[128]{0:T(128)S(1)} %get-tuple-element.927) | copy-start | bytes 1540
  31.5 1.2 %copy-start.9 = (s32[128]{0:T(128)}, s32[128]{0:T(128)S(1)}, u32[]{:S(2)}) copy-start(s32[128]{0:T(128)S(1)} %get-tuple-element.926) | copy-start | bytes 1540
  32.8 2.6 %copy-start.3 = (s32[128]{0:T(128)}, s32[128]{0:T(128)S(1)}, u32[]{:S(2)}) copy-start(s32[128]{0:T(128)S(1)} %get-tuple-element.929) | copy-start | bytes 1540
  32.8 2.6 %copy-start.5 = (s32[128]{0:T(128)}, s32[128]{0:T(128)S(1)}, u32[]{:S(2)}) copy-start(s32[128]{0:T(128)S(1)} %get-tuple-element.928) | copy-start | bytes 1540
  34.0 1.4 %copy-start.11 = (s32[128]{0:T(128)}, s32[128]{0:T(128)S(1)}, u32[]{:S(2)}) copy-start(s32[128]{0:T(128)S(1)} %get-tuple-element.925) | copy-start | bytes 1540
  34.0 1.4 %copy-start.12 = (s32[128]{0:T(128)}, s32[128]{0:T(128)S(1)}, u32[]{:S(2)}) copy-start(s32[128]{0:T(128)S(1)} %get-tuple-element.924) | copy-start | bytes 1540
  34.7 0.7 copy-start.15
  35.4 23.0 %copy-start.13 = (s32[128]{0:T(128)}, s32[128]{0:T(128)S(1)}, u32[]{:S(2)}) copy-start(s32[128]{0:T(128)S(1)} %broadcast_select_fusion.6) | copy-start | bytes 1540
  58.5 9.8 %collective-permute-start.2 = (bf16[2,128,256]{2,1,0:T(8,128)(2,1)}, bf16[2,128,256]{2,1,0:T(8,128)(2,1)S(1)}, u32[]{:S(2)}, u32[]{:S(2)}) collective-permute-start(bf16[2,128,256]{2,1,0:T(8,128)(2,1)} %pad_maximum_fusion), channel_id=1, source_target_pairs={{0,2},{1,3},{2,4},{3,5},{4,6},{5,7},{6,8},{7,9},{8,10},{9,11},{10,... | collective-permute-start | bytes 393224 | tf_op jit(solution)/shard_map/ppermute | solution.py:19
  62.6 9.0 %collective-permute-start.1 = (bf16[2,128,256]{2,1,0:T(8,128)(2,1)}, bf16[2,128,256]{2,1,0:T(8,128)(2,1)}, u32[]{:S(2)}, u32[]{:S(2)}) collective-permute-start(bf16[2,128,256]{2,1,0:T(8,128)(2,1)} %pad_maximum_fusion), channel_id=1, source_target_pairs={{1,0},{2,1},{3,2},{4,3},{5,4},{6,5},{7,6},{8,7},{9,8},{10,9},{11,1... | collective-permute-start | bytes 393224 | tf_op jit(solution)/shard_map/ppermute | solution.py:19
  64.6 7.9 %collective-permute-start = (bf16[2,128,256]{2,1,0:T(8,128)(2,1)}, bf16[2,128,256]{2,1,0:T(8,128)(2,1)}, u32[]{:S(2)}, u32[]{:S(2)}) collective-permute-start(bf16[2,128,256]{2,1,0:T(8,128)(2,1)} %pad_maximum_fusion), channel_id=1, source_target_pairs={{0,1},{1,2},{2,3},{3,4},{4,5},{5,6},{6,7},{7,8},{8,9},{9,10},{10,1... | collective-permute-start | bytes 393224 | tf_op jit(solution)/shard_map/ppermute | solution.py:19
  98.5 4.1 %copy-start.10 = (s32[128]{0:T(128)S(1)}, s32[128]{0:T(128)}, u32[]{:S(2)}) copy-start(s32[128]{0:T(128)} %copy-done.9) | copy-start | bytes 1540
  98.6 4.1 %copy-start.8 = (s32[128]{0:T(128)S(1)}, s32[128]{0:T(128)}, u32[]{:S(2)}) copy-start(s32[128]{0:T(128)} %copy-done.7) | copy-start | bytes 1540
  100.6 4.1 %copy-start.6 = (s32[128]{0:T(128)S(1)}, s32[128]{0:T(128)}, u32[]{:S(2)}) copy-start(s32[128]{0:T(128)} %copy-done.5) | copy-start | bytes 1540
  102.6 2.1 %copy-start.4 = (s32[128]{0:T(128)S(1)}, s32[128]{0:T(128)}, u32[]{:S(2)}) copy-start(s32[128]{0:T(128)} %copy-done.3) | copy-start | bytes 1540
  102.7 4.2 %copy-start.14 = (s32[128]{0:T(128)S(1)}, s32[128]{0:T(128)}, u32[]{:S(2)}) copy-start(s32[128]{0:T(128)} %copy-done.13) | copy-start | bytes 1540
  104.7 2.3 %copy-start.16 = (s32[128]{0:T(128)S(1)}, s32[128]{0:T(128)}, u32[]{:S(2)}) copy-start(s32[128]{0:T(128)} %copy-done.15) | copy-start | bytes 1540
Sparse Core Ops, SparseCore 0:
  9.4 82.2 all-gather.1
where the time goes:
time: 119 us
  between operations  35.8 us (30%)
  starting transfers between devices  28.4 us (24%)
  waiting for transfers between devices  20.7 us (17%)
  matrix products  13.7 us (12%)
  local copies, waits for them, and re-layouts  12.3 us (10%)
  other arithmetic  7.04 us (6%)
    ppermute x8, starting transfers between devices, from_behind(): lax.ppermute(value, axis, [(source, source + steps) for source in range(l...  28.4 us
    all_gather x1, waiting for transfers between devices, body(): lax.all_gather(query_weight, 'ctx', axis=1, tiled=True)  16.8 us
    dot_general x1, matrix products, body(): jnp.dot(tokens, lax.all_gather(query_weight, 'ctx', axis=1, tiled=True),...  4.65 us
    eq x6, other arithmetic, work(): allowed = (query_docs[:, None] == key_docs[None, :])[None, None]  4.41 us
    slice x7, local copies, waits for them, and re-layouts, attend(): key_docs[0] <= query_docs[-1]  4.24 us
    dot_general x6, matrix products, work(): jnp.einsum('kgqm,mkd->kgqd', weights.astype(jnp.bfloat16), value_block, p...  4.06 us
    ppermute x8, waiting for transfers between devices, from_behind(): lax.ppermute(value, axis, [(source, source + steps) for source in range(l...  3.2 us
    slice x7, local copies, waits for them, and re-layouts, body(): arrived[1].reshape(token_rows, KEY_VALUE_HEADS, HEAD_SIZE)  2.43 us
  transfers between devices with their start and end apart: 9, of which 2 were waited for; matrix products, arithmetic and copies ran while one was open for 24% of the time, Pallas kernels for 0%

commit v1 on v0

v1 whole, which is shorter than its diff:
```python
import functools
import math

import jax
import jax.numpy as jnp
from jax import lax
from jax.experimental import pallas as pl
from jax.experimental.pallas import tpu as pltpu
from jax.sharding import PartitionSpec as P

QUERY_HEADS = 16
HEAD_SIZE = 128
WIDTH = 2048
ROWS = 128
NEG = -1e30

YS, XS, ZS, CORES = 8, 4, 8, 2
AXES = ("dp", "ctx")
ORDER = ((5, 3, 1, 7, 4, 2, 0, 6), (7, 3, 0, 6, 2, 4, 1, 5))


def flat(y, x, z, c):
    return (((y % YS) * XS + x % XS) * ZS + z % ZS) * CORES + c


def color_of(y, x, z):
    return (2 * x + 3 * y + z) % 8


def everyone():
    return [(y, x, z, c) for y in range(YS) for x in range(XS) for z in range(ZS) for c in range(CORES)]


def first_moves():
    pairs = []
    for y, x, z, c in everyone():
        head = 8 * c + ORDER[c][color_of(y, x, z)]
        pairs.append((flat(y, x, head // 2, head % 2), flat(y, x, z, c)))
    return pairs


def moves(step):
    pairs = []
    for y, x, z, c in everyone():
        dy, dx, dz = step(c)
        pairs.append((flat(y + dy, x + dx, z + dz, c), flat(y, x, z, c)))
    return pairs


def swap_cores():
    return [(flat(y, x, z, 1 - c), flat(y, x, z, c)) for y, x, z, c in everyone()]


def kv_kernel(core_ref, own_ref, other_ref, key_ref, value_ref, out_ref):
    for first, rows in ((0, own_ref), (ROWS, other_ref)):
        for column, matrix in ((0, key_ref), (HEAD_SIZE, value_ref)):
            out_ref[first : first + ROWS, column : column + HEAD_SIZE] = jnp.dot(
                rows[...], matrix[...], preferred_element_type=jnp.float32
            ).astype(jnp.bfloat16)


def kv_project(core, own, other, key_matrix, value_matrix):
    whole = pl.BlockSpec((ROWS, WIDTH), lambda i, s: (0, 0))
    mine = pl.BlockSpec((WIDTH, HEAD_SIZE), lambda i, s: (0, s[0]))
    return pl.pallas_call(
        kv_kernel,
        grid_spec=pltpu.PrefetchScalarGridSpec(
            num_scalar_prefetch=1,
            grid=(1,),
            in_specs=[whole, whole, mine, mine],
            out_specs=pl.BlockSpec((2 * ROWS, 2 * HEAD_SIZE), lambda i, s: (0, 0)),
        ),
        out_shape=jax.ShapeDtypeStruct((2 * ROWS, 2 * HEAD_SIZE), jnp.bfloat16),
        compiler_params=pltpu.CompilerParams(vmem_limit_bytes=24 * 2**20),
        cost_estimate=pl.CostEstimate(flops=2**28, bytes_accessed=2**21, transcendentals=0),
    )(core, own, other, key_matrix, value_matrix)


def head_kernel(pieces, *refs):
    slot_ref, own_ref, other_ref = refs[:3]
    weights = refs[3 : 3 + pieces]
    kv = refs[3 + pieces : 8 + pieces]
    row_docs, key_docs, held_ref, out_ref = refs[8 + pieces :]
    depth = WIDTH // pieces
    parts = []
    for rows in (own_ref, other_ref):
        total = None
        for i in range(pieces):
            term = jnp.dot(
                rows[:, i * depth : (i + 1) * depth], weights[i][...], preferred_element_type=jnp.float32
            )
            total = term if total is None else total + term
        parts.append(total.astype(jnp.bfloat16))
    queries = jnp.concatenate(parts, axis=0)
    factor = math.log2(math.e) / math.sqrt(HEAD_SIZE)
    docs = row_docs[...]
    scores = []
    for i in range(5):
        product = lax.dot_general(
            queries, kv[i][:, :HEAD_SIZE], (((1,), (1,)), ((), ())), preferred_element_type=jnp.float32
        )
        allowed = docs == key_docs[:, i * 2 * ROWS : (i + 1) * 2 * ROWS]
        scores.append(jnp.where(allowed, product, NEG))
    highest = functools.reduce(jnp.maximum, [jnp.max(s, axis=1, keepdims=True) for s in scores])
    summed, mixed = 0.0, 0.0
    for i in range(5):
        part = jnp.exp2((scores[i] - highest) * factor)
        summed = summed + jnp.sum(part, axis=1, keepdims=True)
        mixed = mixed + jnp.dot(
            part.astype(jnp.bfloat16), kv[i][:, HEAD_SIZE:], preferred_element_type=jnp.float32
        )
    out_ref[...] = (mixed / summed).astype(jnp.bfloat16)


def one_head(slot, own, other, weights, kv, row_docs, key_docs, held):
    def whole(array):
        return pl.BlockSpec(array.shape, lambda i, s: (0, 0))

    inputs = [own, other, *weights, *kv, row_docs, key_docs]
    return pl.pallas_call(
        functools.partial(head_kernel, len(weights)),
        grid_spec=pltpu.PrefetchScalarGridSpec(
            num_scalar_prefetch=1,
            grid=(1,),
            in_specs=[whole(a) for a in inputs] + [pl.BlockSpec(memory_space=pl.ANY)],
            out_specs=pl.BlockSpec((2 * ROWS, HEAD_SIZE), lambda i, s: (0, s[0])),
        ),
        out_shape=jax.ShapeDtypeStruct(held.shape, held.dtype),
        input_output_aliases={1 + len(inputs): 0},
        compiler_params=pltpu.CompilerParams(vmem_limit_bytes=32 * 2**20),
        cost_estimate=pl.CostEstimate(flops=2**28, bytes_accessed=2**21, transcendentals=2**18),
    )(slot, *inputs, held)


def join_kernel(core_ref, mine_ref, other_ref, out_ref):
    half = mine_ref.shape[1]
    core = core_ref[0]
    out_ref[:, pl.ds(pl.multiple_of(core * half, half), half)] = mine_ref[...]
    out_ref[:, pl.ds(pl.multiple_of((1 - core) * half, half), half)] = other_ref[...]


def join(core, held, arrived):
    half = held.shape[1]
    return pl.pallas_call(
        join_kernel,
        grid_spec=pltpu.PrefetchScalarGridSpec(
            num_scalar_prefetch=1,
            grid=(1,),
            in_specs=[pl.BlockSpec((ROWS, half), lambda i, s: (0, 0))] * 2,
            out_specs=pl.BlockSpec((ROWS, 2 * half), lambda i, s: (0, 0)),
        ),
        out_shape=jax.ShapeDtypeStruct((ROWS, 2 * half), held.dtype),
        compiler_params=pltpu.CompilerParams(vmem_limit_bytes=8 * 2**20),
    )(core, held, arrived)


def body(tokens, query_weight, key_matrix, value_matrix, doc_lengths):
    dp, ctx = lax.axis_index("dp"), lax.axis_index("ctx")
    y, x, z, c = dp // XS, dp % XS, ctx // CORES, ctx % CORES
    core = c.reshape(1).astype(jnp.int32)

    other = lax.ppermute(tokens, AXES, swap_cores())
    held_weight = lax.ppermute(query_weight, AXES, first_moves())
    kv = kv_project(core, tokens, other, key_matrix, value_matrix)

    around = (0, 1, -1, 2, -2)
    kv_all = [kv] + [lax.ppermute(kv, AXES, moves(lambda c, d=d: (0, 0, d))) for d in around[1:]]

    slots16 = jnp.arange(16, dtype=jnp.int32)
    ends = jnp.sum(jnp.where(slots16[:, None] <= slots16[None, :], doc_lengths[:, None], 0), axis=0)
    row = jnp.arange(2 * ROWS, dtype=jnp.int32)
    within = jnp.where(row < ROWS, row + ROWS * c, row - ROWS * c)
    key_positions = jnp.concatenate([within + 2 * ROWS * ((z + d) % ZS) for d in around])
    key_docs = jnp.sum((key_positions[None, :] >= ends[:, None]).astype(jnp.int32), axis=0, keepdims=True)
    row_docs = jnp.sum(
        ((within + 2 * ROWS * z)[:, None] >= ends[None, :]).astype(jnp.int32), axis=1, keepdims=True
    )

    half = WIDTH // 2
    low = lax.ppermute(held_weight[:half], AXES, moves(lambda c: (0, 2, 0)))
    high = lax.ppermute(held_weight[half:], AXES, moves(lambda c: (1, 0, 1) if c == 0 else (-1, 0, -1)))
    steps = ((2, (0, 1, 0)), (-2, (0, -1, 0)), (3, (1, 0, 0)), (-3, (-1, 0, 0)), (1, (0, 0, 1)), (-1, (0, 0, -1)))
    arrivals = [(0, [held_weight])]
    for shift, step in steps:
        arrivals.append((shift, [lax.ppermute(held_weight, AXES, moves(lambda c, step=step: step))]))
    arrivals.append((4, [low, high]))

    order = jnp.array(ORDER, jnp.int32)
    mine = jnp.where(c == 0, order[0], order[1])
    color = (2 * x + 3 * y + z) % 8
    held = jnp.zeros((2 * ROWS, WIDTH // 2), jnp.bfloat16)
    for shift, weights in arrivals:
        slot = lax.dynamic_slice(mine, ((color + shift) % 8,), (1,))
        held = one_head(slot, tokens, other, weights, kv_all, row_docs, key_docs, held)
    arrived = lax.ppermute(held[ROWS:], AXES, swap_cores())
    return join(core, held, arrived)


def solution(mesh):
    in_specs = (P(("dp", "ctx"), None), P(None, "ctx"), P(), P(), P("dp"))
    out_specs = P(("dp", "ctx"), None)
    return jax.shard_map(body, mesh=mesh, in_specs=in_specs, out_specs=out_specs, check_vma=False)
```

time: 119 us -> 108 us (0.908)
  the two profiles are of different devices: /device:TPU:127 before, /device:TPU:1 now
where the time goes in v1:
time: 108 us; the launch traced here: 106 us
  starting transfers between devices  74.3 us (69%)
  Pallas kernels  20.8 us (19%)
  local copies, waits for them, and re-layouts  5.9 us (5%)
  waiting for transfers between devices  4.45 us (4%)
    ppermute x6, starting transfers between devices, body(): lax.ppermute(held_weight, AXES, moves(lambda c, step=step: step))  29.6 us
    pallas_call x8, Pallas kernels, one_head(): pl.pallas_call(functools.partial(head_kernel, len(weights)), grid_spec=pl...  19.2 us
    ppermute x1, starting transfers between devices, body(): arrived = lax.ppermute(held[ROWS:], AXES, swap_cores())  12.1 us
    ppermute x4, starting transfers between devices, body(): lax.ppermute(kv, AXES, moves(lambda c, d=d: (0, 0, d)))  11.5 us
    ppermute x1, starting transfers between devices, body(): held_weight = lax.ppermute(query_weight, AXES, first_moves())  7.19 us
    ppermute x1, starting transfers between devices, body(): other = lax.ppermute(tokens, AXES, swap_cores())  7.15 us
    unnamed x14, local copies, waits for them, and re-layouts  4.14 us
    ppermute x1, starting transfers between devices, body(): lax.ppermute(held_weight[half:], AXES, moves(lambda c: (1, 0, 1) if c ==...  3.4 us
  transfers between devices with their start and end apart: 15, of which 2 were waited for; matrix products, arithmetic and copies ran while one was open for 2% of the time, Pallas kernels for 16%

profile of v1, /device:TPU:1, one launch (start us, length us, event | category | flops | bytes accessed | tf_op | source)
XLA Modules:
  0.0 106.4 jit_solution(5516456439957978095)
XLA Ops:
  0.0 7.2 %collective-permute-start.1 = (bf16[2048,128]{1,0:T(8,128)(2,1)}, bf16[2048,128]{1,0:T(8,128)(2,1)S(1)}, u32[]{:S(2)}, u32[]{:S(2)}) collective-permute-start(bf16[2048,128]{1,0:T(8,128)(2,1)} %param.7), channel_id=1, source_target_pairs={{5,0},{15,1},{3,2},{11,3},{1,4},{8,5},{7,6},{14,7},{4,8},{10,9},{2... | collective-permute-start | bytes 1572872 | tf_op jit(solution)/shard_map/ppermute | solution.py:163
  7.2 7.2 %collective-permute-start = (bf16[128,2048]{1,0:T(8,128)(2,1)}, bf16[128,2048]{1,0:T(8,128)(2,1)S(1)}, u32[]{:S(2)}, u32[]{:S(2)}) collective-permute-start(bf16[128,2048]{1,0:T(8,128)(2,1)} %refs_1_.15), channel_id=1, source_target_pairs={{1,0},{0,1},{3,2},{2,3},{5,4},{4,5},{7,6},{6,7},{9,8},{8,9},{11,10... | collective-permute-start | bytes 1572872 | tf_op jit(solution)/shard_map/ppermute | solution.py:162
  14.4 0.0 copy-start.4
  14.5 0.0 copy-start.5
  14.5 0.6 copy-done.4
  15.1 0.0 copy-done.5
  15.1 3.3 %collective-permute-done.1.refs_3_ = bf16[2048,128]{1,0:T(8,128)(2,1)S(1)} collective-permute-done((bf16[2048,128]{1,0:T(8,128)(2,1)}, bf16[2048,128]{1,0:T(8,128)(2,1)S(1)}, u32[]{:S(2)}, u32[]{:S(2)}) %collective-permute-start.1) | collective-permute-done | bytes 524320 | tf_op jit(solution)/shard_map/ppermute | solution.py:163
  18.4 15.6 %collective-permute-start.13 = (bf16[2048,128]{1,0:T(8,128)(2,1)S(1)}, bf16[2048,128]{1,0:T(8,128)(2,1)S(1)}, u32[]{:S(2)}, u32[]{:S(2)}) collective-permute-start(bf16[2048,128]{1,0:T(8,128)(2,1)S(1)} %collective-permute-done.1.refs_3_), channel_id=1, source_target_pairs={{16,0},{17,1},{18,2},{19,3},{20,4},{21,5},{22,6},{23,7},{24,8},{25... | collective-permute-start | bytes 1572872 | tf_op jit(solution)/shard_map/ppermute | solution.py:185
  34.0 0.0 collective-permute-done.other_ref.refs_2_
  34.0 0.0 copy-start
  34.0 1.0 copy-done
  35.1 0.0 copy-start.2
  35.1 1.2 %copy-done.2 = bf16[2048,256]{1,0:T(8,128)(2,1)S(1)} copy-done((bf16[2048,256]{1,0:T(8,128)(2,1)S(1)}, bf16[2048,256]{1,0:T(8,128)(2,1)}, u32[]{:S(2)}) %copy-start.2) | copy-done | bytes 1048600
  36.3 0.0 copy-start.3
  36.3 1.2 %copy-done.3 = bf16[2048,256]{1,0:T(8,128)(2,1)S(1)} copy-done((bf16[2048,256]{1,0:T(8,128)(2,1)S(1)}, bf16[2048,256]{1,0:T(8,128)(2,1)}, u32[]{:S(2)}) %copy-start.3) | copy-done | bytes 1048600
  37.5 0.8 shard_map.64.refs_4_.refs_5_
  38.3 2.1 %collective-permute-start.4 = (bf16[256,256]{1,0:T(8,128)(2,1)S(1)}, bf16[256,256]{1,0:T(8,128)(2,1)S(1)}, u32[]{:S(2)}, u32[]{:S(2)}) collective-permute-start(bf16[256,256]{1,0:T(8,128)(2,1)S(1)} %shard_map.64.refs_4_.refs_5_), channel_id=1, source_target_pairs={{2,0},{3,1},{4,2},{5,3},{6,4},{7,5},{8,6},{9,7},{10,8},{11,9},{12,... | collective-permute-start | bytes 393224 | tf_op jit(solution)/shard_map/ppermute | solution.py:167
  40.5 3.2 %collective-permute-start.5 = (bf16[256,256]{1,0:T(8,128)(2,1)S(1)}, bf16[256,256]{1,0:T(8,128)(2,1)S(1)}, u32[]{:S(2)}, u32[]{:S(2)}) collective-permute-start(bf16[256,256]{1,0:T(8,128)(2,1)S(1)} %shard_map.64.refs_4_.refs_5_), channel_id=1, source_target_pairs={{14,0},{15,1},{0,2},{1,3},{2,4},{3,5},{4,6},{5,7},{6,8},{7,9},{8,1... | collective-permute-start | bytes 393224 | tf_op jit(solution)/shard_map/ppermute | solution.py:167
  43.7 0.0 copy-start.6
  43.7 1.9 %collective-permute-start.6 = (bf16[256,256]{1,0:T(8,128)(2,1)S(1)}, bf16[256,256]{1,0:T(8,128)(2,1)S(1)}, u32[]{:S(2)}, u32[]{:S(2)}) collective-permute-start(bf16[256,256]{1,0:T(8,128)(2,1)S(1)} %shard_map.64.refs_4_.refs_5_), channel_id=1, source_target_pairs={{4,0},{5,1},{6,2},{7,3},{8,4},{9,5},{10,6},{11,7},{12,8},{13,9},{1... | collective-permute-start | bytes 393224 | tf_op jit(solution)/shard_map/ppermute | solution.py:167
  45.6 4.3 %collective-permute-start.7 = (bf16[256,256]{1,0:T(8,128)(2,1)S(1)}, bf16[256,256]{1,0:T(8,128)(2,1)S(1)}, u32[]{:S(2)}, u32[]{:S(2)}) collective-permute-start(bf16[256,256]{1,0:T(8,128)(2,1)S(1)} %shard_map.64.refs_4_.refs_5_), channel_id=1, source_target_pairs={{12,0},{13,1},{14,2},{15,3},{0,4},{1,5},{2,6},{3,7},{4,8},{5,9},{6... | collective-permute-start | bytes 393224 | tf_op jit(solution)/shard_map/ppermute | solution.py:167
  49.9 0.0 collective-permute-done.4.refs_5_.refs_6_
  49.9 1.9 %collective-permute-start.12 = (bf16[2048,128]{1,0:T(8,128)(2,1)S(1)}, bf16[2048,128]{1,0:T(8,128)(2,1)S(1)}, u32[]{:S(2)}, u32[]{:S(2)}) collective-permute-start(bf16[2048,128]{1,0:T(8,128)(2,1)S(1)} %collective-permute-done.1.refs_3_), channel_id=1, source_target_pairs={{48,0},{49,1},{50,2},{51,3},{52,4},{53,5},{54,6},{55,7},{56,8},{57... | collective-permute-start | bytes 1572872 | tf_op jit(solution)/shard_map/ppermute | solution.py:185
  51.8 0.0 collective-permute-done.5.refs_6_.refs_7_
  51.9 4.0 %collective-permute-start.11 = (bf16[2048,128]{1,0:T(8,128)(2,1)S(1)}, bf16[2048,128]{1,0:T(8,128)(2,1)}, u32[]{:S(2)}, u32[]{:S(2)}) collective-permute-start(bf16[2048,128]{1,0:T(8,128)(2,1)S(1)} %collective-permute-done.1.refs_3_), channel_id=1, source_target_pairs={{64,0},{65,1},{66,2},{67,3},{68,4},{69,5},{70,6},{71,7},{72,8},{73... | collective-permute-start | bytes 1572872 | tf_op jit(solution)/shard_map/ppermute | solution.py:185
  55.9 0.0 copy-done.6
  55.9 0.1 select_reduce_fusion
  56.0 0.0 collective-permute-done.6.refs_7_.refs_8_
  56.0 1.9 %collective-permute-start.10 = (bf16[2048,128]{1,0:T(8,128)(2,1)S(1)}, bf16[2048,128]{1,0:T(8,128)(2,1)}, u32[]{:S(2)}, u32[]{:S(2)}) collective-permute-start(bf16[2048,128]{1,0:T(8,128)(2,1)S(1)} %collective-permute-done.1.refs_3_), channel_id=1, source_target_pairs={{448,0},{449,1},{450,2},{451,3},{452,4},{453,5},{454,6},{455,7},{4... | collective-permute-start | bytes 1572872 | tf_op jit(solution)/shard_map/ppermute | solution.py:185
  57.9 0.0 collective-permute-done.7.refs_8_.refs_9_
  57.9 4.3 %collective-permute-start.9 = (bf16[2048,128]{1,0:T(8,128)(2,1)S(1)}, bf16[2048,128]{1,0:T(8,128)(2,1)}, u32[]{:S(2)}, u32[]{:S(2)}) collective-permute-start(bf16[2048,128]{1,0:T(8,128)(2,1)S(1)} %collective-permute-done.1.refs_3_), channel_id=1, source_target_pairs={{2,0},{3,1},{4,2},{5,3},{6,4},{7,5},{8,6},{9,7},{10,8},{11,9},{12,... | collective-permute-start | bytes 1572872 | tf_op jit(solution)/shard_map/ppermute | solution.py:185
  62.2 0.0 collective-permute-done.13.refs_3_
  62.3 1.9 %collective-permute-start.8 = (bf16[2048,128]{1,0:T(8,128)(2,1)S(1)}, bf16[2048,128]{1,0:T(8,128)(2,1)}, u32[]{:S(2)}, u32[]{:S(2)}) collective-permute-start(bf16[2048,128]{1,0:T(8,128)(2,1)S(1)} %collective-permute-done.1.refs_3_), channel_id=1, source_target_pairs={{14,0},{15,1},{0,2},{1,3},{2,4},{3,5},{4,6},{5,7},{6,8},{7,9},{8,1... | collective-permute-start | bytes 1572872 | tf_op jit(solution)/shard_map/ppermute | solution.py:185
  64.2 0.1 convert_reduce_fusion.1
  64.4 0.1 copy.30.refs_9_.refs_10_
  64.6 0.8 fusion
  65.4 0.0 copy-start.1
  65.4 0.0 collective-permute-done.12.refs_3_
  65.4 3.3 %collective-permute-start.2 = (bf16[1024,128]{1,0:T(8,128)(2,1)}, bf16[1024,128]{1,0:T(8,128)(2,1)}, u32[]{:S(2)}, u32[]{:S(2)}) collective-permute-start(bf16[1024,128]{1,0:T(8,128)(2,1)} %get-tuple-element.6), channel_id=1, source_target_pairs={{32,0},{33,1},{34,2},{35,3},{36,4},{37,5},{38,6},{39,7},{40,8},{41... | collective-permute-start | bytes 786440 | tf_op jit(solution)/shard_map/ppermute | solution.py:180
  68.7 0.0 collective-permute-done.11.refs_3_
  68.7 3.4 %collective-permute-start.3 = (bf16[1024,128]{1,0:T(8,128)(2,1)}, bf16[1024,128]{1,0:T(8,128)(2,1)}, u32[]{:S(2)}, u32[]{:S(2)}) collective-permute-start(bf16[1024,128]{1,0:T(8,128)(2,1)} %get-tuple-element.5), channel_id=1, source_target_pairs={{66,0},{463,1},{68,2},{449,3},{70,4},{451,5},{72,6},{453,7},{74,8}... | collective-permute-start | bytes 786440 | tf_op jit(solution)/shard_map/ppermute | solution.py:181
  72.1 0.1 convert_reduce_fusion
  72.3 0.7 constant_dynamic-slice_fusion.6
  73.0 0.1 broadcast_in_dim.32.refs_11_
  73.1 0.0 copy-done.1
  73.1 1.7 %shard_map.65.refs_11_ = bf16[256,1024]{1,0:T(8,128)(2,1)S(1)} custom-call(s32[1]{0:T(128)} %bitcast.9.refs_0_, bf16[128,2048]{1,0:T(8,128)(2,1)S(1)} %copy-done.1, bf16[128,2048]{1,0:T(8,128)(2,1)S(1)} %collective-permute-done.other_ref.refs_2_, bf16[2048,128]{1,0:T(8,128)(2,1)S(1)} %collective-permute-done.1.refs_3_, ...), custom_call_target="tpu_custom_call", output_to_operand_aliasing={{}: (11, {})} | custom-call | flops 268435456 | bytes 2097152 | tf_op jit(solution)/shard_map/pallas_call | solution.py:120
  74.8 1.7 %shard_map.66.refs_11_ = bf16[256,1024]{1,0:T(8,128)(2,1)S(1)} custom-call(s32[1]{0:T(128)} %bitcast.8.refs_0_, bf16[128,2048]{1,0:T(8,128)(2,1)S(1)} %copy-done.1, bf16[128,2048]{1,0:T(8,128)(2,1)S(1)} %collective-permute-done.other_ref.refs_2_, bf16[2048,128]{1,0:T(8,128)(2,1)S(1)} %collective-permute-done.13.refs_3_, ...), custom_call_target="tpu_custom_call", output_to_operand_aliasing={{}: (11, {})} | custom-call | flops 268435456 | bytes 2097152 | tf_op jit(solution)/shard_map/pallas_call | solution.py:120
  76.4 1.8 %shard_map.67.refs_11_ = bf16[256,1024]{1,0:T(8,128)(2,1)S(1)} custom-call(s32[1]{0:T(128)} %bitcast.7.refs_0_, bf16[128,2048]{1,0:T(8,128)(2,1)S(1)} %copy-done.1, bf16[128,2048]{1,0:T(8,128)(2,1)S(1)} %collective-permute-done.other_ref.refs_2_, bf16[2048,128]{1,0:T(8,128)(2,1)S(1)} %collective-permute-done.12.refs_3_, ...), custom_call_target="tpu_custom_call", output_to_operand_aliasing={{}: (11, {})} | custom-call | flops 268435456 | bytes 2097152 | tf_op jit(solution)/shard_map/pallas_call | solution.py:120
  78.2 2.9 %shard_map.68.refs_11_ = bf16[256,1024]{1,0:T(8,128)(2,1)S(1)} custom-call(s32[1]{0:T(128)} %bitcast.6.refs_0_, bf16[128,2048]{1,0:T(8,128)(2,1)S(1)} %copy-done.1, bf16[128,2048]{1,0:T(8,128)(2,1)S(1)} %collective-permute-done.other_ref.refs_2_, bf16[2048,128]{1,0:T(8,128)(2,1)} %collective-permute-done.11.refs_3_, ...), custom_call_target="tpu_custom_call", output_to_operand_aliasing={{}: (11, {})} | custom-call | flops 268435456 | bytes 2097152 | tf_op jit(solution)/shard_map/pallas_call | solution.py:120
  81.1 0.0 collective-permute-done.10.refs_3_
  81.1 2.8 %shard_map.69.refs_11_ = bf16[256,1024]{1,0:T(8,128)(2,1)S(1)} custom-call(s32[1]{0:T(128)} %bitcast.5.refs_0_, bf16[128,2048]{1,0:T(8,128)(2,1)S(1)} %copy-done.1, bf16[128,2048]{1,0:T(8,128)(2,1)S(1)} %collective-permute-done.other_ref.refs_2_, bf16[2048,128]{1,0:T(8,128)(2,1)} %collective-permute-done.10.refs_3_, ...), custom_call_target="tpu_custom_call", output_to_operand_aliasing={{}: (11, {})} | custom-call | flops 268435456 | bytes 2097152 | tf_op jit(solution)/shard_map/pallas_call | solution.py:120
  83.9 0.0 collective-permute-done.9.refs_3_
  83.9 2.7 %shard_map.70.refs_11_ = bf16[256,1024]{1,0:T(8,128)(2,1)S(1)} custom-call(s32[1]{0:T(128)} %bitcast.4.refs_0_, bf16[128,2048]{1,0:T(8,128)(2,1)S(1)} %copy-done.1, bf16[128,2048]{1,0:T(8,128)(2,1)S(1)} %collective-permute-done.other_ref.refs_2_, bf16[2048,128]{1,0:T(8,128)(2,1)} %collective-permute-done.9.refs_3_, ...), custom_call_target="tpu_custom_call", output_to_operand_aliasing={{}: (11, {})} | custom-call | flops 268435456 | bytes 2097152 | tf_op jit(solution)/shard_map/pallas_call | solution.py:120
  86.6 0.0 collective-permute-done.8.refs_3_
  86.7 2.7 %shard_map.71.refs_12_ = bf16[256,1024]{1,0:T(8,128)(2,1)S(1)} custom-call(s32[1]{0:T(128)} %bitcast.3.refs_0_, bf16[128,2048]{1,0:T(8,128)(2,1)S(1)} %copy-done.1, bf16[128,2048]{1,0:T(8,128)(2,1)S(1)} %collective-permute-done.other_ref.refs_2_, bf16[2048,128]{1,0:T(8,128)(2,1)} %collective-permute-done.8.refs_3_, ...), custom_call_target="tpu_custom_call", output_to_operand_aliasing={{}: (11, {})} | custom-call | flops 268435456 | bytes 2097152 | tf_op jit(solution)/shard_map/pallas_call | solution.py:120
  89.4 0.0 collective-permute-done.2.refs_3_
  89.4 0.0 collective-permute-done.3.refs_4_
  89.4 2.8 %shard_map.72.mine_ref = bf16[256,1024]{1,0:T(8,128)(2,1)S(1)} custom-call(s32[1]{0:T(128)} %bitcast.1.refs_0_, bf16[128,2048]{1,0:T(8,128)(2,1)S(1)} %copy-done.1, bf16[128,2048]{1,0:T(8,128)(2,1)S(1)} %collective-permute-done.other_ref.refs_2_, bf16[1024,128]{1,0:T(8,128)(2,1)} %collective-permute-done.2.refs_3_, ...), custom_call_target="tpu_custom_call", output_to_operand_aliasing={{}: (12, {})} | custom-call | flops 268435456 | bytes 2097152 | tf_op jit(solution)/shard_map/pallas_call | solution.py:120
  92.3 12.1 %collective-permute-start.14 = (bf16[128,1024]{1,0:T(8,128)(2,1)S(1)}, bf16[128,1024]{1,0:T(8,128)(2,1)S(1)}, u32[]{:S(2)}, u32[]{:S(2)}) collective-permute-start(bf16[128,1024]{1,0:T(8,128)(2,1)S(1)} %slice.22), channel_id=1, source_target_pairs={{1,0},{0,1},{3,2},{2,3},{5,4},{4,5},{7,6},{6,7},{9,8},{8,9},{11,10... | collective-permute-start | bytes 786440 | tf_op jit(solution)/shard_map/ppermute | solution.py:195
  104.4 1.1 %collective-permute-done.14.other_ref = bf16[128,1024]{1,0:T(8,128)(2,1)S(1)} collective-permute-done((bf16[128,1024]{1,0:T(8,128)(2,1)S(1)}, bf16[128,1024]{1,0:T(8,128)(2,1)S(1)}, u32[]{:S(2)}, u32[]{:S(2)}) %collective-permute-start.14) | collective-permute-done | bytes 262176 | tf_op jit(solution)/shard_map/ppermute | solution.py:195
  105.6 0.8 shard_map.73
  (9 shorter events, 0.1 us)
Async XLA Ops:
  0.0 18.4 %collective-permute-start.1 = (bf16[2048,128]{1,0:T(8,128)(2,1)}, bf16[2048,128]{1,0:T(8,128)(2,1)S(1)}, u32[]{:S(2)}, u32[]{:S(2)}) collective-permute-start(bf16[2048,128]{1,0:T(8,128)(2,1)} %param.7), channel_id=1, source_target_pairs={{5,0},{15,1},{3,2},{11,3},{1,4},{8,5},{7,6},{14,7},{4,8},{10,9},{2... | collective-permute-start | bytes 1572872 | tf_op jit(solution)/shard_map/ppermute | solution.py:163
  7.2 26.8 %collective-permute-start = (bf16[128,2048]{1,0:T(8,128)(2,1)}, bf16[128,2048]{1,0:T(8,128)(2,1)S(1)}, u32[]{:S(2)}, u32[]{:S(2)}) collective-permute-start(bf16[128,2048]{1,0:T(8,128)(2,1)} %refs_1_.15), channel_id=1, source_target_pairs={{1,0},{0,1},{3,2},{2,3},{5,4},{4,5},{7,6},{6,7},{9,8},{8,9},{11,10... | collective-permute-start | bytes 1572872 | tf_op jit(solution)/shard_map/ppermute | solution.py:162
  14.4 0.7 copy-start.4
  14.5 0.7 copy-start.5
  18.4 43.9 %collective-permute-start.13 = (bf16[2048,128]{1,0:T(8,128)(2,1)S(1)}, bf16[2048,128]{1,0:T(8,128)(2,1)S(1)}, u32[]{:S(2)}, u32[]{:S(2)}) collective-permute-start(bf16[2048,128]{1,0:T(8,128)(2,1)S(1)} %collective-permute-done.1.refs_3_), channel_id=1, source_target_pairs={{16,0},{17,1},{18,2},{19,3},{20,4},{21,5},{22,6},{23,7},{24,8},{25... | collective-permute-start | bytes 1572872 | tf_op jit(solution)/shard_map/ppermute | solution.py:185
  34.0 1.0 copy-start
  35.1 1.2 %copy-start.2 = (bf16[2048,256]{1,0:T(8,128)(2,1)S(1)}, bf16[2048,256]{1,0:T(8,128)(2,1)}, u32[]{:S(2)}) copy-start(bf16[2048,256]{1,0:T(8,128)(2,1)} %key_ref.1) | copy-start | bytes 3145732
  36.3 1.2 %copy-start.3 = (bf16[2048,256]{1,0:T(8,128)(2,1)S(1)}, bf16[2048,256]{1,0:T(8,128)(2,1)}, u32[]{:S(2)}) copy-start(bf16[2048,256]{1,0:T(8,128)(2,1)} %value_ref.1) | copy-start | bytes 3145732
  38.3 11.6 %collective-permute-start.4 = (bf16[256,256]{1,0:T(8,128)(2,1)S(1)}, bf16[256,256]{1,0:T(8,128)(2,1)S(1)}, u32[]{:S(2)}, u32[]{:S(2)}) collective-permute-start(bf16[256,256]{1,0:T(8,128)(2,1)S(1)} %shard_map.64.refs_4_.refs_5_), channel_id=1, source_target_pairs={{2,0},{3,1},{4,2},{5,3},{6,4},{7,5},{8,6},{9,7},{10,8},{11,9},{12,... | collective-permute-start | bytes 393224 | tf_op jit(solution)/shard_map/ppermute | solution.py:167
  40.5 11.4 %collective-permute-start.5 = (bf16[256,256]{1,0:T(8,128)(2,1)S(1)}, bf16[256,256]{1,0:T(8,128)(2,1)S(1)}, u32[]{:S(2)}, u32[]{:S(2)}) collective-permute-start(bf16[256,256]{1,0:T(8,128)(2,1)S(1)} %shard_map.64.refs_4_.refs_5_), channel_id=1, source_target_pairs={{14,0},{15,1},{0,2},{1,3},{2,4},{3,5},{4,6},{5,7},{6,8},{7,9},{8,1... | collective-permute-start | bytes 393224 | tf_op jit(solution)/shard_map/ppermute | solution.py:167
  43.7 12.2 %copy-start.6 = (s32[16]{0:T(128)S(1)}, s32[16]{0:T(128)}, u32[]{:S(2)}) copy-start(s32[16]{0:T(128)} %param.10) | copy-start | bytes 196
  43.7 12.3 %collective-permute-start.6 = (bf16[256,256]{1,0:T(8,128)(2,1)S(1)}, bf16[256,256]{1,0:T(8,128)(2,1)S(1)}, u32[]{:S(2)}, u32[]{:S(2)}) collective-permute-start(bf16[256,256]{1,0:T(8,128)(2,1)S(1)} %shard_map.64.refs_4_.refs_5_), channel_id=1, source_target_pairs={{4,0},{5,1},{6,2},{7,3},{8,4},{9,5},{10,6},{11,7},{12,8},{13,9},{1... | collective-permute-start | bytes 393224 | tf_op jit(solution)/shard_map/ppermute | solution.py:167
  45.6 12.3 %collective-permute-start.7 = (bf16[256,256]{1,0:T(8,128)(2,1)S(1)}, bf16[256,256]{1,0:T(8,128)(2,1)S(1)}, u32[]{:S(2)}, u32[]{:S(2)}) collective-permute-start(bf16[256,256]{1,0:T(8,128)(2,1)S(1)} %shard_map.64.refs_4_.refs_5_), channel_id=1, source_target_pairs={{12,0},{13,1},{14,2},{15,3},{0,4},{1,5},{2,6},{3,7},{4,8},{5,9},{6... | collective-permute-start | bytes 393224 | tf_op jit(solution)/shard_map/ppermute | solution.py:167
  49.9 15.5 %collective-permute-start.12 = (bf16[2048,128]{1,0:T(8,128)(2,1)S(1)}, bf16[2048,128]{1,0:T(8,128)(2,1)S(1)}, u32[]{:S(2)}, u32[]{:S(2)}) collective-permute-start(bf16[2048,128]{1,0:T(8,128)(2,1)S(1)} %collective-permute-done.1.refs_3_), channel_id=1, source_target_pairs={{48,0},{49,1},{50,2},{51,3},{52,4},{53,5},{54,6},{55,7},{56,8},{57... | collective-permute-start | bytes 1572872 | tf_op jit(solution)/shard_map/ppermute | solution.py:185
  51.9 16.9 %collective-permute-start.11 = (bf16[2048,128]{1,0:T(8,128)(2,1)S(1)}, bf16[2048,128]{1,0:T(8,128)(2,1)}, u32[]{:S(2)}, u32[]{:S(2)}) collective-permute-start(bf16[2048,128]{1,0:T(8,128)(2,1)S(1)} %collective-permute-done.1.refs_3_), channel_id=1, source_target_pairs={{64,0},{65,1},{66,2},{67,3},{68,4},{69,5},{70,6},{71,7},{72,8},{73... | collective-permute-start | bytes 1572872 | tf_op jit(solution)/shard_map/ppermute | solution.py:185
  56.0 25.1 %collective-permute-start.10 = (bf16[2048,128]{1,0:T(8,128)(2,1)S(1)}, bf16[2048,128]{1,0:T(8,128)(2,1)}, u32[]{:S(2)}, u32[]{:S(2)}) collective-permute-start(bf16[2048,128]{1,0:T(8,128)(2,1)S(1)} %collective-permute-done.1.refs_3_), channel_id=1, source_target_pairs={{448,0},{449,1},{450,2},{451,3},{452,4},{453,5},{454,6},{455,7},{4... | collective-permute-start | bytes 1572872 | tf_op jit(solution)/shard_map/ppermute | solution.py:185
  57.9 26.0 %collective-permute-start.9 = (bf16[2048,128]{1,0:T(8,128)(2,1)S(1)}, bf16[2048,128]{1,0:T(8,128)(2,1)}, u32[]{:S(2)}, u32[]{:S(2)}) collective-permute-start(bf16[2048,128]{1,0:T(8,128)(2,1)S(1)} %collective-permute-done.1.refs_3_), channel_id=1, source_target_pairs={{2,0},{3,1},{4,2},{5,3},{6,4},{7,5},{8,6},{9,7},{10,8},{11,9},{12,... | collective-permute-start | bytes 1572872 | tf_op jit(solution)/shard_map/ppermute | solution.py:185
  62.3 24.4 %collective-permute-start.8 = (bf16[2048,128]{1,0:T(8,128)(2,1)S(1)}, bf16[2048,128]{1,0:T(8,128)(2,1)}, u32[]{:S(2)}, u32[]{:S(2)}) collective-permute-start(bf16[2048,128]{1,0:T(8,128)(2,1)S(1)} %collective-permute-done.1.refs_3_), channel_id=1, source_target_pairs={{14,0},{15,1},{0,2},{1,3},{2,4},{3,5},{4,6},{5,7},{6,8},{7,9},{8,1... | collective-permute-start | bytes 1572872 | tf_op jit(solution)/shard_map/ppermute | solution.py:185
  65.4 7.7 %copy-start.1 = (bf16[128,2048]{1,0:T(8,128)(2,1)S(1)}, bf16[128,2048]{1,0:T(8,128)(2,1)}, u32[]{:S(2)}) copy-start(bf16[128,2048]{1,0:T(8,128)(2,1)} %refs_1_.15) | copy-start | bytes 1572868
  65.4 24.0 %collective-permute-start.2 = (bf16[1024,128]{1,0:T(8,128)(2,1)}, bf16[1024,128]{1,0:T(8,128)(2,1)}, u32[]{:S(2)}, u32[]{:S(2)}) collective-permute-start(bf16[1024,128]{1,0:T(8,128)(2,1)} %get-tuple-element.6), channel_id=1, source_target_pairs={{32,0},{33,1},{34,2},{35,3},{36,4},{37,5},{38,6},{39,7},{40,8},{41... | collective-permute-start | bytes 786440 | tf_op jit(solution)/shard_map/ppermute | solution.py:180
  68.7 20.7 %collective-permute-start.3 = (bf16[1024,128]{1,0:T(8,128)(2,1)}, bf16[1024,128]{1,0:T(8,128)(2,1)}, u32[]{:S(2)}, u32[]{:S(2)}) collective-permute-start(bf16[1024,128]{1,0:T(8,128)(2,1)} %get-tuple-element.5), channel_id=1, source_target_pairs={{66,0},{463,1},{68,2},{449,3},{70,4},{451,5},{72,6},{453,7},{74,8}... | collective-permute-start | bytes 786440 | tf_op jit(solution)/shard_map/ppermute | solution.py:181
  92.3 13.3 %collective-permute-start.14 = (bf16[128,1024]{1,0:T(8,128)(2,1)S(1)}, bf16[128,1024]{1,0:T(8,128)(2,1)S(1)}, u32[]{:S(2)}, u32[]{:S(2)}) collective-permute-start(bf16[128,1024]{1,0:T(8,128)(2,1)S(1)} %slice.22), channel_id=1, source_target_pairs={{1,0},{0,1},{3,2},{2,3},{5,4},{4,5},{7,6},{6,7},{9,8},{8,9},{11,10... | collective-permute-start | bytes 786440 | tf_op jit(solution)/shard_map/ppermute | solution.py:195

commit v2 on v1

v2 whole, which is shorter than its diff:
```python
import functools
import math

import jax
import jax.numpy as jnp
from jax import lax
from jax.experimental import pallas as pl
from jax.experimental.pallas import tpu as pltpu
from jax.sharding import PartitionSpec as P

HEAD_SIZE = 128
WIDTH = 2048
ROWS = 128
PAIR = 2 * ROWS
HALF = 8 * HEAD_SIZE
NEG = -1e30

YS, XS, ZS, CORES = 8, 4, 8, 2
AXES = ("dp", "ctx")
ORDER = ((5, 3, 1, 7, 4, 2, 0, 6), (7, 3, 0, 6, 2, 4, 1, 5))
AROUND = (0, 1, -1, 2, -2)
VMEM = pl.BlockSpec(memory_space=pltpu.VMEM)
SMEM = pl.BlockSpec(memory_space=pltpu.SMEM)


def flat(y, x, z, c):
    return (((y % YS) * XS + x % XS) * ZS + z % ZS) * CORES + c


def everyone():
    return [(y, x, z, c) for y in range(YS) for x in range(XS) for z in range(ZS) for c in range(CORES)]


def first_moves():
    pairs = []
    for y, x, z, c in everyone():
        head = 8 * c + ORDER[c][(2 * x + 3 * y + z) % 8]
        pairs.append((flat(y, x, head // 2, head % 2), flat(y, x, z, c)))
    return pairs


def moves(step):
    pairs = []
    for y, x, z, c in everyone():
        dy, dx, dz = step(c)
        pairs.append((flat(y + dy, x + dx, z + dz, c), flat(y, x, z, c)))
    return pairs


def swap_cores(value):
    return lax.ppermute(value, AXES, [(flat(y, x, z, 1 - c), flat(y, x, z, c)) for y, x, z, c in everyone()])


def place():
    dp, ctx = lax.axis_index("dp"), lax.axis_index("ctx")
    return dp // XS, dp % XS, ctx // CORES, ctx % CORES


def kv_rows(rows, key_ref, value_ref, c, kv_ref, first):
    mine = pl.ds(pl.multiple_of(c * HEAD_SIZE, HEAD_SIZE), HEAD_SIZE)
    for column, matrix in ((0, key_ref), (HEAD_SIZE, value_ref)):
        kv_ref[first : first + ROWS, column : column + HEAD_SIZE] = jnp.dot(
            rows[...], matrix[:, mine], preferred_element_type=jnp.float32
        ).astype(jnp.bfloat16)


def own_kv_kernel(lengths_ref, own_ref, key_ref, value_ref, kv_ref, row_docs_ref, key_docs_ref):
    y, x, z, c = place()
    kv_rows(own_ref, key_ref, value_ref, c, kv_ref, 0)

    def positions(shape, axis, block):
        row = lax.broadcasted_iota(jnp.int32, shape, axis)
        return jnp.where(row < ROWS, row + ROWS * c, row - ROWS * c) + PAIR * block

    def docs(place_in_group):
        end = 0
        total = jnp.zeros(place_in_group.shape, jnp.int32)
        for e in range(16):
            end = end + lengths_ref[e]
            total = total + (place_in_group >= end).astype(jnp.int32)
        return total

    row_docs_ref[...] = docs(positions((PAIR, 1), 0, z))
    for i, step in enumerate(AROUND):
        key_docs_ref[:, i * PAIR : (i + 1) * PAIR] = docs(positions((1, PAIR), 1, (z + step + ZS) % ZS))


def other_kv_kernel(other_ref, key_ref, value_ref, held_ref, kv_ref):
    y, x, z, c = place()
    kv_rows(other_ref, key_ref, value_ref, c, kv_ref, ROWS)


def kv_project(lengths, own, other, key_matrix, value_matrix):
    kv_shape = jax.ShapeDtypeStruct((PAIR, 2 * HEAD_SIZE), jnp.bfloat16)
    settings = dict(
        compiler_params=pltpu.CompilerParams(vmem_limit_bytes=8 * 2**20),
        cost_estimate=pl.CostEstimate(flops=2**27, bytes_accessed=2**21, transcendentals=0),
    )
    kv, row_docs, key_docs = pl.pallas_call(
        own_kv_kernel,
        in_specs=[SMEM, VMEM, VMEM, VMEM],
        out_specs=[VMEM] * 3,
        out_shape=[
            kv_shape,
            jax.ShapeDtypeStruct((PAIR, 1), jnp.int32),
            jax.ShapeDtypeStruct((1, len(AROUND) * PAIR), jnp.int32),
        ],
        **settings,
    )(lengths, own, key_matrix, value_matrix)
    kv = pl.pallas_call(
        other_kv_kernel,
        in_specs=[VMEM] * 4,
        out_specs=VMEM,
        out_shape=kv_shape,
        input_output_aliases={3: 0},
        **settings,
    )(other, key_matrix, value_matrix, kv)
    return kv, row_docs, key_docs


def head_kernel(shift, own_ref, other_ref, weight_ref, *refs):
    kv, (row_docs, key_docs, _, _, keep_ref, send_ref) = refs[:5], refs[5:]
    y, x, z, c = place()
    color = (2 * x + 3 * y + z + shift) % 8
    slot = 0
    for k in range(8):
        slot = slot + jnp.where(color == k, jnp.where(c == 0, ORDER[0][k], ORDER[1][k]), 0)
    queries = jnp.concatenate(
        [
            jnp.dot(rows[...], weight_ref[...], preferred_element_type=jnp.float32).astype(jnp.bfloat16)
            for rows in (own_ref, other_ref)
        ],
        axis=0,
    )
    factor = math.log2(math.e) / math.sqrt(HEAD_SIZE)
    docs = row_docs[...]
    scores = []
    for i in range(5):
        product = lax.dot_general(
            queries, kv[i][:, :HEAD_SIZE], (((1,), (1,)), ((), ())), preferred_element_type=jnp.float32
        )
        allowed = docs == key_docs[:, i * PAIR : (i + 1) * PAIR]
        scores.append(jnp.where(allowed, product, NEG))
    highest = functools.reduce(jnp.maximum, [jnp.max(s, axis=1, keepdims=True) for s in scores])
    summed, mixed = 0.0, 0.0
    for i in range(5):
        part = jnp.exp2((scores[i] - highest) * factor)
        summed = summed + jnp.sum(part, axis=1, keepdims=True)
        mixed = mixed + jnp.dot(
            part.astype(jnp.bfloat16), kv[i][:, HEAD_SIZE:], preferred_element_type=jnp.float32
        )
    result = (mixed / summed).astype(jnp.bfloat16)
    columns = pl.ds(pl.multiple_of(slot * HEAD_SIZE, HEAD_SIZE), HEAD_SIZE)
    keep_ref[:, columns] = result[:ROWS]
    send_ref[:, columns] = result[ROWS:]


def one_head(shift, own, other, weight, kv, row_docs, key_docs, keep, send):
    inputs = [own, other, weight, *kv, row_docs, key_docs, keep, send]
    shape = jax.ShapeDtypeStruct(keep.shape, keep.dtype)
    return pl.pallas_call(
        functools.partial(head_kernel, shift),
        in_specs=[VMEM] * len(inputs),
        out_specs=[VMEM, VMEM],
        out_shape=[shape, shape],
        input_output_aliases={len(inputs) - 2: 0, len(inputs) - 1: 1},
        compiler_params=pltpu.CompilerParams(vmem_limit_bytes=12 * 2**20),
        cost_estimate=pl.CostEstimate(flops=2**28, bytes_accessed=2**21, transcendentals=2**18),
    )(*inputs)


def gate_kernel(*refs):
    pass


def gate(value, *after):
    return pl.pallas_call(
        gate_kernel,
        in_specs=[VMEM] * (1 + len(after)),
        out_specs=VMEM,
        out_shape=jax.ShapeDtypeStruct(value.shape, value.dtype),
        input_output_aliases={0: 0},
        compiler_params=pltpu.CompilerParams(vmem_limit_bytes=2**20),
    )(value, *after)


def join_kernel(mine_ref, other_ref, out_ref):
    y, x, z, c = place()
    out_ref[:, pl.ds(pl.multiple_of(c * HALF, HALF), HALF)] = mine_ref[...]
    out_ref[:, pl.ds(pl.multiple_of((1 - c) * HALF, HALF), HALF)] = other_ref[...]


def join(keep, arrived):
    return pl.pallas_call(
        join_kernel,
        grid=(1,),
        in_specs=[pl.BlockSpec((ROWS, HALF), lambda i: (0, 0))] * 2,
        out_specs=pl.BlockSpec((ROWS, 2 * HALF), lambda i: (0, 0)),
        out_shape=jax.ShapeDtypeStruct((ROWS, 2 * HALF), keep.dtype),
        compiler_params=pltpu.CompilerParams(vmem_limit_bytes=8 * 2**20),
    )(keep, arrived)


def body(tokens, query_weight, key_matrix, value_matrix, doc_lengths):
    other = swap_cores(tokens)
    weight = lax.ppermute(query_weight, AXES, first_moves())
    kv, row_docs, key_docs = kv_project(doc_lengths, tokens, other, key_matrix, value_matrix)
    kv_all = [kv] + [lax.ppermute(kv, AXES, moves(lambda c, d=d: (0, 0, d))) for d in AROUND[1:]]

    weight = gate(weight, *kv_all)
    arrivals = [(0, weight)]
    steps = (
        (4, lambda c: (1, 0, 1) if c == 0 else (-1, 0, -1)),
        (2, lambda c: (0, 1, 0)),
        (-2, lambda c: (0, -1, 0)),
        (3, lambda c: (1, 0, 0)),
        (-3, lambda c: (-1, 0, 0)),
        (1, lambda c: (0, 0, 1)),
        (-1, lambda c: (0, 0, -1)),
    )
    for shift, step in steps:
        arrivals.append((shift, lax.ppermute(weight, AXES, moves(step))))

    keep = jnp.zeros((ROWS, HALF), jnp.bfloat16)
    send = jnp.zeros((ROWS, HALF), jnp.bfloat16)
    for shift, w in arrivals:
        keep, send = one_head(shift, tokens, other, w, kv_all, row_docs, key_docs, keep, send)
    return join(keep, swap_cores(send))


def solution(mesh):
    in_specs = (P(("dp", "ctx"), None), P(None, "ctx"), P(), P(), P("dp"))
    out_specs = P(("dp", "ctx"), None)
    return jax.shard_map(body, mesh=mesh, in_specs=in_specs, out_specs=out_specs, check_vma=False)
```

time: 108 us -> 83.8 us (0.78)
  starting transfers between devices: 74.3 us -> 55.4 us
  Pallas kernels: 20.8 us -> 11.5 us
  waiting for transfers between devices: 4.45 us -> 10.9 us
  local copies, waits for them, and re-layouts: 5.9 us -> 4.19 us
    ppermute x11 -> x10, starting transfers between devices: 62.8 us -> 40.5 us  [the longest x7 23.3 us: body(): arrivals.append((shift, lax.ppermute(weight, AXES, moves(step))))]
    pallas_call x10 -> x12, Pallas kernels: 20.8 us -> 11.5 us  [the longest x8 8.97 us: one_head(): pl.pallas_call(functools.partial(head_kernel, shift), in_specs=[VMEM] * l...]
    ppermute x4, waiting for transfers between devices: 0.01 us -> 7.12 us  [body(): lax.ppermute(kv, AXES, moves(lambda c, d=d: (0, 0, d)))]
    ppermute x4, starting transfers between devices: 11.5 us -> 14.9 us  [body(): lax.ppermute(kv, AXES, moves(lambda c, d=d: (0, 0, d)))]
    ppermute x11 -> x10, waiting for transfers between devices: 4.44 us -> 3.73 us  [the longest x7 2.59 us: body(): arrivals.append((shift, lax.ppermute(weight, AXES, moves(step))))]
    unnamed x14 -> x12, local copies, waits for them, and re-layouts: 4.14 us -> 4.15 us
  transfers between devices with their start and end apart: 15 -> 14, of which waited for: 2 -> 4; matrix products, arithmetic and copies ran while one was open for 2% -> 0% of each run, Pallas kernels for 16% -> 12%
where the time goes in v2:
time: 83.8 us; the launch traced here: 82.2 us
  starting transfers between devices  55.4 us (66%)
  Pallas kernels  11.5 us (14%)
  waiting for transfers between devices  10.9 us (13%)
  local copies, waits for them, and re-layouts  4.19 us (5%)
    ppermute x7, starting transfers between devices, body(): arrivals.append((shift, lax.ppermute(weight, AXES, moves(step))))  23.3 us
    ppermute x2, starting transfers between devices, swap_cores(): lax.ppermute(value, AXES, [(flat(y, x, z, 1 - c), flat(y, x, z, c)) for y...  15.3 us
    ppermute x4, starting transfers between devices, body(): lax.ppermute(kv, AXES, moves(lambda c, d=d: (0, 0, d)))  14.9 us
    pallas_call x8, Pallas kernels, one_head(): pl.pallas_call(functools.partial(head_kernel, shift), in_specs=[VMEM] * l...  8.97 us
    ppermute x4, waiting for transfers between devices, body(): lax.ppermute(kv, AXES, moves(lambda c, d=d: (0, 0, d)))  7.12 us
    unnamed x12, local copies, waits for them, and re-layouts  4.15 us
    ppermute x7, waiting for transfers between devices, body(): arrivals.append((shift, lax.ppermute(weight, AXES, moves(step))))  2.59 us
    ppermute x1, starting transfers between devices, body(): weight = lax.ppermute(query_weight, AXES, first_moves())  1.92 us
  transfers between devices with their start and end apart: 14, of which 4 were waited for; matrix products, arithmetic and copies ran while one was open for 0% of the time, Pallas kernels for 12%

profile of v2, /device:TPU:1, one launch (start us, length us, event | category | flops | bytes accessed | tf_op | source)
XLA Modules:
  0.0 82.2 jit_solution(17300682294904082989)
XLA Ops:
  0.0 8.8 %collective-permute-start = (bf16[128,2048]{1,0:T(8,128)(2,1)}, bf16[128,2048]{1,0:T(8,128)(2,1)S(1)}, u32[]{:S(2)}, u32[]{:S(2)}) collective-permute-start(bf16[128,2048]{1,0:T(8,128)(2,1)} %own_ref.17), channel_id=1, source_target_pairs={{1,0},{0,1},{3,2},{2,3},{5,4},{4,5},{7,6},{6,7},{9,8},{8,9},{11,10... | collective-permute-start | bytes 1572872 | tf_op jit(solution)/shard_map/ppermute | solution.py:51
  8.8 1.9 %collective-permute-start.1 = (bf16[2048,128]{1,0:T(8,128)(2,1)}, bf16[2048,128]{1,0:T(8,128)(2,1)S(1)}, u32[]{:S(2)}, u32[]{:S(2)}) collective-permute-start(bf16[2048,128]{1,0:T(8,128)(2,1)} %param.6), channel_id=1, source_target_pairs={{5,0},{15,1},{3,2},{11,3},{1,4},{8,5},{7,6},{14,7},{4,8},{10,9},{2... | collective-permute-start | bytes 1572872 | tf_op jit(solution)/shard_map/ppermute | solution.py:206
  10.7 0.0 copy-start
  10.7 1.0 %copy-done = bf16[128,2048]{1,0:T(8,128)(2,1)S(1)} copy-done((bf16[128,2048]{1,0:T(8,128)(2,1)S(1)}, bf16[128,2048]{1,0:T(8,128)(2,1)}, u32[]{:S(2)}) %copy-start) | copy-done | bytes 524312
  11.8 0.0 copy-start.2
  11.8 1.2 %copy-done.2 = bf16[2048,256]{1,0:T(8,128)(2,1)S(1)} copy-done((bf16[2048,256]{1,0:T(8,128)(2,1)S(1)}, bf16[2048,256]{1,0:T(8,128)(2,1)}, u32[]{:S(2)}) %copy-start.2) | copy-done | bytes 1048600
  13.0 0.0 copy-start.4
  13.0 1.2 %copy-done.4 = bf16[2048,256]{1,0:T(8,128)(2,1)S(1)} copy-done((bf16[2048,256]{1,0:T(8,128)(2,1)S(1)}, bf16[2048,256]{1,0:T(8,128)(2,1)}, u32[]{:S(2)}) %copy-start.4) | copy-done | bytes 1048600
  14.2 0.0 copy-start.5
  14.2 0.7 copy-done.5
  14.9 0.0 copy-start.3
  14.9 1.2 %shard_map.55 = (bf16[256,256]{1,0:T(8,128)(2,1)S(1)}, s32[256,1]{1,0:T(8,128)S(1)}, s32[1,1280]{1,0:T(1,128)S(1)}) custom-call(s32[16]{0:T(128)S(1)} %copy-done.5, bf16[128,2048]{1,0:T(8,128)(2,1)S(1)} %copy-done, bf16[2048,256]{1,0:T(8,128)(2,1)S(1)} %copy-done.2, bf16[2048,256]{1,0:T(8,128)(2,1)S(1)} %copy-done.4), custom_call_target="tpu_custom_call" | custom-call | flops 134217728 | bytes 2097152 | tf_op jit(solution)/shard_map/pallas_call | solution.py:99
  16.1 0.0 collective-permute-done.other_ref
  16.1 0.0 copy-done.3
  16.1 0.4 shard_map.56.refs_1_.refs_0_
  16.6 4.2 %collective-permute-start.5 = (bf16[256,256]{1,0:T(8,128)(2,1)S(1)}, bf16[256,256]{1,0:T(8,128)(2,1)S(1)}, u32[]{:S(2)}, u32[]{:S(2)}) collective-permute-start(bf16[256,256]{1,0:T(8,128)(2,1)S(1)} %shard_map.56.refs_1_.refs_0_), channel_id=1, source_target_pairs={{12,0},{13,1},{14,2},{15,3},{0,4},{1,5},{2,6},{3,7},{4,8},{5,9},{6... | collective-permute-start | bytes 393224 | tf_op jit(solution)/shard_map/ppermute | solution.py:208
  20.8 4.2 %collective-permute-start.4 = (bf16[256,256]{1,0:T(8,128)(2,1)S(1)}, bf16[256,256]{1,0:T(8,128)(2,1)S(1)}, u32[]{:S(2)}, u32[]{:S(2)}) collective-permute-start(bf16[256,256]{1,0:T(8,128)(2,1)S(1)} %shard_map.56.refs_1_.refs_0_), channel_id=1, source_target_pairs={{4,0},{5,1},{6,2},{7,3},{8,4},{9,5},{10,6},{11,7},{12,8},{13,9},{1... | collective-permute-start | bytes 393224 | tf_op jit(solution)/shard_map/ppermute | solution.py:208
  25.0 1.9 %collective-permute-start.3 = (bf16[256,256]{1,0:T(8,128)(2,1)S(1)}, bf16[256,256]{1,0:T(8,128)(2,1)S(1)}, u32[]{:S(2)}, u32[]{:S(2)}) collective-permute-start(bf16[256,256]{1,0:T(8,128)(2,1)S(1)} %shard_map.56.refs_1_.refs_0_), channel_id=1, source_target_pairs={{14,0},{15,1},{0,2},{1,3},{2,4},{3,5},{4,6},{5,7},{6,8},{7,9},{8,1... | collective-permute-start | bytes 393224 | tf_op jit(solution)/shard_map/ppermute | solution.py:208
  26.9 4.6 %collective-permute-start.2 = (bf16[256,256]{1,0:T(8,128)(2,1)S(1)}, bf16[256,256]{1,0:T(8,128)(2,1)S(1)}, u32[]{:S(2)}, u32[]{:S(2)}) collective-permute-start(bf16[256,256]{1,0:T(8,128)(2,1)S(1)} %shard_map.56.refs_1_.refs_0_), channel_id=1, source_target_pairs={{2,0},{3,1},{4,2},{5,3},{6,4},{7,5},{8,6},{9,7},{10,8},{11,9},{12,... | collective-permute-start | bytes 393224 | tf_op jit(solution)/shard_map/ppermute | solution.py:208
  31.5 0.0 collective-permute-done.1.refs_0_
  31.5 0.0 collective-permute-done.5.refs_5_.refs_4_
  31.5 2.6 %collective-permute-done.4.refs_4_.refs_3_ = bf16[256,256]{1,0:T(8,128)(2,1)S(1)} collective-permute-done((bf16[256,256]{1,0:T(8,128)(2,1)S(1)}, bf16[256,256]{1,0:T(8,128)(2,1)S(1)}, u32[]{:S(2)}, u32[]{:S(2)}) %collective-permute-start.4) | collective-permute-done | bytes 131104 | tf_op jit(solution)/shard_map/ppermute | solution.py:208
  34.1 0.0 collective-permute-done.3.refs_3_.refs_2_
  34.1 4.5 %collective-permute-done.2.refs_2_.refs_1_ = bf16[256,256]{1,0:T(8,128)(2,1)S(1)} collective-permute-done((bf16[256,256]{1,0:T(8,128)(2,1)S(1)}, bf16[256,256]{1,0:T(8,128)(2,1)S(1)}, u32[]{:S(2)}, u32[]{:S(2)}) %collective-permute-start.2) | collective-permute-done | bytes 131104 | tf_op jit(solution)/shard_map/ppermute | solution.py:208
  38.6 0.0 copy-start.1
  38.6 2.0 %collective-permute-start.12 = (bf16[2048,128]{1,0:T(8,128)(2,1)S(1)}, bf16[2048,128]{1,0:T(8,128)(2,1)S(1)}, u32[]{:S(2)}, u32[]{:S(2)}) collective-permute-start(bf16[2048,128]{1,0:T(8,128)(2,1)S(1)} %shard_map.57.weight_ref), channel_id=1, source_target_pairs={{66,0},{463,1},{68,2},{449,3},{70,4},{451,5},{72,6},{453,7},{74,8}... | collective-permute-start | bytes 1572872 | tf_op jit(solution)/shard_map/ppermute | solution.py:222
  40.7 6.3 %collective-permute-start.11 = (bf16[2048,128]{1,0:T(8,128)(2,1)S(1)}, bf16[2048,128]{1,0:T(8,128)(2,1)S(1)}, u32[]{:S(2)}, u32[]{:S(2)}) collective-permute-start(bf16[2048,128]{1,0:T(8,128)(2,1)S(1)} %shard_map.57.weight_ref), channel_id=1, source_target_pairs={{16,0},{17,1},{18,2},{19,3},{20,4},{21,5},{22,6},{23,7},{24,8},{25... | collective-permute-start | bytes 1572872 | tf_op jit(solution)/shard_map/ppermute | solution.py:222
  47.0 1.9 %collective-permute-start.10 = (bf16[2048,128]{1,0:T(8,128)(2,1)S(1)}, bf16[2048,128]{1,0:T(8,128)(2,1)S(1)}, u32[]{:S(2)}, u32[]{:S(2)}) collective-permute-start(bf16[2048,128]{1,0:T(8,128)(2,1)S(1)} %shard_map.57.weight_ref), channel_id=1, source_target_pairs={{48,0},{49,1},{50,2},{51,3},{52,4},{53,5},{54,6},{55,7},{56,8},{57... | collective-permute-start | bytes 1572872 | tf_op jit(solution)/shard_map/ppermute | solution.py:222
  48.9 5.8 %collective-permute-start.9 = (bf16[2048,128]{1,0:T(8,128)(2,1)S(1)}, bf16[2048,128]{1,0:T(8,128)(2,1)S(1)}, u32[]{:S(2)}, u32[]{:S(2)}) collective-permute-start(bf16[2048,128]{1,0:T(8,128)(2,1)S(1)} %shard_map.57.weight_ref), channel_id=1, source_target_pairs={{64,0},{65,1},{66,2},{67,3},{68,4},{69,5},{70,6},{71,7},{72,8},{73... | collective-permute-start | bytes 1572872 | tf_op jit(solution)/shard_map/ppermute | solution.py:222
  54.8 1.9 %collective-permute-start.8 = (bf16[2048,128]{1,0:T(8,128)(2,1)S(1)}, bf16[2048,128]{1,0:T(8,128)(2,1)S(1)}, u32[]{:S(2)}, u32[]{:S(2)}) collective-permute-start(bf16[2048,128]{1,0:T(8,128)(2,1)S(1)} %shard_map.57.weight_ref), channel_id=1, source_target_pairs={{448,0},{449,1},{450,2},{451,3},{452,4},{453,5},{454,6},{455,7},{4... | collective-permute-start | bytes 1572872 | tf_op jit(solution)/shard_map/ppermute | solution.py:222
  56.7 0.0 collective-permute-done.12.weight_ref
  56.7 3.0 %collective-permute-start.7 = (bf16[2048,128]{1,0:T(8,128)(2,1)S(1)}, bf16[2048,128]{1,0:T(8,128)(2,1)S(1)}, u32[]{:S(2)}, u32[]{:S(2)}) collective-permute-start(bf16[2048,128]{1,0:T(8,128)(2,1)S(1)} %shard_map.57.weight_ref), channel_id=1, source_target_pairs={{2,0},{3,1},{4,2},{5,3},{6,4},{7,5},{8,6},{9,7},{10,8},{11,9},{12,... | collective-permute-start | bytes 1572872 | tf_op jit(solution)/shard_map/ppermute | solution.py:222
  59.7 0.0 collective-permute-done.11.weight_ref
  59.7 2.3 %collective-permute-start.6 = (bf16[2048,128]{1,0:T(8,128)(2,1)S(1)}, bf16[2048,128]{1,0:T(8,128)(2,1)S(1)}, u32[]{:S(2)}, u32[]{:S(2)}) collective-permute-start(bf16[2048,128]{1,0:T(8,128)(2,1)S(1)} %shard_map.57.weight_ref), channel_id=1, source_target_pairs={{14,0},{15,1},{0,2},{1,3},{2,4},{3,5},{4,6},{5,7},{6,8},{7,9},{8,1... | collective-permute-start | bytes 1572872 | tf_op jit(solution)/shard_map/ppermute | solution.py:222
  62.1 0.0 copy-done.1
  62.1 1.1 %shard_map.58 = (bf16[128,1024]{1,0:T(8,128)(2,1)S(1)}, bf16[128,1024]{1,0:T(8,128)(2,1)S(1)}) custom-call(bf16[128,2048]{1,0:T(8,128)(2,1)S(1)} %copy-done.1, bf16[128,2048]{1,0:T(8,128)(2,1)S(1)} %collective-permute-done.other_ref, bf16[2048,128]{1,0:T(8,128)(2,1)S(1)} %shard_map.57.weight_ref, ...), custom_call_target="tpu_custom_call", output_to_operand_aliasing={{0}: (10, {}), {1}: (11, {})} | custom-call | flops 268435456 | bytes 2097152 | tf_op jit(solution)/shard_map/pallas_call | solution.py:161
  63.2 1.1 %shard_map.59 = (bf16[128,1024]{1,0:T(8,128)(2,1)S(1)}, bf16[128,1024]{1,0:T(8,128)(2,1)S(1)}) custom-call(bf16[128,2048]{1,0:T(8,128)(2,1)S(1)} %copy-done.1, bf16[128,2048]{1,0:T(8,128)(2,1)S(1)} %collective-permute-done.other_ref, bf16[2048,128]{1,0:T(8,128)(2,1)S(1)} %collective-permute-done.12.weight_ref, ...), custom_call_target="tpu_custom_call", output_to_operand_aliasing={{0}: (10, {}), {1}: (11, {})} | custom-call | flops 268435456 | bytes 2097152 | tf_op jit(solution)/shard_map/pallas_call | solution.py:161
  64.3 1.1 %shard_map.60 = (bf16[128,1024]{1,0:T(8,128)(2,1)S(1)}, bf16[128,1024]{1,0:T(8,128)(2,1)S(1)}) custom-call(bf16[128,2048]{1,0:T(8,128)(2,1)S(1)} %copy-done.1, bf16[128,2048]{1,0:T(8,128)(2,1)S(1)} %collective-permute-done.other_ref, bf16[2048,128]{1,0:T(8,128)(2,1)S(1)} %collective-permute-done.11.weight_ref, ...), custom_call_target="tpu_custom_call", output_to_operand_aliasing={{0}: (10, {}), {1}: (11, {})} | custom-call | flops 268435456 | bytes 2097152 | tf_op jit(solution)/shard_map/pallas_call | solution.py:161
  65.5 0.0 collective-permute-done.10.weight_ref
  65.5 1.1 %shard_map.61 = (bf16[128,1024]{1,0:T(8,128)(2,1)S(1)}, bf16[128,1024]{1,0:T(8,128)(2,1)S(1)}) custom-call(bf16[128,2048]{1,0:T(8,128)(2,1)S(1)} %copy-done.1, bf16[128,2048]{1,0:T(8,128)(2,1)S(1)} %collective-permute-done.other_ref, bf16[2048,128]{1,0:T(8,128)(2,1)S(1)} %collective-permute-done.10.weight_ref, ...), custom_call_target="tpu_custom_call", output_to_operand_aliasing={{0}: (10, {}), {1}: (11, {})} | custom-call | flops 268435456 | bytes 2097152 | tf_op jit(solution)/shard_map/pallas_call | solution.py:161
  66.6 0.0 collective-permute-done.9.weight_ref
  66.6 1.1 %shard_map.62 = (bf16[128,1024]{1,0:T(8,128)(2,1)S(1)}, bf16[128,1024]{1,0:T(8,128)(2,1)S(1)}) custom-call(bf16[128,2048]{1,0:T(8,128)(2,1)S(1)} %copy-done.1, bf16[128,2048]{1,0:T(8,128)(2,1)S(1)} %collective-permute-done.other_ref, bf16[2048,128]{1,0:T(8,128)(2,1)S(1)} %collective-permute-done.9.weight_ref, ...), custom_call_target="tpu_custom_call", output_to_operand_aliasing={{0}: (10, {}), {1}: (11, {})} | custom-call | flops 268435456 | bytes 2097152 | tf_op jit(solution)/shard_map/pallas_call | solution.py:161
  67.7 0.0 collective-permute-done.8.weight_ref
  67.7 1.1 %shard_map.63 = (bf16[128,1024]{1,0:T(8,128)(2,1)S(1)}, bf16[128,1024]{1,0:T(8,128)(2,1)S(1)}) custom-call(bf16[128,2048]{1,0:T(8,128)(2,1)S(1)} %copy-done.1, bf16[128,2048]{1,0:T(8,128)(2,1)S(1)} %collective-permute-done.other_ref, bf16[2048,128]{1,0:T(8,128)(2,1)S(1)} %collective-permute-done.8.weight_ref, ...), custom_call_target="tpu_custom_call", output_to_operand_aliasing={{0}: (10, {}), {1}: (11, {})} | custom-call | flops 268435456 | bytes 2097152 | tf_op jit(solution)/shard_map/pallas_call | solution.py:161
  68.9 0.0 collective-permute-done.7.weight_ref
  68.9 1.1 %shard_map.64 = (bf16[128,1024]{1,0:T(8,128)(2,1)S(1)}, bf16[128,1024]{1,0:T(8,128)(2,1)S(1)}) custom-call(bf16[128,2048]{1,0:T(8,128)(2,1)S(1)} %copy-done.1, bf16[128,2048]{1,0:T(8,128)(2,1)S(1)} %collective-permute-done.other_ref, bf16[2048,128]{1,0:T(8,128)(2,1)S(1)} %collective-permute-done.7.weight_ref, ...), custom_call_target="tpu_custom_call", output_to_operand_aliasing={{0}: (10, {}), {1}: (11, {})} | custom-call | flops 268435456 | bytes 2097152 | tf_op jit(solution)/shard_map/pallas_call | solution.py:161
  70.0 2.6 %collective-permute-done.6.weight_ref = bf16[2048,128]{1,0:T(8,128)(2,1)S(1)} collective-permute-done((bf16[2048,128]{1,0:T(8,128)(2,1)S(1)}, bf16[2048,128]{1,0:T(8,128)(2,1)S(1)}, u32[]{:S(2)}, u32[]{:S(2)}) %collective-permute-start.6) | collective-permute-done | bytes 524320 | tf_op jit(solution)/shard_map/ppermute | solution.py:222
  72.6 1.1 %shard_map.65 = (bf16[128,1024]{1,0:T(8,128)(2,1)S(1)}, bf16[128,1024]{1,0:T(8,128)(2,1)S(1)}) custom-call(bf16[128,2048]{1,0:T(8,128)(2,1)S(1)} %copy-done.1, bf16[128,2048]{1,0:T(8,128)(2,1)S(1)} %collective-permute-done.other_ref, bf16[2048,128]{1,0:T(8,128)(2,1)S(1)} %collective-permute-done.6.weight_ref, ...), custom_call_target="tpu_custom_call", output_to_operand_aliasing={{0}: (10, {}), {1}: (11, {})} | custom-call | flops 268435456 | bytes 2097152 | tf_op jit(solution)/shard_map/pallas_call | solution.py:161
  73.7 6.5 %collective-permute-start.13 = (bf16[128,1024]{1,0:T(8,128)(2,1)S(1)}, bf16[128,1024]{1,0:T(8,128)(2,1)S(1)}, u32[]{:S(2)}, u32[]{:S(2)}) collective-permute-start(bf16[128,1024]{1,0:T(8,128)(2,1)S(1)} %get-tuple-element.42), channel_id=1, source_target_pairs={{1,0},{0,1},{3,2},{2,3},{5,4},{4,5},{7,6},{6,7},{9,8},{8,9},{11,10... | collective-permute-start | bytes 786440 | tf_op jit(solution)/shard_map/ppermute | solution.py:51
  80.2 1.1 %collective-permute-done.13.other_ref = bf16[128,1024]{1,0:T(8,128)(2,1)S(1)} collective-permute-done((bf16[128,1024]{1,0:T(8,128)(2,1)S(1)}, bf16[128,1024]{1,0:T(8,128)(2,1)S(1)}, u32[]{:S(2)}, u32[]{:S(2)}) %collective-permute-start.13) | collective-permute-done | bytes 262176 | tf_op jit(solution)/shard_map/ppermute | solution.py:51
  81.4 0.8 %shard_map.66 = bf16[128,2048]{1,0:T(8,128)(2,1)} custom-call(bf16[128,1024]{1,0:T(8,128)(2,1)S(1)} %get-tuple-element.41.mine_ref, bf16[128,1024]{1,0:T(8,128)(2,1)S(1)} %collective-permute-done.13.other_ref), custom_call_target="tpu_custom_call" | custom-call | tf_op jit(solution)/shard_map/pallas_call | solution.py:194
  (3 shorter events, 0.0 us)
Async XLA Ops:
  0.0 16.1 %collective-permute-start = (bf16[128,2048]{1,0:T(8,128)(2,1)}, bf16[128,2048]{1,0:T(8,128)(2,1)S(1)}, u32[]{:S(2)}, u32[]{:S(2)}) collective-permute-start(bf16[128,2048]{1,0:T(8,128)(2,1)} %own_ref.17), channel_id=1, source_target_pairs={{1,0},{0,1},{3,2},{2,3},{5,4},{4,5},{7,6},{6,7},{9,8},{8,9},{11,10... | collective-permute-start | bytes 1572872 | tf_op jit(solution)/shard_map/ppermute | solution.py:51
  8.8 22.7 %collective-permute-start.1 = (bf16[2048,128]{1,0:T(8,128)(2,1)}, bf16[2048,128]{1,0:T(8,128)(2,1)S(1)}, u32[]{:S(2)}, u32[]{:S(2)}) collective-permute-start(bf16[2048,128]{1,0:T(8,128)(2,1)} %param.6), channel_id=1, source_target_pairs={{5,0},{15,1},{3,2},{11,3},{1,4},{8,5},{7,6},{14,7},{4,8},{10,9},{2... | collective-permute-start | bytes 1572872 | tf_op jit(solution)/shard_map/ppermute | solution.py:206
  10.7 1.0 %copy-start = (bf16[128,2048]{1,0:T(8,128)(2,1)S(1)}, bf16[128,2048]{1,0:T(8,128)(2,1)}, u32[]{:S(2)}) copy-start(bf16[128,2048]{1,0:T(8,128)(2,1)} %own_ref.17) | copy-start | bytes 1572868
  11.8 1.2 %copy-start.2 = (bf16[2048,256]{1,0:T(8,128)(2,1)S(1)}, bf16[2048,256]{1,0:T(8,128)(2,1)}, u32[]{:S(2)}) copy-start(bf16[2048,256]{1,0:T(8,128)(2,1)} %key_ref.3) | copy-start | bytes 3145732
  13.0 1.2 %copy-start.4 = (bf16[2048,256]{1,0:T(8,128)(2,1)S(1)}, bf16[2048,256]{1,0:T(8,128)(2,1)}, u32[]{:S(2)}) copy-start(bf16[2048,256]{1,0:T(8,128)(2,1)} %value_ref.3) | copy-start | bytes 3145732
  14.2 0.7 copy-start.5
  14.9 1.3 %copy-start.3 = (bf16[2048,256]{1,0:T(8,128)(2,1)S(1)}, bf16[2048,256]{1,0:T(8,128)(2,1)}, u32[]{:S(2)}) copy-start(bf16[2048,256]{1,0:T(8,128)(2,1)} %key_ref.3) | copy-start | bytes 3145732
  16.6 14.9 %collective-permute-start.5 = (bf16[256,256]{1,0:T(8,128)(2,1)S(1)}, bf16[256,256]{1,0:T(8,128)(2,1)S(1)}, u32[]{:S(2)}, u32[]{:S(2)}) collective-permute-start(bf16[256,256]{1,0:T(8,128)(2,1)S(1)} %shard_map.56.refs_1_.refs_0_), channel_id=1, source_target_pairs={{12,0},{13,1},{14,2},{15,3},{0,4},{1,5},{2,6},{3,7},{4,8},{5,9},{6... | collective-permute-start | bytes 393224 | tf_op jit(solution)/shard_map/ppermute | solution.py:208
  20.8 13.3 %collective-permute-start.4 = (bf16[256,256]{1,0:T(8,128)(2,1)S(1)}, bf16[256,256]{1,0:T(8,128)(2,1)S(1)}, u32[]{:S(2)}, u32[]{:S(2)}) collective-permute-start(bf16[256,256]{1,0:T(8,128)(2,1)S(1)} %shard_map.56.refs_1_.refs_0_), channel_id=1, source_target_pairs={{4,0},{5,1},{6,2},{7,3},{8,4},{9,5},{10,6},{11,7},{12,8},{13,9},{1... | collective-permute-start | bytes 393224 | tf_op jit(solution)/shard_map/ppermute | solution.py:208
  25.0 9.1 %collective-permute-start.3 = (bf16[256,256]{1,0:T(8,128)(2,1)S(1)}, bf16[256,256]{1,0:T(8,128)(2,1)S(1)}, u32[]{:S(2)}, u32[]{:S(2)}) collective-permute-start(bf16[256,256]{1,0:T(8,128)(2,1)S(1)} %shard_map.56.refs_1_.refs_0_), channel_id=1, source_target_pairs={{14,0},{15,1},{0,2},{1,3},{2,4},{3,5},{4,6},{5,7},{6,8},{7,9},{8,1... | collective-permute-start | bytes 393224 | tf_op jit(solution)/shard_map/ppermute | solution.py:208
  26.9 11.7 %collective-permute-start.2 = (bf16[256,256]{1,0:T(8,128)(2,1)S(1)}, bf16[256,256]{1,0:T(8,128)(2,1)S(1)}, u32[]{:S(2)}, u32[]{:S(2)}) collective-permute-start(bf16[256,256]{1,0:T(8,128)(2,1)S(1)} %shard_map.56.refs_1_.refs_0_), channel_id=1, source_target_pairs={{2,0},{3,1},{4,2},{5,3},{6,4},{7,5},{8,6},{9,7},{10,8},{11,9},{12,... | collective-permute-start | bytes 393224 | tf_op jit(solution)/shard_map/ppermute | solution.py:208
  38.6 23.4 %copy-start.1 = (bf16[128,2048]{1,0:T(8,128)(2,1)S(1)}, bf16[128,2048]{1,0:T(8,128)(2,1)}, u32[]{:S(2)}) copy-start(bf16[128,2048]{1,0:T(8,128)(2,1)} %own_ref.17) | copy-start | bytes 1572868
  38.6 18.0 %collective-permute-start.12 = (bf16[2048,128]{1,0:T(8,128)(2,1)S(1)}, bf16[2048,128]{1,0:T(8,128)(2,1)S(1)}, u32[]{:S(2)}, u32[]{:S(2)}) collective-permute-start(bf16[2048,128]{1,0:T(8,128)(2,1)S(1)} %shard_map.57.weight_ref), channel_id=1, source_target_pairs={{66,0},{463,1},{68,2},{449,3},{70,4},{451,5},{72,6},{453,7},{74,8}... | collective-permute-start | bytes 1572872 | tf_op jit(solution)/shard_map/ppermute | solution.py:222
  40.7 19.0 %collective-permute-start.11 = (bf16[2048,128]{1,0:T(8,128)(2,1)S(1)}, bf16[2048,128]{1,0:T(8,128)(2,1)S(1)}, u32[]{:S(2)}, u32[]{:S(2)}) collective-permute-start(bf16[2048,128]{1,0:T(8,128)(2,1)S(1)} %shard_map.57.weight_ref), channel_id=1, source_target_pairs={{16,0},{17,1},{18,2},{19,3},{20,4},{21,5},{22,6},{23,7},{24,8},{25... | collective-permute-start | bytes 1572872 | tf_op jit(solution)/shard_map/ppermute | solution.py:222
  47.0 18.5 %collective-permute-start.10 = (bf16[2048,128]{1,0:T(8,128)(2,1)S(1)}, bf16[2048,128]{1,0:T(8,128)(2,1)S(1)}, u32[]{:S(2)}, u32[]{:S(2)}) collective-permute-start(bf16[2048,128]{1,0:T(8,128)(2,1)S(1)} %shard_map.57.weight_ref), channel_id=1, source_target_pairs={{48,0},{49,1},{50,2},{51,3},{52,4},{53,5},{54,6},{55,7},{56,8},{57... | collective-permute-start | bytes 1572872 | tf_op jit(solution)/shard_map/ppermute | solution.py:222
  48.9 17.7 %collective-permute-start.9 = (bf16[2048,128]{1,0:T(8,128)(2,1)S(1)}, bf16[2048,128]{1,0:T(8,128)(2,1)S(1)}, u32[]{:S(2)}, u32[]{:S(2)}) collective-permute-start(bf16[2048,128]{1,0:T(8,128)(2,1)S(1)} %shard_map.57.weight_ref), channel_id=1, source_target_pairs={{64,0},{65,1},{66,2},{67,3},{68,4},{69,5},{70,6},{71,7},{72,8},{73... | collective-permute-start | bytes 1572872 | tf_op jit(solution)/shard_map/ppermute | solution.py:222
  54.8 13.0 %collective-permute-start.8 = (bf16[2048,128]{1,0:T(8,128)(2,1)S(1)}, bf16[2048,128]{1,0:T(8,128)(2,1)S(1)}, u32[]{:S(2)}, u32[]{:S(2)}) collective-permute-start(bf16[2048,128]{1,0:T(8,128)(2,1)S(1)} %shard_map.57.weight_ref), channel_id=1, source_target_pairs={{448,0},{449,1},{450,2},{451,3},{452,4},{453,5},{454,6},{455,7},{4... | collective-permute-start | bytes 1572872 | tf_op jit(solution)/shard_map/ppermute | solution.py:222
  56.7 12.2 %collective-permute-start.7 = (bf16[2048,128]{1,0:T(8,128)(2,1)S(1)}, bf16[2048,128]{1,0:T(8,128)(2,1)S(1)}, u32[]{:S(2)}, u32[]{:S(2)}) collective-permute-start(bf16[2048,128]{1,0:T(8,128)(2,1)S(1)} %shard_map.57.weight_ref), channel_id=1, source_target_pairs={{2,0},{3,1},{4,2},{5,3},{6,4},{7,5},{8,6},{9,7},{10,8},{11,9},{12,... | collective-permute-start | bytes 1572872 | tf_op jit(solution)/shard_map/ppermute | solution.py:222
  59.7 12.8 %collective-permute-start.6 = (bf16[2048,128]{1,0:T(8,128)(2,1)S(1)}, bf16[2048,128]{1,0:T(8,128)(2,1)S(1)}, u32[]{:S(2)}, u32[]{:S(2)}) collective-permute-start(bf16[2048,128]{1,0:T(8,128)(2,1)S(1)} %shard_map.57.weight_ref), channel_id=1, source_target_pairs={{14,0},{15,1},{0,2},{1,3},{2,4},{3,5},{4,6},{5,7},{6,8},{7,9},{8,1... | collective-permute-start | bytes 1572872 | tf_op jit(solution)/shard_map/ppermute | solution.py:222
  73.7 7.7 %collective-permute-start.13 = (bf16[128,1024]{1,0:T(8,128)(2,1)S(1)}, bf16[128,1024]{1,0:T(8,128)(2,1)S(1)}, u32[]{:S(2)}, u32[]{:S(2)}) collective-permute-start(bf16[128,1024]{1,0:T(8,128)(2,1)S(1)} %get-tuple-element.42), channel_id=1, source_target_pairs={{1,0},{0,1},{3,2},{2,3},{5,4},{4,5},{7,6},{6,7},{9,8},{8,9},{11,10... | collective-permute-start | bytes 786440 | tf_op jit(solution)/shard_map/ppermute | solution.py:51

commit v3 on v2

v3 whole, which is shorter than its diff:
```python
import functools
import math

import jax
import jax.numpy as jnp
from jax import lax
from jax.experimental import pallas as pl
from jax.experimental.pallas import tpu as pltpu
from jax.sharding import PartitionSpec as P

HEAD_SIZE = 128
WIDTH = 2048
ROWS = 128
PAIR = 2 * ROWS
HALF = 8 * HEAD_SIZE
NEG = -1e30

YS, XS, ZS, CORES = 8, 4, 8, 2
AXES = ("dp", "ctx")
ORDER = ((5, 3, 1, 7, 4, 2, 0, 6), (7, 3, 0, 6, 2, 4, 1, 5))
AROUND = (0, 1, -1, 2, -2)
VMEM = pl.BlockSpec(memory_space=pltpu.VMEM)
HBM = pl.BlockSpec(memory_space=pltpu.HBM)


def flat(y, x, z, c):
    return (((y % YS) * XS + x % XS) * ZS + z % ZS) * CORES + c


def everyone():
    return [(y, x, z, c) for y in range(YS) for x in range(XS) for z in range(ZS) for c in range(CORES)]


def first_moves():
    pairs = []
    for y, x, z, c in everyone():
        head = 8 * c + ORDER[c][(2 * x + 3 * y + z) % 8]
        pairs.append((flat(y, x, head // 2, head % 2), flat(y, x, z, c)))
    return pairs


def moves(step):
    pairs = []
    for y, x, z, c in everyone():
        dy, dx, dz = step(c)
        pairs.append((flat(y + dy, x + dx, z + dz, c), flat(y, x, z, c)))
    return pairs


def swap_cores(value):
    return lax.ppermute(value, AXES, [(flat(y, x, z, 1 - c), flat(y, x, z, c)) for y, x, z, c in everyone()])


def place():
    dp, ctx = lax.axis_index("dp"), lax.axis_index("ctx")
    return dp // XS, dp % XS, ctx // CORES, ctx % CORES


def kv_rows(rows, key_ref, value_ref, kv_ref, first):
    for base, matrix in ((0, key_ref), (PAIR, value_ref)):
        kv_ref[base + first : base + first + ROWS] = jnp.dot(
            rows[...], matrix[...], preferred_element_type=jnp.float32
        ).astype(jnp.bfloat16)


def own_kv_kernel(
    lengths_hbm, own_hbm, key_hbm, value_hbm, own_ref, key_ref, value_ref, kv_ref, row_docs_ref, key_docs_ref, lengths, sems
):
    y, x, z, c = place()
    mine = pl.ds(pl.multiple_of(c * HEAD_SIZE, HEAD_SIZE), HEAD_SIZE)
    copies = [
        pltpu.make_async_copy(own_hbm, own_ref, sems.at[0]),
        pltpu.make_async_copy(key_hbm.at[:, mine], key_ref, sems.at[1]),
        pltpu.make_async_copy(value_hbm.at[:, mine], value_ref, sems.at[2]),
        pltpu.make_async_copy(lengths_hbm, lengths, sems.at[3]),
    ]
    for copy in copies:
        copy.start()

    def positions(shape, axis, block):
        row = lax.broadcasted_iota(jnp.int32, shape, axis)
        return jnp.where(row < ROWS, row + ROWS * c, row - ROWS * c) + PAIR * block

    def docs(place_in_group):
        end = 0
        total = jnp.zeros(place_in_group.shape, jnp.int32)
        for e in range(16):
            end = end + lengths[e]
            total = total + (place_in_group >= end).astype(jnp.int32)
        return total

    copies[3].wait()
    row_docs_ref[...] = docs(positions((PAIR, 1), 0, z))
    for i, step in enumerate(AROUND):
        key_docs_ref[:, i * PAIR : (i + 1) * PAIR] = docs(positions((1, PAIR), 1, (z + step + ZS) % ZS))
    for copy in copies[:3]:
        copy.wait()
    kv_rows(own_ref, key_ref, value_ref, kv_ref, 0)


def own_kv(lengths, own, key_matrix, value_matrix):
    kind = jnp.bfloat16
    return pl.pallas_call(
        own_kv_kernel,
        in_specs=[HBM] * 4,
        out_specs=[VMEM] * 6,
        out_shape=[
            jax.ShapeDtypeStruct((ROWS, WIDTH), kind),
            jax.ShapeDtypeStruct((WIDTH, HEAD_SIZE), kind),
            jax.ShapeDtypeStruct((WIDTH, HEAD_SIZE), kind),
            jax.ShapeDtypeStruct((2 * PAIR, HEAD_SIZE), kind),
            jax.ShapeDtypeStruct((PAIR, 1), jnp.int32),
            jax.ShapeDtypeStruct((1, len(AROUND) * PAIR), jnp.int32),
        ],
        scratch_shapes=[pltpu.SMEM((16,), jnp.int32), pltpu.SemaphoreType.DMA((4,))],
        compiler_params=pltpu.CompilerParams(vmem_limit_bytes=52 * 2**20),
        cost_estimate=pl.CostEstimate(flops=2**27, bytes_accessed=2**21, transcendentals=0),
    )(lengths, own, key_matrix, value_matrix)


def other_kv_kernel(other_ref, key_ref, value_ref, held_ref, kv_ref):
    kv_rows(other_ref, key_ref, value_ref, kv_ref, ROWS)


def other_kv(other, key_mine, value_mine, kv):
    return pl.pallas_call(
        other_kv_kernel,
        in_specs=[VMEM] * 4,
        out_specs=VMEM,
        out_shape=jax.ShapeDtypeStruct(kv.shape, kv.dtype),
        input_output_aliases={3: 0},
        compiler_params=pltpu.CompilerParams(vmem_limit_bytes=8 * 2**20),
        cost_estimate=pl.CostEstimate(flops=2**27, bytes_accessed=2**21, transcendentals=0),
    )(other, key_mine, value_mine, kv)


def pack_kernel(weight_ref, kv_ref, first_ref, second_ref, same_ref, packed_ref):
    packed_ref[:WIDTH] = weight_ref[...]
    packed_ref[WIDTH:] = kv_ref[...]


def pack(weight, kv, after):
    rows = weight.shape[0] + kv.shape[0]
    return pl.pallas_call(
        pack_kernel,
        in_specs=[VMEM] * 4,
        out_specs=[VMEM] * 2,
        out_shape=[
            jax.ShapeDtypeStruct(weight.shape, weight.dtype),
            jax.ShapeDtypeStruct((rows, HEAD_SIZE), weight.dtype),
        ],
        input_output_aliases={0: 0},
        compiler_params=pltpu.CompilerParams(vmem_limit_bytes=4 * 2**20),
    )(weight, kv, *after)


def head_kernel(shift, bases, own_ref, other_ref, weight_ref, *refs):
    kv, (row_docs, key_docs, _, _, keep_ref, send_ref) = refs[:5], refs[5:]
    y, x, z, c = place()
    color = (2 * x + 3 * y + z + shift) % 8
    slot = 0
    for k in range(8):
        slot = slot + jnp.where(color == k, jnp.where(c == 0, ORDER[0][k], ORDER[1][k]), 0)
    queries = jnp.concatenate(
        [
            jnp.dot(rows[...], weight_ref[:WIDTH], preferred_element_type=jnp.float32).astype(jnp.bfloat16)
            for rows in (own_ref, other_ref)
        ],
        axis=0,
    )
    factor = math.log2(math.e) / math.sqrt(HEAD_SIZE)
    docs = row_docs[...]
    scores = []
    for i in range(5):
        product = lax.dot_general(
            queries, kv[i][bases[i] : bases[i] + PAIR], (((1,), (1,)), ((), ())), preferred_element_type=jnp.float32
        )
        allowed = docs == key_docs[:, i * PAIR : (i + 1) * PAIR]
        scores.append(jnp.where(allowed, product, NEG))
    highest = functools.reduce(jnp.maximum, [jnp.max(s, axis=1, keepdims=True) for s in scores])
    summed, mixed = 0.0, 0.0
    for i in range(5):
        part = jnp.exp2((scores[i] - highest) * factor)
        summed = summed + jnp.sum(part, axis=1, keepdims=True)
        mixed = mixed + jnp.dot(
            part.astype(jnp.bfloat16), kv[i][bases[i] + PAIR : bases[i] + 2 * PAIR], preferred_element_type=jnp.float32
        )
    result = (mixed / summed).astype(jnp.bfloat16)
    columns = pl.ds(pl.multiple_of(slot * HEAD_SIZE, HEAD_SIZE), HEAD_SIZE)
    keep_ref[:, columns] = result[:ROWS]
    send_ref[:, columns] = result[ROWS:]


def one_head(shift, own, other, weight, kv, row_docs, key_docs, keep, send):
    inputs = [own, other, weight, *kv, row_docs, key_docs, keep, send]
    bases = [array.shape[0] - 2 * PAIR for array in kv]
    shape = jax.ShapeDtypeStruct(keep.shape, keep.dtype)
    return pl.pallas_call(
        functools.partial(head_kernel, shift, bases),
        in_specs=[VMEM] * len(inputs),
        out_specs=[VMEM, VMEM],
        out_shape=[shape, shape],
        input_output_aliases={len(inputs) - 2: 0, len(inputs) - 1: 1},
        compiler_params=pltpu.CompilerParams(vmem_limit_bytes=12 * 2**20),
        cost_estimate=pl.CostEstimate(flops=2**28, bytes_accessed=2**21, transcendentals=2**18),
    )(*inputs)


def join_kernel(mine_ref, other_ref, out_ref):
    y, x, z, c = place()
    out_ref[:, pl.ds(pl.multiple_of(c * HALF, HALF), HALF)] = mine_ref[...]
    out_ref[:, pl.ds(pl.multiple_of((1 - c) * HALF, HALF), HALF)] = other_ref[...]


def join(keep, arrived):
    return pl.pallas_call(
        join_kernel,
        grid=(1,),
        in_specs=[pl.BlockSpec((ROWS, HALF), lambda i: (0, 0))] * 2,
        out_specs=pl.BlockSpec((ROWS, 2 * HALF), lambda i: (0, 0)),
        out_shape=jax.ShapeDtypeStruct((ROWS, 2 * HALF), keep.dtype),
        compiler_params=pltpu.CompilerParams(vmem_limit_bytes=8 * 2**20),
    )(keep, arrived)


def body(tokens, query_weight, key_matrix, value_matrix, doc_lengths):
    weight = lax.ppermute(query_weight, AXES, first_moves())
    own, key_mine, value_mine, kv, row_docs, key_docs = own_kv(doc_lengths, tokens, key_matrix, value_matrix)
    other = swap_cores(tokens)
    kv = other_kv(other, key_mine, value_mine, kv)
    far = [lax.ppermute(kv, AXES, moves(lambda c, d=d: (0, 0, d))) for d in (2, -2)]

    weight, packed = pack(weight, kv, far)
    above = lax.ppermute(packed, AXES, moves(lambda c: (0, 0, 1)))
    below = lax.ppermute(packed, AXES, moves(lambda c: (0, 0, -1)))
    arrivals = [(0, weight), (1, above), (-1, below)]
    steps = (
        (4, lambda c: (1, 0, 1) if c == 0 else (-1, 0, -1)),
        (2, lambda c: (0, 1, 0)),
        (-2, lambda c: (0, -1, 0)),
        (3, lambda c: (1, 0, 0)),
        (-3, lambda c: (-1, 0, 0)),
    )
    for shift, step in steps:
        arrivals.append((shift, lax.ppermute(weight, AXES, moves(step))))
    kv_all = [kv, above, below, *far]

    keep = jnp.zeros((ROWS, HALF), jnp.bfloat16)
    send = jnp.zeros((ROWS, HALF), jnp.bfloat16)
    for shift, w in arrivals:
        keep, send = one_head(shift, own, other, w, kv_all, row_docs, key_docs, keep, send)
    return join(keep, swap_cores(send))


def solution(mesh):
    in_specs = (P(("dp", "ctx"), None), P(None, "ctx"), P(), P(), P("dp"))
    out_specs = P(("dp", "ctx"), None)
    return jax.shard_map(body, mesh=mesh, in_specs=in_specs, out_specs=out_specs, check_vma=False)
```

time: 83.8 us -> 89.1 us (1.063); the launches traced: 82.2 us -> 88.6 us
  waiting for transfers between devices: 10.9 us -> 17.3 us
  local copies, waits for them, and re-layouts: 4.19 us -> 0.69 us
  starting transfers between devices: 55.4 us -> 58.3 us
    ppermute x4 -> x2, starting transfers between devices: 14.9 us -> 8.39 us  [body(): lax.ppermute(kv, AXES, moves(lambda c, d=d: (0, 0, d)))]
    ppermute x7 -> x5, starting transfers between devices: 23.3 us -> 29.4 us  [body(): arrivals.append((shift, lax.ppermute(weight, AXES, moves(step))))]
    ppermute x0 -> x2, starting transfers between devices: none -> 5.28 us  [the longest x1 3.36 us: body(): below = lax.ppermute(packed, AXES, moves(lambda c: (0, 0, -1)))]
    ppermute x4 -> x2, waiting for transfers between devices: 7.12 us -> 11.2 us  [body(): lax.ppermute(kv, AXES, moves(lambda c, d=d: (0, 0, d)))]
    unnamed x12 -> x2, local copies, waits for them, and re-layouts: 4.15 us -> 0.65 us
    ppermute x7 -> x5, waiting for transfers between devices: 2.59 us -> 4.9 us  [body(): arrivals.append((shift, lax.ppermute(weight, AXES, moves(step))))]
    ppermute x2, starting transfers between devices: 15.3 us -> 13.3 us  [swap_cores(): lax.ppermute(value, AXES, [(flat(y, x, z, 1 - c), flat(y, x, z, c)) for y...]
  transfers between devices with their start and end apart: 14 -> 12, of which waited for: 4 -> 4; matrix products, arithmetic and copies ran while one was open for 0% -> 0% of each run, Pallas kernels for 12% -> 11%
where the time goes in v3:
time: 89.1 us; the launch traced here: 88.6 us
  starting transfers between devices  58.3 us (65%)
  waiting for transfers between devices  17.3 us (19%)
  Pallas kernels  12.1 us (14%)
    ppermute x5, starting transfers between devices, body(): arrivals.append((shift, lax.ppermute(weight, AXES, moves(step))))  29.4 us
    ppermute x2, starting transfers between devices, swap_cores(): lax.ppermute(value, AXES, [(flat(y, x, z, 1 - c), flat(y, x, z, c)) for y...  13.3 us
    ppermute x2, waiting for transfers between devices, body(): lax.ppermute(kv, AXES, moves(lambda c, d=d: (0, 0, d)))  11.2 us
    pallas_call x8, Pallas kernels, one_head(): pl.pallas_call(functools.partial(head_kernel, shift, bases), in_specs=[VM...  8.98 us
    ppermute x2, starting transfers between devices, body(): lax.ppermute(kv, AXES, moves(lambda c, d=d: (0, 0, d)))  8.39 us
    ppermute x5, waiting for transfers between devices, body(): arrivals.append((shift, lax.ppermute(weight, AXES, moves(step))))  4.9 us
    ppermute x1, starting transfers between devices, body(): below = lax.ppermute(packed, AXES, moves(lambda c: (0, 0, -1)))  3.36 us
    ppermute x1, starting transfers between devices, body(): above = lax.ppermute(packed, AXES, moves(lambda c: (0, 0, 1)))  1.92 us
  transfers between devices with their start and end apart: 12, of which 4 were waited for; matrix products, arithmetic and copies ran while one was open for 0% of the time, Pallas kernels for 11%

profile of v3, /device:TPU:1, one launch (start us, length us, event | category | flops | bytes accessed | tf_op | source)
XLA Modules:
  0.0 88.6 jit_solution(15978787255667192011)
XLA Ops:
  0.0 8.8 %collective-permute-start = (bf16[128,2048]{1,0:T(8,128)(2,1)}, bf16[128,2048]{1,0:T(8,128)(2,1)S(1)}, u32[]{:S(2)}, u32[]{:S(2)}) collective-permute-start(bf16[128,2048]{1,0:T(8,128)(2,1)} %own_hbm.1), channel_id=1, source_target_pairs={{1,0},{0,1},{3,2},{2,3},{5,4},{4,5},{7,6},{6,7},{9,8},{8,9},{11,10... | collective-permute-start | bytes 1572872 | tf_op jit(solution)/shard_map/ppermute | solution.py:51
  8.8 1.9 %collective-permute-start.1 = (bf16[2048,128]{1,0:T(8,128)(2,1)}, bf16[2048,128]{1,0:T(8,128)(2,1)S(1)}, u32[]{:S(2)}, u32[]{:S(2)}) collective-permute-start(bf16[2048,128]{1,0:T(8,128)(2,1)} %param.6), channel_id=1, source_target_pairs={{5,0},{15,1},{3,2},{11,3},{1,4},{8,5},{7,6},{14,7},{4,8},{10,9},{2... | collective-permute-start | bytes 1572872 | tf_op jit(solution)/shard_map/ppermute | solution.py:227
  10.7 0.0 copy-start
  10.7 0.6 copy-done
  11.4 1.8 %shard_map.55 = (bf16[128,2048]{1,0:T(8,128)(2,1)S(1)}, bf16[2048,128]{1,0:T(8,128)(2,1)S(1)}, bf16[2048,128]{1,0:T(8,128)(2,1)S(1)}, bf16[512,128]{1,0:T(8,128)...) custom-call(s32[16]{0:T(128)S(1)} %copy-done, bf16[128,2048]{1,0:T(8,128)(2,1)} %own_hbm.1, ...), custom_call_target="tpu_custom_call" | custom-call | flops 134217728 | bytes 2097152 | tf_op jit(solution)/shard_map/pallas_call | solution.py:103
  13.2 0.0 collective-permute-done.other_ref
  13.2 0.4 shard_map.56.kv_ref.refs_0_
  13.6 6.5 %collective-permute-start.2 = (bf16[512,128]{1,0:T(8,128)(2,1)S(1)}, bf16[512,128]{1,0:T(8,128)(2,1)S(1)}, u32[]{:S(2)}, u32[]{:S(2)}) collective-permute-start(bf16[512,128]{1,0:T(8,128)(2,1)S(1)} %shard_map.56.kv_ref.refs_0_), channel_id=1, source_target_pairs={{4,0},{5,1},{6,2},{7,3},{8,4},{9,5},{10,6},{11,7},{12,8},{13,9},{1... | collective-permute-start | bytes 393224 | tf_op jit(solution)/shard_map/ppermute | solution.py:231
  20.1 1.9 %collective-permute-start.3 = (bf16[512,128]{1,0:T(8,128)(2,1)S(1)}, bf16[512,128]{1,0:T(8,128)(2,1)S(1)}, u32[]{:S(2)}, u32[]{:S(2)}) collective-permute-start(bf16[512,128]{1,0:T(8,128)(2,1)S(1)} %shard_map.56.kv_ref.refs_0_), channel_id=1, source_target_pairs={{12,0},{13,1},{14,2},{15,3},{0,4},{1,5},{2,6},{3,7},{4,8},{5,9},{6... | collective-permute-start | bytes 393224 | tf_op jit(solution)/shard_map/ppermute | solution.py:231
  22.0 0.0 collective-permute-done.1.weight_ref
  22.1 11.2 %collective-permute-done.2.first_ref.refs_3_ = bf16[512,128]{1,0:T(8,128)(2,1)S(1)} collective-permute-done((bf16[512,128]{1,0:T(8,128)(2,1)S(1)}, bf16[512,128]{1,0:T(8,128)(2,1)S(1)}, u32[]{:S(2)}, u32[]{:S(2)}) %collective-permute-start.2) | collective-permute-done | bytes 131104 | tf_op jit(solution)/shard_map/ppermute | solution.py:231
  33.3 0.0 collective-permute-done.3.second_ref.refs_4_
  33.3 1.9 %collective-permute-start.5 = (bf16[2560,128]{1,0:T(8,128)(2,1)S(1)}, bf16[2560,128]{1,0:T(8,128)(2,1)S(1)}, u32[]{:S(2)}, u32[]{:S(2)}) collective-permute-start(bf16[2560,128]{1,0:T(8,128)(2,1)S(1)} %get-tuple-element.34), channel_id=1, source_target_pairs={{2,0},{3,1},{4,2},{5,3},{6,4},{7,5},{8,6},{9,7},{10,8},{11,9},{12,... | collective-permute-start | bytes 1966088 | tf_op jit(solution)/shard_map/ppermute | solution.py:234
  35.2 3.4 %collective-permute-start.6 = (bf16[2560,128]{1,0:T(8,128)(2,1)S(1)}, bf16[2560,128]{1,0:T(8,128)(2,1)S(1)}, u32[]{:S(2)}, u32[]{:S(2)}) collective-permute-start(bf16[2560,128]{1,0:T(8,128)(2,1)S(1)} %get-tuple-element.34), channel_id=1, source_target_pairs={{14,0},{15,1},{0,2},{1,3},{2,4},{3,5},{4,6},{5,7},{6,8},{7,9},{8,1... | collective-permute-start | bytes 1966088 | tf_op jit(solution)/shard_map/ppermute | solution.py:235
  38.6 3.4 %collective-permute-start.10 = (bf16[2048,128]{1,0:T(8,128)(2,1)S(1)}, bf16[2048,128]{1,0:T(8,128)(2,1)S(1)}, u32[]{:S(2)}, u32[]{:S(2)}) collective-permute-start(bf16[2048,128]{1,0:T(8,128)(2,1)S(1)} %get-tuple-element.33.weight_ref), channel_id=1, source_target_pairs={{66,0},{463,1},{68,2},{449,3},{70,4},{451,5},{72,6},{453,7},{74,8}... | collective-permute-start | bytes 1572872 | tf_op jit(solution)/shard_map/ppermute | solution.py:245
  42.0 7.2 %collective-permute-start.9 = (bf16[2048,128]{1,0:T(8,128)(2,1)S(1)}, bf16[2048,128]{1,0:T(8,128)(2,1)S(1)}, u32[]{:S(2)}, u32[]{:S(2)}) collective-permute-start(bf16[2048,128]{1,0:T(8,128)(2,1)S(1)} %get-tuple-element.33.weight_ref), channel_id=1, source_target_pairs={{16,0},{17,1},{18,2},{19,3},{20,4},{21,5},{22,6},{23,7},{24,8},{25... | collective-permute-start | bytes 1572872 | tf_op jit(solution)/shard_map/ppermute | solution.py:245
  49.2 1.9 %collective-permute-start.8 = (bf16[2048,128]{1,0:T(8,128)(2,1)S(1)}, bf16[2048,128]{1,0:T(8,128)(2,1)S(1)}, u32[]{:S(2)}, u32[]{:S(2)}) collective-permute-start(bf16[2048,128]{1,0:T(8,128)(2,1)S(1)} %get-tuple-element.33.weight_ref), channel_id=1, source_target_pairs={{48,0},{49,1},{50,2},{51,3},{52,4},{53,5},{54,6},{55,7},{56,8},{57... | collective-permute-start | bytes 1572872 | tf_op jit(solution)/shard_map/ppermute | solution.py:245
  51.2 0.0 collective-permute-done.5.refs_1_.weight_ref
  51.2 15.0 %collective-permute-start.7 = (bf16[2048,128]{1,0:T(8,128)(2,1)S(1)}, bf16[2048,128]{1,0:T(8,128)(2,1)S(1)}, u32[]{:S(2)}, u32[]{:S(2)}) collective-permute-start(bf16[2048,128]{1,0:T(8,128)(2,1)S(1)} %get-tuple-element.33.weight_ref), channel_id=1, source_target_pairs={{64,0},{65,1},{66,2},{67,3},{68,4},{69,5},{70,6},{71,7},{72,8},{73... | collective-permute-start | bytes 1572872 | tf_op jit(solution)/shard_map/ppermute | solution.py:245
  66.1 0.0 collective-permute-done.6.refs_2_.weight_ref
  66.1 1.9 %collective-permute-start.4 = (bf16[2048,128]{1,0:T(8,128)(2,1)S(1)}, bf16[2048,128]{1,0:T(8,128)(2,1)S(1)}, u32[]{:S(2)}, u32[]{:S(2)}) collective-permute-start(bf16[2048,128]{1,0:T(8,128)(2,1)S(1)} %get-tuple-element.33.weight_ref), channel_id=1, source_target_pairs={{448,0},{449,1},{450,2},{451,3},{452,4},{453,5},{454,6},{455,7},{4... | collective-permute-start | bytes 1572872 | tf_op jit(solution)/shard_map/ppermute | solution.py:245
  68.1 1.1 %shard_map.58 = (bf16[128,1024]{1,0:T(8,128)(2,1)S(1)}, bf16[128,1024]{1,0:T(8,128)(2,1)S(1)}) custom-call(bf16[128,2048]{1,0:T(8,128)(2,1)S(1)} %get-tuple-element.29.own_ref, bf16[128,2048]{1,0:T(8,128)(2,1)S(1)} %collective-permute-done.other_ref, ...), custom_call_target="tpu_custom_call", output_to_operand_aliasing={{0}: (10, {}), {1}: (11, {})} | custom-call | flops 268435456 | bytes 2097152 | tf_op jit(solution)/shard_map/pallas_call | solution.py:198
  69.3 1.1 %shard_map.59 = (bf16[128,1024]{1,0:T(8,128)(2,1)S(1)}, bf16[128,1024]{1,0:T(8,128)(2,1)S(1)}) custom-call(bf16[128,2048]{1,0:T(8,128)(2,1)S(1)} %get-tuple-element.29.own_ref, bf16[128,2048]{1,0:T(8,128)(2,1)S(1)} %collective-permute-done.other_ref, ...), custom_call_target="tpu_custom_call", output_to_operand_aliasing={{0}: (10, {}), {1}: (11, {})} | custom-call | flops 268435456 | bytes 2097152 | tf_op jit(solution)/shard_map/pallas_call | solution.py:198
  70.4 1.1 %shard_map.60 = (bf16[128,1024]{1,0:T(8,128)(2,1)S(1)}, bf16[128,1024]{1,0:T(8,128)(2,1)S(1)}) custom-call(bf16[128,2048]{1,0:T(8,128)(2,1)S(1)} %get-tuple-element.29.own_ref, bf16[128,2048]{1,0:T(8,128)(2,1)S(1)} %collective-permute-done.other_ref, ...), custom_call_target="tpu_custom_call", output_to_operand_aliasing={{0}: (10, {}), {1}: (11, {})} | custom-call | flops 268435456 | bytes 2097152 | tf_op jit(solution)/shard_map/pallas_call | solution.py:198
  71.5 0.0 collective-permute-done.10.weight_ref
  71.5 1.1 %shard_map.61 = (bf16[128,1024]{1,0:T(8,128)(2,1)S(1)}, bf16[128,1024]{1,0:T(8,128)(2,1)S(1)}) custom-call(bf16[128,2048]{1,0:T(8,128)(2,1)S(1)} %get-tuple-element.29.own_ref, bf16[128,2048]{1,0:T(8,128)(2,1)S(1)} %collective-permute-done.other_ref, ...), custom_call_target="tpu_custom_call", output_to_operand_aliasing={{0}: (10, {}), {1}: (11, {})} | custom-call | flops 268435456 | bytes 2097152 | tf_op jit(solution)/shard_map/pallas_call | solution.py:198
  72.7 0.0 collective-permute-done.9.weight_ref
  72.7 1.1 %shard_map.62 = (bf16[128,1024]{1,0:T(8,128)(2,1)S(1)}, bf16[128,1024]{1,0:T(8,128)(2,1)S(1)}) custom-call(bf16[128,2048]{1,0:T(8,128)(2,1)S(1)} %get-tuple-element.29.own_ref, bf16[128,2048]{1,0:T(8,128)(2,1)S(1)} %collective-permute-done.other_ref, ...), custom_call_target="tpu_custom_call", output_to_operand_aliasing={{0}: (10, {}), {1}: (11, {})} | custom-call | flops 268435456 | bytes 2097152 | tf_op jit(solution)/shard_map/pallas_call | solution.py:198
  73.8 0.0 collective-permute-done.8.weight_ref
  73.8 1.1 %shard_map.63 = (bf16[128,1024]{1,0:T(8,128)(2,1)S(1)}, bf16[128,1024]{1,0:T(8,128)(2,1)S(1)}) custom-call(bf16[128,2048]{1,0:T(8,128)(2,1)S(1)} %get-tuple-element.29.own_ref, bf16[128,2048]{1,0:T(8,128)(2,1)S(1)} %collective-permute-done.other_ref, ...), custom_call_target="tpu_custom_call", output_to_operand_aliasing={{0}: (10, {}), {1}: (11, {})} | custom-call | flops 268435456 | bytes 2097152 | tf_op jit(solution)/shard_map/pallas_call | solution.py:198
  74.9 1.0 %collective-permute-done.7.weight_ref = bf16[2048,128]{1,0:T(8,128)(2,1)S(1)} collective-permute-done((bf16[2048,128]{1,0:T(8,128)(2,1)S(1)}, bf16[2048,128]{1,0:T(8,128)(2,1)S(1)}, u32[]{:S(2)}, u32[]{:S(2)}) %collective-permute-start.7) | collective-permute-done | bytes 524320 | tf_op jit(solution)/shard_map/ppermute | solution.py:245
  75.9 1.1 %shard_map.64 = (bf16[128,1024]{1,0:T(8,128)(2,1)S(1)}, bf16[128,1024]{1,0:T(8,128)(2,1)S(1)}) custom-call(bf16[128,2048]{1,0:T(8,128)(2,1)S(1)} %get-tuple-element.29.own_ref, bf16[128,2048]{1,0:T(8,128)(2,1)S(1)} %collective-permute-done.other_ref, ...), custom_call_target="tpu_custom_call", output_to_operand_aliasing={{0}: (10, {}), {1}: (11, {})} | custom-call | flops 268435456 | bytes 2097152 | tf_op jit(solution)/shard_map/pallas_call | solution.py:198
  77.0 3.9 %collective-permute-done.4.weight_ref = bf16[2048,128]{1,0:T(8,128)(2,1)S(1)} collective-permute-done((bf16[2048,128]{1,0:T(8,128)(2,1)S(1)}, bf16[2048,128]{1,0:T(8,128)(2,1)S(1)}, u32[]{:S(2)}, u32[]{:S(2)}) %collective-permute-start.4) | collective-permute-done | bytes 524320 | tf_op jit(solution)/shard_map/ppermute | solution.py:245
  80.9 1.1 %shard_map.65 = (bf16[128,1024]{1,0:T(8,128)(2,1)S(1)}, bf16[128,1024]{1,0:T(8,128)(2,1)S(1)}) custom-call(bf16[128,2048]{1,0:T(8,128)(2,1)S(1)} %get-tuple-element.29.own_ref, bf16[128,2048]{1,0:T(8,128)(2,1)S(1)} %collective-permute-done.other_ref, ...), custom_call_target="tpu_custom_call", output_to_operand_aliasing={{0}: (10, {}), {1}: (11, {})} | custom-call | flops 268435456 | bytes 2097152 | tf_op jit(solution)/shard_map/pallas_call | solution.py:198
  82.1 4.6 %collective-permute-start.11 = (bf16[128,1024]{1,0:T(8,128)(2,1)S(1)}, bf16[128,1024]{1,0:T(8,128)(2,1)S(1)}, u32[]{:S(2)}, u32[]{:S(2)}) collective-permute-start(bf16[128,1024]{1,0:T(8,128)(2,1)S(1)} %get-tuple-element.52), channel_id=1, source_target_pairs={{1,0},{0,1},{3,2},{2,3},{5,4},{4,5},{7,6},{6,7},{9,8},{8,9},{11,10... | collective-permute-start | bytes 786440 | tf_op jit(solution)/shard_map/ppermute | solution.py:51
  86.6 1.1 %collective-permute-done.11.other_ref = bf16[128,1024]{1,0:T(8,128)(2,1)S(1)} collective-permute-done((bf16[128,1024]{1,0:T(8,128)(2,1)S(1)}, bf16[128,1024]{1,0:T(8,128)(2,1)S(1)}, u32[]{:S(2)}, u32[]{:S(2)}) %collective-permute-start.11) | collective-permute-done | bytes 262176 | tf_op jit(solution)/shard_map/ppermute | solution.py:51
  87.8 0.8 shard_map.66
  (3 shorter events, 0.1 us)
Async XLA Ops:
  0.0 13.2 %collective-permute-start = (bf16[128,2048]{1,0:T(8,128)(2,1)}, bf16[128,2048]{1,0:T(8,128)(2,1)S(1)}, u32[]{:S(2)}, u32[]{:S(2)}) collective-permute-start(bf16[128,2048]{1,0:T(8,128)(2,1)} %own_hbm.1), channel_id=1, source_target_pairs={{1,0},{0,1},{3,2},{2,3},{5,4},{4,5},{7,6},{6,7},{9,8},{8,9},{11,10... | collective-permute-start | bytes 1572872 | tf_op jit(solution)/shard_map/ppermute | solution.py:51
  8.8 13.3 %collective-permute-start.1 = (bf16[2048,128]{1,0:T(8,128)(2,1)}, bf16[2048,128]{1,0:T(8,128)(2,1)S(1)}, u32[]{:S(2)}, u32[]{:S(2)}) collective-permute-start(bf16[2048,128]{1,0:T(8,128)(2,1)} %param.6), channel_id=1, source_target_pairs={{5,0},{15,1},{3,2},{11,3},{1,4},{8,5},{7,6},{14,7},{4,8},{10,9},{2... | collective-permute-start | bytes 1572872 | tf_op jit(solution)/shard_map/ppermute | solution.py:227
  10.7 0.7 copy-start
  13.6 19.6 %collective-permute-start.2 = (bf16[512,128]{1,0:T(8,128)(2,1)S(1)}, bf16[512,128]{1,0:T(8,128)(2,1)S(1)}, u32[]{:S(2)}, u32[]{:S(2)}) collective-permute-start(bf16[512,128]{1,0:T(8,128)(2,1)S(1)} %shard_map.56.kv_ref.refs_0_), channel_id=1, source_target_pairs={{4,0},{5,1},{6,2},{7,3},{8,4},{9,5},{10,6},{11,7},{12,8},{13,9},{1... | collective-permute-start | bytes 393224 | tf_op jit(solution)/shard_map/ppermute | solution.py:231
  20.1 13.2 %collective-permute-start.3 = (bf16[512,128]{1,0:T(8,128)(2,1)S(1)}, bf16[512,128]{1,0:T(8,128)(2,1)S(1)}, u32[]{:S(2)}, u32[]{:S(2)}) collective-permute-start(bf16[512,128]{1,0:T(8,128)(2,1)S(1)} %shard_map.56.kv_ref.refs_0_), channel_id=1, source_target_pairs={{12,0},{13,1},{14,2},{15,3},{0,4},{1,5},{2,6},{3,7},{4,8},{5,9},{6... | collective-permute-start | bytes 393224 | tf_op jit(solution)/shard_map/ppermute | solution.py:231
  33.3 17.8 %collective-permute-start.5 = (bf16[2560,128]{1,0:T(8,128)(2,1)S(1)}, bf16[2560,128]{1,0:T(8,128)(2,1)S(1)}, u32[]{:S(2)}, u32[]{:S(2)}) collective-permute-start(bf16[2560,128]{1,0:T(8,128)(2,1)S(1)} %get-tuple-element.34), channel_id=1, source_target_pairs={{2,0},{3,1},{4,2},{5,3},{6,4},{7,5},{8,6},{9,7},{10,8},{11,9},{12,... | collective-permute-start | bytes 1966088 | tf_op jit(solution)/shard_map/ppermute | solution.py:234
  35.2 30.9 %collective-permute-start.6 = (bf16[2560,128]{1,0:T(8,128)(2,1)S(1)}, bf16[2560,128]{1,0:T(8,128)(2,1)S(1)}, u32[]{:S(2)}, u32[]{:S(2)}) collective-permute-start(bf16[2560,128]{1,0:T(8,128)(2,1)S(1)} %get-tuple-element.34), channel_id=1, source_target_pairs={{14,0},{15,1},{0,2},{1,3},{2,4},{3,5},{4,6},{5,7},{6,8},{7,9},{8,1... | collective-permute-start | bytes 1966088 | tf_op jit(solution)/shard_map/ppermute | solution.py:235
  38.6 32.9 %collective-permute-start.10 = (bf16[2048,128]{1,0:T(8,128)(2,1)S(1)}, bf16[2048,128]{1,0:T(8,128)(2,1)S(1)}, u32[]{:S(2)}, u32[]{:S(2)}) collective-permute-start(bf16[2048,128]{1,0:T(8,128)(2,1)S(1)} %get-tuple-element.33.weight_ref), channel_id=1, source_target_pairs={{66,0},{463,1},{68,2},{449,3},{70,4},{451,5},{72,6},{453,7},{74,8}... | collective-permute-start | bytes 1572872 | tf_op jit(solution)/shard_map/ppermute | solution.py:245
  42.0 30.6 %collective-permute-start.9 = (bf16[2048,128]{1,0:T(8,128)(2,1)S(1)}, bf16[2048,128]{1,0:T(8,128)(2,1)S(1)}, u32[]{:S(2)}, u32[]{:S(2)}) collective-permute-start(bf16[2048,128]{1,0:T(8,128)(2,1)S(1)} %get-tuple-element.33.weight_ref), channel_id=1, source_target_pairs={{16,0},{17,1},{18,2},{19,3},{20,4},{21,5},{22,6},{23,7},{24,8},{25... | collective-permute-start | bytes 1572872 | tf_op jit(solution)/shard_map/ppermute | solution.py:245
  49.2 24.6 %collective-permute-start.8 = (bf16[2048,128]{1,0:T(8,128)(2,1)S(1)}, bf16[2048,128]{1,0:T(8,128)(2,1)S(1)}, u32[]{:S(2)}, u32[]{:S(2)}) collective-permute-start(bf16[2048,128]{1,0:T(8,128)(2,1)S(1)} %get-tuple-element.33.weight_ref), channel_id=1, source_target_pairs={{48,0},{49,1},{50,2},{51,3},{52,4},{53,5},{54,6},{55,7},{56,8},{57... | collective-permute-start | bytes 1572872 | tf_op jit(solution)/shard_map/ppermute | solution.py:245
  51.2 24.7 %collective-permute-start.7 = (bf16[2048,128]{1,0:T(8,128)(2,1)S(1)}, bf16[2048,128]{1,0:T(8,128)(2,1)S(1)}, u32[]{:S(2)}, u32[]{:S(2)}) collective-permute-start(bf16[2048,128]{1,0:T(8,128)(2,1)S(1)} %get-tuple-element.33.weight_ref), channel_id=1, source_target_pairs={{64,0},{65,1},{66,2},{67,3},{68,4},{69,5},{70,6},{71,7},{72,8},{73... | collective-permute-start | bytes 1572872 | tf_op jit(solution)/shard_map/ppermute | solution.py:245
  66.1 14.8 %collective-permute-start.4 = (bf16[2048,128]{1,0:T(8,128)(2,1)S(1)}, bf16[2048,128]{1,0:T(8,128)(2,1)S(1)}, u32[]{:S(2)}, u32[]{:S(2)}) collective-permute-start(bf16[2048,128]{1,0:T(8,128)(2,1)S(1)} %get-tuple-element.33.weight_ref), channel_id=1, source_target_pairs={{448,0},{449,1},{450,2},{451,3},{452,4},{453,5},{454,6},{455,7},{4... | collective-permute-start | bytes 1572872 | tf_op jit(solution)/shard_map/ppermute | solution.py:245
  82.1 5.7 %collective-permute-start.11 = (bf16[128,1024]{1,0:T(8,128)(2,1)S(1)}, bf16[128,1024]{1,0:T(8,128)(2,1)S(1)}, u32[]{:S(2)}, u32[]{:S(2)}) collective-permute-start(bf16[128,1024]{1,0:T(8,128)(2,1)S(1)} %get-tuple-element.52), channel_id=1, source_target_pairs={{1,0},{0,1},{3,2},{2,3},{5,4},{4,5},{7,6},{6,7},{9,8},{8,9},{11,10... | collective-permute-start | bytes 786440 | tf_op jit(solution)/shard_map/ppermute | solution.py:51

commit v4 on v3

--- a/solution.py
+++ b/solution.py
@@ -134,24 +134,45 @@
     )(other, key_mine, value_mine, kv)
 
 
-def pack_kernel(weight_ref, kv_ref, first_ref, second_ref, same_ref, packed_ref):
-    packed_ref[:WIDTH] = weight_ref[...]
-    packed_ref[WIDTH:] = kv_ref[...]
-
-
-def pack(weight, kv, after):
-    rows = weight.shape[0] + kv.shape[0]
+def pack_kernel(weight_ref, above_ref, below_ref, same_ref, down_ref, up_ref):
+    down_ref[:WIDTH] = weight_ref[...]
+    down_ref[WIDTH:] = above_ref[...]
+    up_ref[:WIDTH] = weight_ref[...]
+    up_ref[WIDTH:] = below_ref[...]
+
+
+def pack(weight, above, below):
+    packed = jax.ShapeDtypeStruct((weight.shape[0] + above.shape[0], HEAD_SIZE), weight.dtype)
     return pl.pallas_call(
         pack_kernel,
-        in_specs=[VMEM] * 4,
-        out_specs=[VMEM] * 2,
-        out_shape=[
-            jax.ShapeDtypeStruct(weight.shape, weight.dtype),
-            jax.ShapeDtypeStruct((rows, HEAD_SIZE), weight.dtype),
-        ],
+        in_specs=[VMEM] * 3,
+        out_specs=[VMEM] * 3,
+        out_shape=[jax.ShapeDtypeStruct(weight.shape, weight.dtype), packed, packed],
         input_output_aliases={0: 0},
         compiler_params=pltpu.CompilerParams(vmem_limit_bytes=4 * 2**20),
-    )(weight, kv, *after)
+    )(weight, above, below)
+
+
+def choose_kernel(first_ref, second_ref, out_ref):
+    y, x, z, c = place()
+
+    @pl.when(c == 0)
+    def _():
+        out_ref[...] = first_ref[...]
+
+    @pl.when(c == 1)
+    def _():
+        out_ref[...] = second_ref[...]
+
+
+def choose(first, second):
+    return pl.pallas_call(
+        choose_kernel,
+        in_specs=[VMEM] * 2,
+        out_specs=VMEM,
+        out_shape=jax.ShapeDtypeStruct(first.shape, first.dtype),
+        compiler_params=pltpu.CompilerParams(vmem_limit_bytes=4 * 2**20),
+    )(first, second)
 
 
 def head_kernel(shift, bases, own_ref, other_ref, weight_ref, *refs):
@@ -228,22 +249,18 @@
     own, key_mine, value_mine, kv, row_docs, key_docs = own_kv(doc_lengths, tokens, key_matrix, value_matrix)
     other = swap_cores(tokens)
     kv = other_kv(other, key_mine, value_mine, kv)
-    far = [lax.ppermute(kv, AXES, moves(lambda c, d=d: (0, 0, d))) for d in (2, -2)]
-
-    weight, packed = pack(weight, kv, far)
-    above = lax.ppermute(packed, AXES, moves(lambda c: (0, 0, 1)))
-    below = lax.ppermute(packed, AXES, moves(lambda c: (0, 0, -1)))
-    arrivals = [(0, weight), (1, above), (-1, below)]
-    steps = (
-        (4, lambda c: (1, 0, 1) if c == 0 else (-1, 0, -1)),
-        (2, lambda c: (0, 1, 0)),
-        (-2, lambda c: (0, -1, 0)),
-        (3, lambda c: (1, 0, 0)),
-        (-3, lambda c: (-1, 0, 0)),
-    )
-    for shift, step in steps:
-        arrivals.append((shift, lax.ppermute(weight, AXES, moves(step))))
-    kv_all = [kv, above, below, *far]
+    near = [lax.ppermute(kv, AXES, moves(lambda c, d=d: (0, 0, d))) for d in (1, -1)]
+
+    weight, down, up = pack(weight, *near)
+    right = lax.ppermute(weight, AXES, moves(lambda c: (0, 1, 0)))
+    left = lax.ppermute(weight, AXES, moves(lambda c: (0, -1, 0)))
+    above = lax.ppermute(down, AXES, moves(lambda c: (0, 0, 1)))
+    below = lax.ppermute(up, AXES, moves(lambda c: (0, 0, -1)))
+    front = lax.ppermute(weight, AXES, moves(lambda c: (1, 0, 0)))
+    back = lax.ppermute(weight, AXES, moves(lambda c: (-1, 0, 0)))
+    across = lax.ppermute(choose(right, left), AXES, moves(lambda c: (0, 1, 0) if c == 0 else (0, -1, 0)))
+    arrivals = [(0, weight), (2, right), (-2, left), (1, above), (-1, below), (3, front), (-3, back), (4, across)]
+    kv_all = [kv, *near, above, below]
 
     keep = jnp.zeros((ROWS, HALF), jnp.bfloat16)
     send = jnp.zeros((ROWS, HALF), jnp.bfloat16)

time: 89.1 us -> 78.7 us (0.88)
  the two profiles are of different devices: /device:TPU:1 before, /device:TPU:17 now
where the time goes in v4:
time: 78.7 us; the launch traced here: 78.2 us
  starting transfers between devices  41.1 us (52%)
  waiting for transfers between devices  24.1 us (31%)
  Pallas kernels  12.2 us (16%)
    ppermute x2, waiting for transfers between devices, body(): lax.ppermute(kv, AXES, moves(lambda c, d=d: (0, 0, d)))  12 us
    ppermute x1, starting transfers between devices, body(): weight = lax.ppermute(query_weight, AXES, first_moves())  10.5 us
    pallas_call x8, Pallas kernels, one_head(): pl.pallas_call(functools.partial(head_kernel, shift, bases), in_specs=[VM...  8.98 us
    ppermute x2, starting transfers between devices, swap_cores(): lax.ppermute(value, AXES, [(flat(y, x, z, 1 - c), flat(y, x, z, c)) for y...  5.89 us
    ppermute x2, starting transfers between devices, body(): lax.ppermute(kv, AXES, moves(lambda c, d=d: (0, 0, d)))  5.28 us
    ppermute x1, starting transfers between devices, body(): above = lax.ppermute(down, AXES, moves(lambda c: (0, 0, 1)))  5.02 us
    ppermute x1, waiting for transfers between devices, body(): below = lax.ppermute(up, AXES, moves(lambda c: (0, 0, -1)))  5.01 us
    ppermute x1, starting transfers between devices, body(): right = lax.ppermute(weight, AXES, moves(lambda c: (0, 1, 0)))  3.86 us
  transfers between devices with their start and end apart: 12, of which 8 were waited for; matrix products, arithmetic and copies ran while one was open for 0% of the time, Pallas kernels for 13%

profile of v4, /device:TPU:17, one launch (start us, length us, event | category | flops | bytes accessed | tf_op | source)
XLA Modules:
  0.0 78.2 jit_solution(7820818881526830761)
XLA Ops:
  0.0 2.6 %collective-permute-start = (bf16[128,2048]{1,0:T(8,128)(2,1)}, bf16[128,2048]{1,0:T(8,128)(2,1)S(1)}, u32[]{:S(2)}, u32[]{:S(2)}) collective-permute-start(bf16[128,2048]{1,0:T(8,128)(2,1)} %own_hbm.1), channel_id=1, source_target_pairs={{1,0},{0,1},{3,2},{2,3},{5,4},{4,5},{7,6},{6,7},{9,8},{8,9},{11,10... | collective-permute-start | bytes 1572872 | tf_op jit(solution)/shard_map/ppermute | solution.py:51
  2.6 10.5 %collective-permute-start.1 = (bf16[2048,128]{1,0:T(8,128)(2,1)}, bf16[2048,128]{1,0:T(8,128)(2,1)S(1)}, u32[]{:S(2)}, u32[]{:S(2)}) collective-permute-start(bf16[2048,128]{1,0:T(8,128)(2,1)} %param.6), channel_id=1, source_target_pairs={{5,0},{15,1},{3,2},{11,3},{1,4},{8,5},{7,6},{14,7},{4,8},{10,9},{2... | collective-permute-start | bytes 1572872 | tf_op jit(solution)/shard_map/ppermute | solution.py:248
  13.1 0.0 copy-start
  13.1 0.6 copy-done
  13.8 1.8 %shard_map.55 = (bf16[128,2048]{1,0:T(8,128)(2,1)S(1)}, bf16[2048,128]{1,0:T(8,128)(2,1)S(1)}, bf16[2048,128]{1,0:T(8,128)(2,1)S(1)}, bf16[512,128]{1,0:T(8,128)...) custom-call(s32[16]{0:T(128)S(1)} %copy-done, bf16[128,2048]{1,0:T(8,128)(2,1)} %own_hbm.1, ...), custom_call_target="tpu_custom_call" | custom-call | flops 134217728 | bytes 2097152 | tf_op jit(solution)/shard_map/pallas_call | solution.py:103
  15.6 0.0 collective-permute-done.other_ref
  15.6 0.4 shard_map.56.refs_0_
  16.1 2.1 %collective-permute-start.2 = (bf16[512,128]{1,0:T(8,128)(2,1)S(1)}, bf16[512,128]{1,0:T(8,128)(2,1)S(1)}, u32[]{:S(2)}, u32[]{:S(2)}) collective-permute-start(bf16[512,128]{1,0:T(8,128)(2,1)S(1)} %shard_map.56.refs_0_), channel_id=1, source_target_pairs={{2,0},{3,1},{4,2},{5,3},{6,4},{7,5},{8,6},{9,7},{10,8},{11,9},{12,... | collective-permute-start | bytes 393224 | tf_op jit(solution)/shard_map/ppermute | solution.py:252
  18.1 3.2 %collective-permute-start.3 = (bf16[512,128]{1,0:T(8,128)(2,1)S(1)}, bf16[512,128]{1,0:T(8,128)(2,1)S(1)}, u32[]{:S(2)}, u32[]{:S(2)}) collective-permute-start(bf16[512,128]{1,0:T(8,128)(2,1)S(1)} %shard_map.56.refs_0_), channel_id=1, source_target_pairs={{14,0},{15,1},{0,2},{1,3},{2,4},{3,5},{4,6},{5,7},{6,8},{7,9},{8,1... | collective-permute-start | bytes 393224 | tf_op jit(solution)/shard_map/ppermute | solution.py:252
  21.3 0.8 collective-permute-done.1.weight_ref
  22.1 1.5 %collective-permute-done.2.above_ref.refs_1_ = bf16[512,128]{1,0:T(8,128)(2,1)S(1)} collective-permute-done((bf16[512,128]{1,0:T(8,128)(2,1)S(1)}, bf16[512,128]{1,0:T(8,128)(2,1)S(1)}, u32[]{:S(2)}, u32[]{:S(2)}) %collective-permute-start.2) | collective-permute-done | bytes 131104 | tf_op jit(solution)/shard_map/ppermute | solution.py:252
  23.7 10.4 %collective-permute-done.3.below_ref.refs_2_ = bf16[512,128]{1,0:T(8,128)(2,1)S(1)} collective-permute-done((bf16[512,128]{1,0:T(8,128)(2,1)S(1)}, bf16[512,128]{1,0:T(8,128)(2,1)S(1)}, u32[]{:S(2)}, u32[]{:S(2)}) %collective-permute-start.3) | collective-permute-done | bytes 131104 | tf_op jit(solution)/shard_map/ppermute | solution.py:252
  34.1 0.1 shard_map.57
  34.2 3.9 %collective-permute-start.4 = (bf16[2048,128]{1,0:T(8,128)(2,1)S(1)}, bf16[2048,128]{1,0:T(8,128)(2,1)S(1)}, u32[]{:S(2)}, u32[]{:S(2)}) collective-permute-start(bf16[2048,128]{1,0:T(8,128)(2,1)S(1)} %get-tuple-element.34.weight_ref), channel_id=1, source_target_pairs={{16,0},{17,1},{18,2},{19,3},{20,4},{21,5},{22,6},{23,7},{24,8},{25... | collective-permute-start | bytes 1572872 | tf_op jit(solution)/shard_map/ppermute | solution.py:255
  38.0 1.9 %collective-permute-start.5 = (bf16[2048,128]{1,0:T(8,128)(2,1)S(1)}, bf16[2048,128]{1,0:T(8,128)(2,1)S(1)}, u32[]{:S(2)}, u32[]{:S(2)}) collective-permute-start(bf16[2048,128]{1,0:T(8,128)(2,1)S(1)} %get-tuple-element.34.weight_ref), channel_id=1, source_target_pairs={{48,0},{49,1},{50,2},{51,3},{52,4},{53,5},{54,6},{55,7},{56,8},{57... | collective-permute-start | bytes 1572872 | tf_op jit(solution)/shard_map/ppermute | solution.py:256
  40.0 5.0 %collective-permute-start.7 = (bf16[2560,128]{1,0:T(8,128)(2,1)S(1)}, bf16[2560,128]{1,0:T(8,128)(2,1)S(1)}, u32[]{:S(2)}, u32[]{:S(2)}) collective-permute-start(bf16[2560,128]{1,0:T(8,128)(2,1)S(1)} %get-tuple-element.35), channel_id=1, source_target_pairs={{2,0},{3,1},{4,2},{5,3},{6,4},{7,5},{8,6},{9,7},{10,8},{11,9},{12,... | collective-permute-start | bytes 1966088 | tf_op jit(solution)/shard_map/ppermute | solution.py:257
  45.0 1.9 %collective-permute-start.8 = (bf16[2560,128]{1,0:T(8,128)(2,1)S(1)}, bf16[2560,128]{1,0:T(8,128)(2,1)S(1)}, u32[]{:S(2)}, u32[]{:S(2)}) collective-permute-start(bf16[2560,128]{1,0:T(8,128)(2,1)S(1)} %get-tuple-element.36), channel_id=1, source_target_pairs={{14,0},{15,1},{0,2},{1,3},{2,4},{3,5},{4,6},{5,7},{6,8},{7,9},{8,1... | collective-permute-start | bytes 1966088 | tf_op jit(solution)/shard_map/ppermute | solution.py:258
  46.9 1.9 %collective-permute-start.10 = (bf16[2048,128]{1,0:T(8,128)(2,1)S(1)}, bf16[2048,128]{1,0:T(8,128)(2,1)S(1)}, u32[]{:S(2)}, u32[]{:S(2)}) collective-permute-start(bf16[2048,128]{1,0:T(8,128)(2,1)S(1)} %get-tuple-element.34.weight_ref), channel_id=1, source_target_pairs={{64,0},{65,1},{66,2},{67,3},{68,4},{69,5},{70,6},{71,7},{72,8},{73... | collective-permute-start | bytes 1572872 | tf_op jit(solution)/shard_map/ppermute | solution.py:259
  48.9 0.9 %collective-permute-done.4.first_ref.weight_ref = bf16[2048,128]{1,0:T(8,128)(2,1)S(1)} collective-permute-done((bf16[2048,128]{1,0:T(8,128)(2,1)S(1)}, bf16[2048,128]{1,0:T(8,128)(2,1)S(1)}, u32[]{:S(2)}, u32[]{:S(2)}) %collective-permute-start.4) | collective-permute-done | bytes 524320 | tf_op jit(solution)/shard_map/ppermute | solution.py:255
  49.7 2.5 %collective-permute-start.9 = (bf16[2048,128]{1,0:T(8,128)(2,1)S(1)}, bf16[2048,128]{1,0:T(8,128)(2,1)S(1)}, u32[]{:S(2)}, u32[]{:S(2)}) collective-permute-start(bf16[2048,128]{1,0:T(8,128)(2,1)S(1)} %get-tuple-element.34.weight_ref), channel_id=1, source_target_pairs={{448,0},{449,1},{450,2},{451,3},{452,4},{453,5},{454,6},{455,7},{4... | collective-permute-start | bytes 1572872 | tf_op jit(solution)/shard_map/ppermute | solution.py:260
  52.2 1.2 %collective-permute-done.5.second_ref.weight_ref = bf16[2048,128]{1,0:T(8,128)(2,1)S(1)} collective-permute-done((bf16[2048,128]{1,0:T(8,128)(2,1)S(1)}, bf16[2048,128]{1,0:T(8,128)(2,1)S(1)}, u32[]{:S(2)}, u32[]{:S(2)}) %collective-permute-start.5) | collective-permute-done | bytes 524320 | tf_op jit(solution)/shard_map/ppermute | solution.py:256
  53.4 2.2 %collective-permute-start.6 = (bf16[2048,128]{1,0:T(8,128)(2,1)S(1)}, bf16[2048,128]{1,0:T(8,128)(2,1)S(1)}, u32[]{:S(2)}, u32[]{:S(2)}) collective-permute-start(bf16[2048,128]{1,0:T(8,128)(2,1)S(1)} %shard_map.58), channel_id=1, source_target_pairs={{16,0},{49,1},{18,2},{51,3},{20,4},{53,5},{22,6},{55,7},{24,8},{57... | collective-permute-start | bytes 1572872 | tf_op jit(solution)/shard_map/ppermute | solution.py:261
  55.7 3.1 %collective-permute-done.7.refs_3_.weight_ref = bf16[2560,128]{1,0:T(8,128)(2,1)S(1)} collective-permute-done((bf16[2560,128]{1,0:T(8,128)(2,1)S(1)}, bf16[2560,128]{1,0:T(8,128)(2,1)S(1)}, u32[]{:S(2)}, u32[]{:S(2)}) %collective-permute-start.7) | collective-permute-done | bytes 655392 | tf_op jit(solution)/shard_map/ppermute | solution.py:257
  58.8 5.0 %collective-permute-done.8.refs_4_.weight_ref = bf16[2560,128]{1,0:T(8,128)(2,1)S(1)} collective-permute-done((bf16[2560,128]{1,0:T(8,128)(2,1)S(1)}, bf16[2560,128]{1,0:T(8,128)(2,1)S(1)}, u32[]{:S(2)}, u32[]{:S(2)}) %collective-permute-start.8) | collective-permute-done | bytes 655392 | tf_op jit(solution)/shard_map/ppermute | solution.py:258
  63.9 1.1 %shard_map.59 = (bf16[128,1024]{1,0:T(8,128)(2,1)S(1)}, bf16[128,1024]{1,0:T(8,128)(2,1)S(1)}) custom-call(bf16[128,2048]{1,0:T(8,128)(2,1)S(1)} %get-tuple-element.30.own_ref, bf16[128,2048]{1,0:T(8,128)(2,1)S(1)} %collective-permute-done.other_ref, ...), custom_call_target="tpu_custom_call", output_to_operand_aliasing={{0}: (10, {}), {1}: (11, {})} | custom-call | flops 268435456 | bytes 2097152 | tf_op jit(solution)/shard_map/pallas_call | solution.py:219
  65.0 1.1 %shard_map.60 = (bf16[128,1024]{1,0:T(8,128)(2,1)S(1)}, bf16[128,1024]{1,0:T(8,128)(2,1)S(1)}) custom-call(bf16[128,2048]{1,0:T(8,128)(2,1)S(1)} %get-tuple-element.30.own_ref, bf16[128,2048]{1,0:T(8,128)(2,1)S(1)} %collective-permute-done.other_ref, ...), custom_call_target="tpu_custom_call", output_to_operand_aliasing={{0}: (10, {}), {1}: (11, {})} | custom-call | flops 268435456 | bytes 2097152 | tf_op jit(solution)/shard_map/pallas_call | solution.py:219
  66.1 1.1 %shard_map.61 = (bf16[128,1024]{1,0:T(8,128)(2,1)S(1)}, bf16[128,1024]{1,0:T(8,128)(2,1)S(1)}) custom-call(bf16[128,2048]{1,0:T(8,128)(2,1)S(1)} %get-tuple-element.30.own_ref, bf16[128,2048]{1,0:T(8,128)(2,1)S(1)} %collective-permute-done.other_ref, ...), custom_call_target="tpu_custom_call", output_to_operand_aliasing={{0}: (10, {}), {1}: (11, {})} | custom-call | flops 268435456 | bytes 2097152 | tf_op jit(solution)/shard_map/pallas_call | solution.py:219
  67.3 1.1 %shard_map.62 = (bf16[128,1024]{1,0:T(8,128)(2,1)S(1)}, bf16[128,1024]{1,0:T(8,128)(2,1)S(1)}) custom-call(bf16[128,2048]{1,0:T(8,128)(2,1)S(1)} %get-tuple-element.30.own_ref, bf16[128,2048]{1,0:T(8,128)(2,1)S(1)} %collective-permute-done.other_ref, ...), custom_call_target="tpu_custom_call", output_to_operand_aliasing={{0}: (10, {}), {1}: (11, {})} | custom-call | flops 268435456 | bytes 2097152 | tf_op jit(solution)/shard_map/pallas_call | solution.py:219
  68.4 1.1 %shard_map.63 = (bf16[128,1024]{1,0:T(8,128)(2,1)S(1)}, bf16[128,1024]{1,0:T(8,128)(2,1)S(1)}) custom-call(bf16[128,2048]{1,0:T(8,128)(2,1)S(1)} %get-tuple-element.30.own_ref, bf16[128,2048]{1,0:T(8,128)(2,1)S(1)} %collective-permute-done.other_ref, ...), custom_call_target="tpu_custom_call", output_to_operand_aliasing={{0}: (10, {}), {1}: (11, {})} | custom-call | flops 268435456 | bytes 2097152 | tf_op jit(solution)/shard_map/pallas_call | solution.py:219
  69.5 0.0 collective-permute-done.10.weight_ref
  69.5 1.1 %shard_map.64 = (bf16[128,1024]{1,0:T(8,128)(2,1)S(1)}, bf16[128,1024]{1,0:T(8,128)(2,1)S(1)}) custom-call(bf16[128,2048]{1,0:T(8,128)(2,1)S(1)} %get-tuple-element.30.own_ref, bf16[128,2048]{1,0:T(8,128)(2,1)S(1)} %collective-permute-done.other_ref, ...), custom_call_target="tpu_custom_call", output_to_operand_aliasing={{0}: (10, {}), {1}: (11, {})} | custom-call | flops 268435456 | bytes 2097152 | tf_op jit(solution)/shard_map/pallas_call | solution.py:219
  70.7 0.0 collective-permute-done.9.weight_ref
  70.7 1.1 %shard_map.65 = (bf16[128,1024]{1,0:T(8,128)(2,1)S(1)}, bf16[128,1024]{1,0:T(8,128)(2,1)S(1)}) custom-call(bf16[128,2048]{1,0:T(8,128)(2,1)S(1)} %get-tuple-element.30.own_ref, bf16[128,2048]{1,0:T(8,128)(2,1)S(1)} %collective-permute-done.other_ref, ...), custom_call_target="tpu_custom_call", output_to_operand_aliasing={{0}: (10, {}), {1}: (11, {})} | custom-call | flops 268435456 | bytes 2097152 | tf_op jit(solution)/shard_map/pallas_call | solution.py:219
  71.8 0.0 collective-permute-done.6.weight_ref
  71.8 1.1 %shard_map.66 = (bf16[128,1024]{1,0:T(8,128)(2,1)S(1)}, bf16[128,1024]{1,0:T(8,128)(2,1)S(1)}) custom-call(bf16[128,2048]{1,0:T(8,128)(2,1)S(1)} %get-tuple-element.30.own_ref, bf16[128,2048]{1,0:T(8,128)(2,1)S(1)} %collective-permute-done.other_ref, ...), custom_call_target="tpu_custom_call", output_to_operand_aliasing={{0}: (10, {}), {1}: (11, {})} | custom-call | flops 268435456 | bytes 2097152 | tf_op jit(solution)/shard_map/pallas_call | solution.py:219
  72.9 3.3 %collective-permute-start.11 = (bf16[128,1024]{1,0:T(8,128)(2,1)S(1)}, bf16[128,1024]{1,0:T(8,128)(2,1)S(1)}, u32[]{:S(2)}, u32[]{:S(2)}) collective-permute-start(bf16[128,1024]{1,0:T(8,128)(2,1)S(1)} %get-tuple-element.54), channel_id=1, source_target_pairs={{1,0},{0,1},{3,2},{2,3},{5,4},{4,5},{7,6},{6,7},{9,8},{8,9},{11,10... | collective-permute-start | bytes 786440 | tf_op jit(solution)/shard_map/ppermute | solution.py:51
  76.3 1.1 %collective-permute-done.11.other_ref = bf16[128,1024]{1,0:T(8,128)(2,1)S(1)} collective-permute-done((bf16[128,1024]{1,0:T(8,128)(2,1)S(1)}, bf16[128,1024]{1,0:T(8,128)(2,1)S(1)}, u32[]{:S(2)}, u32[]{:S(2)}) %collective-permute-start.11) | collective-permute-done | bytes 262176 | tf_op jit(solution)/shard_map/ppermute | solution.py:51
  77.4 0.8 %shard_map.67 = bf16[128,2048]{1,0:T(8,128)(2,1)} custom-call(bf16[128,1024]{1,0:T(8,128)(2,1)S(1)} %get-tuple-element.53.mine_ref, bf16[128,1024]{1,0:T(8,128)(2,1)S(1)} %collective-permute-done.11.other_ref), custom_call_target="tpu_custom_call" | custom-call | tf_op jit(solution)/shard_map/pallas_call | solution.py:237
  (3 shorter events, 0.1 us)
Async XLA Ops:
  0.0 15.6 %collective-permute-start = (bf16[128,2048]{1,0:T(8,128)(2,1)}, bf16[128,2048]{1,0:T(8,128)(2,1)S(1)}, u32[]{:S(2)}, u32[]{:S(2)}) collective-permute-start(bf16[128,2048]{1,0:T(8,128)(2,1)} %own_hbm.1), channel_id=1, source_target_pairs={{1,0},{0,1},{3,2},{2,3},{5,4},{4,5},{7,6},{6,7},{9,8},{8,9},{11,10... | collective-permute-start | bytes 1572872 | tf_op jit(solution)/shard_map/ppermute | solution.py:51
  2.6 19.5 %collective-permute-start.1 = (bf16[2048,128]{1,0:T(8,128)(2,1)}, bf16[2048,128]{1,0:T(8,128)(2,1)S(1)}, u32[]{:S(2)}, u32[]{:S(2)}) collective-permute-start(bf16[2048,128]{1,0:T(8,128)(2,1)} %param.6), channel_id=1, source_target_pairs={{5,0},{15,1},{3,2},{11,3},{1,4},{8,5},{7,6},{14,7},{4,8},{10,9},{2... | collective-permute-start | bytes 1572872 | tf_op jit(solution)/shard_map/ppermute | solution.py:248
  13.1 0.7 copy-start
  16.1 7.6 %collective-permute-start.2 = (bf16[512,128]{1,0:T(8,128)(2,1)S(1)}, bf16[512,128]{1,0:T(8,128)(2,1)S(1)}, u32[]{:S(2)}, u32[]{:S(2)}) collective-permute-start(bf16[512,128]{1,0:T(8,128)(2,1)S(1)} %shard_map.56.refs_0_), channel_id=1, source_target_pairs={{2,0},{3,1},{4,2},{5,3},{6,4},{7,5},{8,6},{9,7},{10,8},{11,9},{12,... | collective-permute-start | bytes 393224 | tf_op jit(solution)/shard_map/ppermute | solution.py:252
  18.1 16.0 %collective-permute-start.3 = (bf16[512,128]{1,0:T(8,128)(2,1)S(1)}, bf16[512,128]{1,0:T(8,128)(2,1)S(1)}, u32[]{:S(2)}, u32[]{:S(2)}) collective-permute-start(bf16[512,128]{1,0:T(8,128)(2,1)S(1)} %shard_map.56.refs_0_), channel_id=1, source_target_pairs={{14,0},{15,1},{0,2},{1,3},{2,4},{3,5},{4,6},{5,7},{6,8},{7,9},{8,1... | collective-permute-start | bytes 393224 | tf_op jit(solution)/shard_map/ppermute | solution.py:252
  34.2 15.6 %collective-permute-start.4 = (bf16[2048,128]{1,0:T(8,128)(2,1)S(1)}, bf16[2048,128]{1,0:T(8,128)(2,1)S(1)}, u32[]{:S(2)}, u32[]{:S(2)}) collective-permute-start(bf16[2048,128]{1,0:T(8,128)(2,1)S(1)} %get-tuple-element.34.weight_ref), channel_id=1, source_target_pairs={{16,0},{17,1},{18,2},{19,3},{20,4},{21,5},{22,6},{23,7},{24,8},{25... | collective-permute-start | bytes 1572872 | tf_op jit(solution)/shard_map/ppermute | solution.py:255
  38.0 15.4 %collective-permute-start.5 = (bf16[2048,128]{1,0:T(8,128)(2,1)S(1)}, bf16[2048,128]{1,0:T(8,128)(2,1)S(1)}, u32[]{:S(2)}, u32[]{:S(2)}) collective-permute-start(bf16[2048,128]{1,0:T(8,128)(2,1)S(1)} %get-tuple-element.34.weight_ref), channel_id=1, source_target_pairs={{48,0},{49,1},{50,2},{51,3},{52,4},{53,5},{54,6},{55,7},{56,8},{57... | collective-permute-start | bytes 1572872 | tf_op jit(solution)/shard_map/ppermute | solution.py:256
  40.0 18.9 %collective-permute-start.7 = (bf16[2560,128]{1,0:T(8,128)(2,1)S(1)}, bf16[2560,128]{1,0:T(8,128)(2,1)S(1)}, u32[]{:S(2)}, u32[]{:S(2)}) collective-permute-start(bf16[2560,128]{1,0:T(8,128)(2,1)S(1)} %get-tuple-element.35), channel_id=1, source_target_pairs={{2,0},{3,1},{4,2},{5,3},{6,4},{7,5},{8,6},{9,7},{10,8},{11,9},{12,... | collective-permute-start | bytes 1966088 | tf_op jit(solution)/shard_map/ppermute | solution.py:257
  45.0 18.8 %collective-permute-start.8 = (bf16[2560,128]{1,0:T(8,128)(2,1)S(1)}, bf16[2560,128]{1,0:T(8,128)(2,1)S(1)}, u32[]{:S(2)}, u32[]{:S(2)}) collective-permute-start(bf16[2560,128]{1,0:T(8,128)(2,1)S(1)} %get-tuple-element.36), channel_id=1, source_target_pairs={{14,0},{15,1},{0,2},{1,3},{2,4},{3,5},{4,6},{5,7},{6,8},{7,9},{8,1... | collective-permute-start | bytes 1966088 | tf_op jit(solution)/shard_map/ppermute | solution.py:258
  46.9 22.6 %collective-permute-start.10 = (bf16[2048,128]{1,0:T(8,128)(2,1)S(1)}, bf16[2048,128]{1,0:T(8,128)(2,1)S(1)}, u32[]{:S(2)}, u32[]{:S(2)}) collective-permute-start(bf16[2048,128]{1,0:T(8,128)(2,1)S(1)} %get-tuple-element.34.weight_ref), channel_id=1, source_target_pairs={{64,0},{65,1},{66,2},{67,3},{68,4},{69,5},{70,6},{71,7},{72,8},{73... | collective-permute-start | bytes 1572872 | tf_op jit(solution)/shard_map/ppermute | solution.py:259
  49.7 20.9 %collective-permute-start.9 = (bf16[2048,128]{1,0:T(8,128)(2,1)S(1)}, bf16[2048,128]{1,0:T(8,128)(2,1)S(1)}, u32[]{:S(2)}, u32[]{:S(2)}) collective-permute-start(bf16[2048,128]{1,0:T(8,128)(2,1)S(1)} %get-tuple-element.34.weight_ref), channel_id=1, source_target_pairs={{448,0},{449,1},{450,2},{451,3},{452,4},{453,5},{454,6},{455,7},{4... | collective-permute-start | bytes 1572872 | tf_op jit(solution)/shard_map/ppermute | solution.py:260
  53.4 18.4 %collective-permute-start.6 = (bf16[2048,128]{1,0:T(8,128)(2,1)S(1)}, bf16[2048,128]{1,0:T(8,128)(2,1)S(1)}, u32[]{:S(2)}, u32[]{:S(2)}) collective-permute-start(bf16[2048,128]{1,0:T(8,128)(2,1)S(1)} %shard_map.58), channel_id=1, source_target_pairs={{16,0},{49,1},{18,2},{51,3},{20,4},{53,5},{22,6},{55,7},{24,8},{57... | collective-permute-start | bytes 1572872 | tf_op jit(solution)/shard_map/ppermute | solution.py:261
  72.9 4.5 %collective-permute-start.11 = (bf16[128,1024]{1,0:T(8,128)(2,1)S(1)}, bf16[128,1024]{1,0:T(8,128)(2,1)S(1)}, u32[]{:S(2)}, u32[]{:S(2)}) collective-permute-start(bf16[128,1024]{1,0:T(8,128)(2,1)S(1)} %get-tuple-element.54), channel_id=1, source_target_pairs={{1,0},{0,1},{3,2},{2,3},{5,4},{4,5},{7,6},{6,7},{9,8},{8,9},{11,10... | collective-permute-start | bytes 786440 | tf_op jit(solution)/shard_map/ppermute | solution.py:51

commit v5 on v4

--- a/solution.py
+++ b/solution.py
@@ -134,7 +134,22 @@
     )(other, key_mine, value_mine, kv)
 
 
-def pack_kernel(weight_ref, above_ref, below_ref, same_ref, down_ref, up_ref):
+def gate_kernel(*refs):
+    pass
+
+
+def gate(value, *after):
+    return pl.pallas_call(
+        gate_kernel,
+        in_specs=[VMEM] * (1 + len(after)),
+        out_specs=VMEM,
+        out_shape=jax.ShapeDtypeStruct(value.shape, value.dtype),
+        input_output_aliases={0: 0},
+        compiler_params=pltpu.CompilerParams(vmem_limit_bytes=2**20),
+    )(value, *after)
+
+
+def pack_kernel(weight_ref, above_ref, below_ref, down_ref, up_ref):
     down_ref[:WIDTH] = weight_ref[...]
     down_ref[WIDTH:] = above_ref[...]
     up_ref[:WIDTH] = weight_ref[...]
@@ -146,9 +161,8 @@
     return pl.pallas_call(
         pack_kernel,
         in_specs=[VMEM] * 3,
-        out_specs=[VMEM] * 3,
-        out_shape=[jax.ShapeDtypeStruct(weight.shape, weight.dtype), packed, packed],
-        input_output_aliases={0: 0},
+        out_specs=[VMEM] * 2,
+        out_shape=[packed, packed],
         compiler_params=pltpu.CompilerParams(vmem_limit_bytes=4 * 2**20),
     )(weight, above, below)
 
@@ -175,22 +189,8 @@
     )(first, second)
 
 
-def head_kernel(shift, bases, own_ref, other_ref, weight_ref, *refs):
-    kv, (row_docs, key_docs, _, _, keep_ref, send_ref) = refs[:5], refs[5:]
-    y, x, z, c = place()
-    color = (2 * x + 3 * y + z + shift) % 8
-    slot = 0
-    for k in range(8):
-        slot = slot + jnp.where(color == k, jnp.where(c == 0, ORDER[0][k], ORDER[1][k]), 0)
-    queries = jnp.concatenate(
-        [
-            jnp.dot(rows[...], weight_ref[:WIDTH], preferred_element_type=jnp.float32).astype(jnp.bfloat16)
-            for rows in (own_ref, other_ref)
-        ],
-        axis=0,
-    )
+def attend(queries, kv, bases, docs, key_docs):
     factor = math.log2(math.e) / math.sqrt(HEAD_SIZE)
-    docs = row_docs[...]
     scores = []
     for i in range(5):
         product = lax.dot_general(
@@ -206,23 +206,46 @@
         mixed = mixed + jnp.dot(
             part.astype(jnp.bfloat16), kv[i][bases[i] + PAIR : bases[i] + 2 * PAIR], preferred_element_type=jnp.float32
         )
-    result = (mixed / summed).astype(jnp.bfloat16)
-    columns = pl.ds(pl.multiple_of(slot * HEAD_SIZE, HEAD_SIZE), HEAD_SIZE)
-    keep_ref[:, columns] = result[:ROWS]
-    send_ref[:, columns] = result[ROWS:]
-
-
-def one_head(shift, own, other, weight, kv, row_docs, key_docs, keep, send):
-    inputs = [own, other, weight, *kv, row_docs, key_docs, keep, send]
+    return (mixed / summed).astype(jnp.bfloat16)
+
+
+def heads_kernel(shifts, bases, own_ref, other_ref, *refs):
+    weights, refs = refs[: len(shifts)], refs[len(shifts) :]
+    kv, (row_docs, key_docs, _, _, keep_ref, send_ref) = refs[:5], refs[5:]
+    y, x, z, c = place()
+    docs = row_docs[...]
+    for first in range(0, len(shifts), 2):
+        pair = weights[first : first + 2]
+        matrix = jnp.concatenate([w[:WIDTH] for w in pair], axis=1)
+        queries = jnp.concatenate(
+            [
+                jnp.dot(rows[...], matrix, preferred_element_type=jnp.float32).astype(jnp.bfloat16)
+                for rows in (own_ref, other_ref)
+            ],
+            axis=0,
+        )
+        for i, shift in enumerate(shifts[first : first + 2]):
+            color = (2 * x + 3 * y + z + shift) % 8
+            slot = 0
+            for k in range(8):
+                slot = slot + jnp.where(color == k, jnp.where(c == 0, ORDER[0][k], ORDER[1][k]), 0)
+            result = attend(queries[:, i * HEAD_SIZE : (i + 1) * HEAD_SIZE], kv, bases, docs, key_docs)
+            columns = pl.ds(pl.multiple_of(slot * HEAD_SIZE, HEAD_SIZE), HEAD_SIZE)
+            keep_ref[:, columns] = result[:ROWS]
+            send_ref[:, columns] = result[ROWS:]
+
+
+def some_heads(arrivals, own, other, kv, row_docs, key_docs, keep, send):
+    inputs = [own, other, *(w for _, w in arrivals), *kv, row_docs, key_docs, keep, send]
     bases = [array.shape[0] - 2 * PAIR for array in kv]
     shape = jax.ShapeDtypeStruct(keep.shape, keep.dtype)
     return pl.pallas_call(
-        functools.partial(head_kernel, shift, bases),
+        functools.partial(heads_kernel, tuple(shift for shift, _ in arrivals), bases),
         in_specs=[VMEM] * len(inputs),
         out_specs=[VMEM, VMEM],
         out_shape=[shape, shape],
         input_output_aliases={len(inputs) - 2: 0, len(inputs) - 1: 1},
-        compiler_params=pltpu.CompilerParams(vmem_limit_bytes=12 * 2**20),
+        compiler_params=pltpu.CompilerParams(vmem_limit_bytes=16 * 2**20),
         cost_estimate=pl.CostEstimate(flops=2**28, bytes_accessed=2**21, transcendentals=2**18),
     )(*inputs)
 
@@ -251,9 +274,10 @@
     kv = other_kv(other, key_mine, value_mine, kv)
     near = [lax.ppermute(kv, AXES, moves(lambda c, d=d: (0, 0, d))) for d in (1, -1)]
 
-    weight, down, up = pack(weight, *near)
+    weight = gate(weight, *near)
     right = lax.ppermute(weight, AXES, moves(lambda c: (0, 1, 0)))
     left = lax.ppermute(weight, AXES, moves(lambda c: (0, -1, 0)))
+    down, up = pack(weight, *near)
     above = lax.ppermute(down, AXES, moves(lambda c: (0, 0, 1)))
     below = lax.ppermute(up, AXES, moves(lambda c: (0, 0, -1)))
     front = lax.ppermute(weight, AXES, moves(lambda c: (1, 0, 0)))
@@ -264,8 +288,8 @@
 
     keep = jnp.zeros((ROWS, HALF), jnp.bfloat16)
     send = jnp.zeros((ROWS, HALF), jnp.bfloat16)
-    for shift, w in arrivals:
-        keep, send = one_head(shift, own, other, w, kv_all, row_docs, key_docs, keep, send)
+    for some in (arrivals[:4], arrivals[4:6], arrivals[6:]):
+        keep, send = some_heads(some, own, other, kv_all, row_docs, key_docs, keep, send)
     return join(keep, swap_cores(send))
 
 

time: 78.7 us -> 76.5 us (0.972)
  Pallas kernels: 12.2 us -> 9.98 us
    pallas_call x9 -> x5, Pallas kernels: 9.07 us -> 6.85 us  [the longest x3 6.76 us: some_heads(): pl.pallas_call(functools.partial(heads_kernel, tuple((shift for shift, _...]
  transfers between devices with their start and end apart: 12 -> 12, of which waited for: 8 -> 8; matrix products, arithmetic and copies ran while one was open for 0% -> 0% of each run, Pallas kernels for 13% -> 10%
where the time goes in v5:
time: 76.5 us; the launch traced here: 76.1 us
  starting transfers between devices  41.2 us (54%)
  waiting for transfers between devices  24 us (31%)
  Pallas kernels  9.98 us (13%)
    ppermute x2, waiting for transfers between devices, body(): lax.ppermute(kv, AXES, moves(lambda c, d=d: (0, 0, d)))  12 us
    ppermute x1, starting transfers between devices, body(): weight = lax.ppermute(query_weight, AXES, first_moves())  10.5 us
    pallas_call x3, Pallas kernels, some_heads(): pl.pallas_call(functools.partial(heads_kernel, tuple((shift for shift, _...  6.76 us
    ppermute x2, starting transfers between devices, swap_cores(): lax.ppermute(value, AXES, [(flat(y, x, z, 1 - c), flat(y, x, z, c)) for y...  5.94 us
    ppermute x2, starting transfers between devices, body(): lax.ppermute(kv, AXES, moves(lambda c, d=d: (0, 0, d)))  5.28 us
    ppermute x1, starting transfers between devices, body(): above = lax.ppermute(down, AXES, moves(lambda c: (0, 0, 1)))  5.02 us
    ppermute x1, waiting for transfers between devices, body(): below = lax.ppermute(up, AXES, moves(lambda c: (0, 0, -1)))  5.01 us
    ppermute x1, starting transfers between devices, body(): right = lax.ppermute(weight, AXES, moves(lambda c: (0, 1, 0)))  3.85 us
  transfers between devices with their start and end apart: 12, of which 8 were waited for; matrix products, arithmetic and copies ran while one was open for 0% of the time, Pallas kernels for 10%

profile of v5, /device:TPU:17, one launch (start us, length us, event | category | flops | bytes accessed | tf_op | source)
XLA Modules:
  0.0 76.1 jit_solution(12558901303344662349)
XLA Ops:
  0.0 2.6 %collective-permute-start = (bf16[128,2048]{1,0:T(8,128)(2,1)}, bf16[128,2048]{1,0:T(8,128)(2,1)S(1)}, u32[]{:S(2)}, u32[]{:S(2)}) collective-permute-start(bf16[128,2048]{1,0:T(8,128)(2,1)} %own_hbm.1), channel_id=1, source_target_pairs={{1,0},{0,1},{3,2},{2,3},{5,4},{4,5},{7,6},{6,7},{9,8},{8,9},{11,10... | collective-permute-start | bytes 1572872 | tf_op jit(solution)/shard_map/ppermute | solution.py:51
  2.6 10.5 %collective-permute-start.1 = (bf16[2048,128]{1,0:T(8,128)(2,1)}, bf16[2048,128]{1,0:T(8,128)(2,1)S(1)}, u32[]{:S(2)}, u32[]{:S(2)}) collective-permute-start(bf16[2048,128]{1,0:T(8,128)(2,1)} %param.6), channel_id=1, source_target_pairs={{5,0},{15,1},{3,2},{11,3},{1,4},{8,5},{7,6},{14,7},{4,8},{10,9},{2... | collective-permute-start | bytes 1572872 | tf_op jit(solution)/shard_map/ppermute | solution.py:271
  13.1 0.0 copy-start
  13.1 0.6 copy-done
  13.8 1.8 %shard_map.55 = (bf16[128,2048]{1,0:T(8,128)(2,1)S(1)}, bf16[2048,128]{1,0:T(8,128)(2,1)S(1)}, bf16[2048,128]{1,0:T(8,128)(2,1)S(1)}, bf16[512,128]{1,0:T(8,128)...) custom-call(s32[16]{0:T(128)S(1)} %copy-done, bf16[128,2048]{1,0:T(8,128)(2,1)} %own_hbm.1, ...), custom_call_target="tpu_custom_call" | custom-call | flops 134217728 | bytes 2097152 | tf_op jit(solution)/shard_map/pallas_call | solution.py:103
  15.6 0.0 collective-permute-done.other_ref
  15.6 0.4 shard_map.56.refs_4_.refs_2_
  16.1 2.1 %collective-permute-start.2 = (bf16[512,128]{1,0:T(8,128)(2,1)S(1)}, bf16[512,128]{1,0:T(8,128)(2,1)S(1)}, u32[]{:S(2)}, u32[]{:S(2)}) collective-permute-start(bf16[512,128]{1,0:T(8,128)(2,1)S(1)} %shard_map.56.refs_4_.refs_2_), channel_id=1, source_target_pairs={{2,0},{3,1},{4,2},{5,3},{6,4},{7,5},{8,6},{9,7},{10,8},{11,9},{12,... | collective-permute-start | bytes 393224 | tf_op jit(solution)/shard_map/ppermute | solution.py:275
  18.1 3.2 %collective-permute-start.3 = (bf16[512,128]{1,0:T(8,128)(2,1)S(1)}, bf16[512,128]{1,0:T(8,128)(2,1)S(1)}, u32[]{:S(2)}, u32[]{:S(2)}) collective-permute-start(bf16[512,128]{1,0:T(8,128)(2,1)S(1)} %shard_map.56.refs_4_.refs_2_), channel_id=1, source_target_pairs={{14,0},{15,1},{0,2},{1,3},{2,4},{3,5},{4,6},{5,7},{6,8},{7,9},{8,1... | collective-permute-start | bytes 393224 | tf_op jit(solution)/shard_map/ppermute | solution.py:275
  21.3 0.8 %collective-permute-done.1.refs_0_ = bf16[2048,128]{1,0:T(8,128)(2,1)S(1)} collective-permute-done((bf16[2048,128]{1,0:T(8,128)(2,1)}, bf16[2048,128]{1,0:T(8,128)(2,1)S(1)}, u32[]{:S(2)}, u32[]{:S(2)}) %collective-permute-start.1) | collective-permute-done | bytes 524320 | tf_op jit(solution)/shard_map/ppermute | solution.py:271
  22.1 1.5 %collective-permute-done.2.refs_1_.above_ref.refs_5_.refs_3_ = bf16[512,128]{1,0:T(8,128)(2,1)S(1)} collective-permute-done((bf16[512,128]{1,0:T(8,128)(2,1)S(1)}, bf16[512,128]{1,0:T(8,128)(2,1)S(1)}, u32[]{:S(2)}, u32[]{:S(2)}) %collective-permute-start.2) | collective-permute-done | bytes 131104 | tf_op jit(solution)/shard_map/ppermute | solution.py:275
  23.7 10.4 %collective-permute-done.3.refs_2_.below_ref.refs_6_.refs_4_ = bf16[512,128]{1,0:T(8,128)(2,1)S(1)} collective-permute-done((bf16[512,128]{1,0:T(8,128)(2,1)S(1)}, bf16[512,128]{1,0:T(8,128)(2,1)S(1)}, u32[]{:S(2)}, u32[]{:S(2)}) %collective-permute-start.3) | collective-permute-done | bytes 131104 | tf_op jit(solution)/shard_map/ppermute | solution.py:275
  34.1 3.8 %collective-permute-start.5 = (bf16[2048,128]{1,0:T(8,128)(2,1)S(1)}, bf16[2048,128]{1,0:T(8,128)(2,1)S(1)}, u32[]{:S(2)}, u32[]{:S(2)}) collective-permute-start(bf16[2048,128]{1,0:T(8,128)(2,1)S(1)} %shard_map.57.weight_ref.refs_0_), channel_id=1, source_target_pairs={{16,0},{17,1},{18,2},{19,3},{20,4},{21,5},{22,6},{23,7},{24,8},{25... | collective-permute-start | bytes 1572872 | tf_op jit(solution)/shard_map/ppermute | solution.py:278
  37.9 1.9 %collective-permute-start.6 = (bf16[2048,128]{1,0:T(8,128)(2,1)S(1)}, bf16[2048,128]{1,0:T(8,128)(2,1)S(1)}, u32[]{:S(2)}, u32[]{:S(2)}) collective-permute-start(bf16[2048,128]{1,0:T(8,128)(2,1)S(1)} %shard_map.57.weight_ref.refs_0_), channel_id=1, source_target_pairs={{48,0},{49,1},{50,2},{51,3},{52,4},{53,5},{54,6},{55,7},{56,8},{57... | collective-permute-start | bytes 1572872 | tf_op jit(solution)/shard_map/ppermute | solution.py:279
  39.9 0.1 shard_map.59
  40.0 5.0 %collective-permute-start.8 = (bf16[2560,128]{1,0:T(8,128)(2,1)S(1)}, bf16[2560,128]{1,0:T(8,128)(2,1)S(1)}, u32[]{:S(2)}, u32[]{:S(2)}) collective-permute-start(bf16[2560,128]{1,0:T(8,128)(2,1)S(1)} %get-tuple-element.23), channel_id=1, source_target_pairs={{2,0},{3,1},{4,2},{5,3},{6,4},{7,5},{8,6},{9,7},{10,8},{11,9},{12,... | collective-permute-start | bytes 1966088 | tf_op jit(solution)/shard_map/ppermute | solution.py:281
  45.0 1.9 %collective-permute-start.9 = (bf16[2560,128]{1,0:T(8,128)(2,1)S(1)}, bf16[2560,128]{1,0:T(8,128)(2,1)S(1)}, u32[]{:S(2)}, u32[]{:S(2)}) collective-permute-start(bf16[2560,128]{1,0:T(8,128)(2,1)S(1)} %get-tuple-element.24), channel_id=1, source_target_pairs={{14,0},{15,1},{0,2},{1,3},{2,4},{3,5},{4,6},{5,7},{6,8},{7,9},{8,1... | collective-permute-start | bytes 1966088 | tf_op jit(solution)/shard_map/ppermute | solution.py:282
  46.9 1.9 %collective-permute-start.10 = (bf16[2048,128]{1,0:T(8,128)(2,1)S(1)}, bf16[2048,128]{1,0:T(8,128)(2,1)S(1)}, u32[]{:S(2)}, u32[]{:S(2)}) collective-permute-start(bf16[2048,128]{1,0:T(8,128)(2,1)S(1)} %shard_map.57.weight_ref.refs_0_), channel_id=1, source_target_pairs={{64,0},{65,1},{66,2},{67,3},{68,4},{69,5},{70,6},{71,7},{72,8},{73... | collective-permute-start | bytes 1572872 | tf_op jit(solution)/shard_map/ppermute | solution.py:283
  48.8 0.8 %collective-permute-done.5.first_ref.refs_1_ = bf16[2048,128]{1,0:T(8,128)(2,1)S(1)} collective-permute-done((bf16[2048,128]{1,0:T(8,128)(2,1)S(1)}, bf16[2048,128]{1,0:T(8,128)(2,1)S(1)}, u32[]{:S(2)}, u32[]{:S(2)}) %collective-permute-start.5) | collective-permute-done | bytes 524320 | tf_op jit(solution)/shard_map/ppermute | solution.py:278
  49.6 2.6 %collective-permute-start.4 = (bf16[2048,128]{1,0:T(8,128)(2,1)S(1)}, bf16[2048,128]{1,0:T(8,128)(2,1)S(1)}, u32[]{:S(2)}, u32[]{:S(2)}) collective-permute-start(bf16[2048,128]{1,0:T(8,128)(2,1)S(1)} %shard_map.57.weight_ref.refs_0_), channel_id=1, source_target_pairs={{448,0},{449,1},{450,2},{451,3},{452,4},{453,5},{454,6},{455,7},{4... | collective-permute-start | bytes 1572872 | tf_op jit(solution)/shard_map/ppermute | solution.py:284
  52.2 1.1 %collective-permute-done.6.second_ref.refs_2_ = bf16[2048,128]{1,0:T(8,128)(2,1)S(1)} collective-permute-done((bf16[2048,128]{1,0:T(8,128)(2,1)S(1)}, bf16[2048,128]{1,0:T(8,128)(2,1)S(1)}, u32[]{:S(2)}, u32[]{:S(2)}) %collective-permute-start.6) | collective-permute-done | bytes 524320 | tf_op jit(solution)/shard_map/ppermute | solution.py:279
  53.3 2.2 %collective-permute-start.7 = (bf16[2048,128]{1,0:T(8,128)(2,1)S(1)}, bf16[2048,128]{1,0:T(8,128)(2,1)S(1)}, u32[]{:S(2)}, u32[]{:S(2)}) collective-permute-start(bf16[2048,128]{1,0:T(8,128)(2,1)S(1)} %shard_map.58), channel_id=1, source_target_pairs={{16,0},{49,1},{18,2},{51,3},{20,4},{53,5},{22,6},{55,7},{24,8},{57... | collective-permute-start | bytes 1572872 | tf_op jit(solution)/shard_map/ppermute | solution.py:285
  55.6 3.2 %collective-permute-done.8.refs_3_.refs_7_.refs_5_ = bf16[2560,128]{1,0:T(8,128)(2,1)S(1)} collective-permute-done((bf16[2560,128]{1,0:T(8,128)(2,1)S(1)}, bf16[2560,128]{1,0:T(8,128)(2,1)S(1)}, u32[]{:S(2)}, u32[]{:S(2)}) %collective-permute-start.8) | collective-permute-done | bytes 655392 | tf_op jit(solution)/shard_map/ppermute | solution.py:281
  58.8 5.0 %collective-permute-done.9.refs_8_.refs_0_.refs_6_ = bf16[2560,128]{1,0:T(8,128)(2,1)S(1)} collective-permute-done((bf16[2560,128]{1,0:T(8,128)(2,1)S(1)}, bf16[2560,128]{1,0:T(8,128)(2,1)S(1)}, u32[]{:S(2)}, u32[]{:S(2)}) %collective-permute-start.9) | collective-permute-done | bytes 655392 | tf_op jit(solution)/shard_map/ppermute | solution.py:282
  63.9 3.3 %shard_map.60 = (bf16[128,1024]{1,0:T(8,128)(2,1)S(1)}, bf16[128,1024]{1,0:T(8,128)(2,1)S(1)}) custom-call(bf16[128,2048]{1,0:T(8,128)(2,1)S(1)} %get-tuple-element.19.own_ref, bf16[128,2048]{1,0:T(8,128)(2,1)S(1)} %collective-permute-done.other_ref, ...), custom_call_target="tpu_custom_call", output_to_operand_aliasing={{0}: (13, {}), {1}: (14, {})} | custom-call | flops 268435456 | bytes 2097152 | tf_op jit(solution)/shard_map/pallas_call | solution.py:242
  67.2 0.0 collective-permute-done.10.refs_1_
  67.2 1.7 %shard_map.61 = (bf16[128,1024]{1,0:T(8,128)(2,1)S(1)}, bf16[128,1024]{1,0:T(8,128)(2,1)S(1)}) custom-call(bf16[128,2048]{1,0:T(8,128)(2,1)S(1)} %get-tuple-element.19.own_ref, bf16[128,2048]{1,0:T(8,128)(2,1)S(1)} %collective-permute-done.other_ref, ...), custom_call_target="tpu_custom_call", output_to_operand_aliasing={{0}: (11, {}), {1}: (12, {})} | custom-call | flops 268435456 | bytes 2097152 | tf_op jit(solution)/shard_map/pallas_call | solution.py:242
  69.0 0.0 collective-permute-done.4.refs_0_
  69.0 0.0 collective-permute-done.7.refs_1_
  69.0 1.7 %shard_map.62 = (bf16[128,1024]{1,0:T(8,128)(2,1)S(1)}, bf16[128,1024]{1,0:T(8,128)(2,1)S(1)}) custom-call(bf16[128,2048]{1,0:T(8,128)(2,1)S(1)} %get-tuple-element.19.own_ref, bf16[128,2048]{1,0:T(8,128)(2,1)S(1)} %collective-permute-done.other_ref, ...), custom_call_target="tpu_custom_call", output_to_operand_aliasing={{0}: (11, {}), {1}: (12, {})} | custom-call | flops 268435456 | bytes 2097152 | tf_op jit(solution)/shard_map/pallas_call | solution.py:242
  70.7 3.4 %collective-permute-start.11 = (bf16[128,1024]{1,0:T(8,128)(2,1)S(1)}, bf16[128,1024]{1,0:T(8,128)(2,1)S(1)}, u32[]{:S(2)}, u32[]{:S(2)}) collective-permute-start(bf16[128,1024]{1,0:T(8,128)(2,1)S(1)} %get-tuple-element.32), channel_id=1, source_target_pairs={{1,0},{0,1},{3,2},{2,3},{5,4},{4,5},{7,6},{6,7},{9,8},{8,9},{11,10... | collective-permute-start | bytes 786440 | tf_op jit(solution)/shard_map/ppermute | solution.py:51
  74.1 1.1 %collective-permute-done.11.other_ref = bf16[128,1024]{1,0:T(8,128)(2,1)S(1)} collective-permute-done((bf16[128,1024]{1,0:T(8,128)(2,1)S(1)}, bf16[128,1024]{1,0:T(8,128)(2,1)S(1)}, u32[]{:S(2)}, u32[]{:S(2)}) %collective-permute-start.11) | collective-permute-done | bytes 262176 | tf_op jit(solution)/shard_map/ppermute | solution.py:51
  75.2 0.8 %shard_map.63 = bf16[128,2048]{1,0:T(8,128)(2,1)} custom-call(bf16[128,1024]{1,0:T(8,128)(2,1)S(1)} %get-tuple-element.31.mine_ref, bf16[128,1024]{1,0:T(8,128)(2,1)S(1)} %collective-permute-done.11.other_ref), custom_call_target="tpu_custom_call" | custom-call | tf_op jit(solution)/shard_map/pallas_call | solution.py:260
  (4 shorter events, 0.1 us)
Async XLA Ops:
  0.0 15.6 %collective-permute-start = (bf16[128,2048]{1,0:T(8,128)(2,1)}, bf16[128,2048]{1,0:T(8,128)(2,1)S(1)}, u32[]{:S(2)}, u32[]{:S(2)}) collective-permute-start(bf16[128,2048]{1,0:T(8,128)(2,1)} %own_hbm.1), channel_id=1, source_target_pairs={{1,0},{0,1},{3,2},{2,3},{5,4},{4,5},{7,6},{6,7},{9,8},{8,9},{11,10... | collective-permute-start | bytes 1572872 | tf_op jit(solution)/shard_map/ppermute | solution.py:51
  2.6 19.5 %collective-permute-start.1 = (bf16[2048,128]{1,0:T(8,128)(2,1)}, bf16[2048,128]{1,0:T(8,128)(2,1)S(1)}, u32[]{:S(2)}, u32[]{:S(2)}) collective-permute-start(bf16[2048,128]{1,0:T(8,128)(2,1)} %param.6), channel_id=1, source_target_pairs={{5,0},{15,1},{3,2},{11,3},{1,4},{8,5},{7,6},{14,7},{4,8},{10,9},{2... | collective-permute-start | bytes 1572872 | tf_op jit(solution)/shard_map/ppermute | solution.py:271
  13.1 0.7 copy-start
  16.1 7.6 %collective-permute-start.2 = (bf16[512,128]{1,0:T(8,128)(2,1)S(1)}, bf16[512,128]{1,0:T(8,128)(2,1)S(1)}, u32[]{:S(2)}, u32[]{:S(2)}) collective-permute-start(bf16[512,128]{1,0:T(8,128)(2,1)S(1)} %shard_map.56.refs_4_.refs_2_), channel_id=1, source_target_pairs={{2,0},{3,1},{4,2},{5,3},{6,4},{7,5},{8,6},{9,7},{10,8},{11,9},{12,... | collective-permute-start | bytes 393224 | tf_op jit(solution)/shard_map/ppermute | solution.py:275
  18.1 16.0 %collective-permute-start.3 = (bf16[512,128]{1,0:T(8,128)(2,1)S(1)}, bf16[512,128]{1,0:T(8,128)(2,1)S(1)}, u32[]{:S(2)}, u32[]{:S(2)}) collective-permute-start(bf16[512,128]{1,0:T(8,128)(2,1)S(1)} %shard_map.56.refs_4_.refs_2_), channel_id=1, source_target_pairs={{14,0},{15,1},{0,2},{1,3},{2,4},{3,5},{4,6},{5,7},{6,8},{7,9},{8,1... | collective-permute-start | bytes 393224 | tf_op jit(solution)/shard_map/ppermute | solution.py:275
  34.1 15.5 %collective-permute-start.5 = (bf16[2048,128]{1,0:T(8,128)(2,1)S(1)}, bf16[2048,128]{1,0:T(8,128)(2,1)S(1)}, u32[]{:S(2)}, u32[]{:S(2)}) collective-permute-start(bf16[2048,128]{1,0:T(8,128)(2,1)S(1)} %shard_map.57.weight_ref.refs_0_), channel_id=1, source_target_pairs={{16,0},{17,1},{18,2},{19,3},{20,4},{21,5},{22,6},{23,7},{24,8},{25... | collective-permute-start | bytes 1572872 | tf_op jit(solution)/shard_map/ppermute | solution.py:278
  37.9 15.4 %collective-permute-start.6 = (bf16[2048,128]{1,0:T(8,128)(2,1)S(1)}, bf16[2048,128]{1,0:T(8,128)(2,1)S(1)}, u32[]{:S(2)}, u32[]{:S(2)}) collective-permute-start(bf16[2048,128]{1,0:T(8,128)(2,1)S(1)} %shard_map.57.weight_ref.refs_0_), channel_id=1, source_target_pairs={{48,0},{49,1},{50,2},{51,3},{52,4},{53,5},{54,6},{55,7},{56,8},{57... | collective-permute-start | bytes 1572872 | tf_op jit(solution)/shard_map/ppermute | solution.py:279
  40.0 18.9 %collective-permute-start.8 = (bf16[2560,128]{1,0:T(8,128)(2,1)S(1)}, bf16[2560,128]{1,0:T(8,128)(2,1)S(1)}, u32[]{:S(2)}, u32[]{:S(2)}) collective-permute-start(bf16[2560,128]{1,0:T(8,128)(2,1)S(1)} %get-tuple-element.23), channel_id=1, source_target_pairs={{2,0},{3,1},{4,2},{5,3},{6,4},{7,5},{8,6},{9,7},{10,8},{11,9},{12,... | collective-permute-start | bytes 1966088 | tf_op jit(solution)/shard_map/ppermute | solution.py:281
  45.0 18.8 %collective-permute-start.9 = (bf16[2560,128]{1,0:T(8,128)(2,1)S(1)}, bf16[2560,128]{1,0:T(8,128)(2,1)S(1)}, u32[]{:S(2)}, u32[]{:S(2)}) collective-permute-start(bf16[2560,128]{1,0:T(8,128)(2,1)S(1)} %get-tuple-element.24), channel_id=1, source_target_pairs={{14,0},{15,1},{0,2},{1,3},{2,4},{3,5},{4,6},{5,7},{6,8},{7,9},{8,1... | collective-permute-start | bytes 1966088 | tf_op jit(solution)/shard_map/ppermute | solution.py:282
  46.9 20.3 %collective-permute-start.10 = (bf16[2048,128]{1,0:T(8,128)(2,1)S(1)}, bf16[2048,128]{1,0:T(8,128)(2,1)S(1)}, u32[]{:S(2)}, u32[]{:S(2)}) collective-permute-start(bf16[2048,128]{1,0:T(8,128)(2,1)S(1)} %shard_map.57.weight_ref.refs_0_), channel_id=1, source_target_pairs={{64,0},{65,1},{66,2},{67,3},{68,4},{69,5},{70,6},{71,7},{72,8},{73... | collective-permute-start | bytes 1572872 | tf_op jit(solution)/shard_map/ppermute | solution.py:283
  49.6 19.3 %collective-permute-start.4 = (bf16[2048,128]{1,0:T(8,128)(2,1)S(1)}, bf16[2048,128]{1,0:T(8,128)(2,1)S(1)}, u32[]{:S(2)}, u32[]{:S(2)}) collective-permute-start(bf16[2048,128]{1,0:T(8,128)(2,1)S(1)} %shard_map.57.weight_ref.refs_0_), channel_id=1, source_target_pairs={{448,0},{449,1},{450,2},{451,3},{452,4},{453,5},{454,6},{455,7},{4... | collective-permute-start | bytes 1572872 | tf_op jit(solution)/shard_map/ppermute | solution.py:284
  53.3 15.6 %collective-permute-start.7 = (bf16[2048,128]{1,0:T(8,128)(2,1)S(1)}, bf16[2048,128]{1,0:T(8,128)(2,1)S(1)}, u32[]{:S(2)}, u32[]{:S(2)}) collective-permute-start(bf16[2048,128]{1,0:T(8,128)(2,1)S(1)} %shard_map.58), channel_id=1, source_target_pairs={{16,0},{49,1},{18,2},{51,3},{20,4},{53,5},{22,6},{55,7},{24,8},{57... | collective-permute-start | bytes 1572872 | tf_op jit(solution)/shard_map/ppermute | solution.py:285
  70.7 4.5 %collective-permute-start.11 = (bf16[128,1024]{1,0:T(8,128)(2,1)S(1)}, bf16[128,1024]{1,0:T(8,128)(2,1)S(1)}, u32[]{:S(2)}, u32[]{:S(2)}) collective-permute-start(bf16[128,1024]{1,0:T(8,128)(2,1)S(1)} %get-tuple-element.32), channel_id=1, source_target_pairs={{1,0},{0,1},{3,2},{2,3},{5,4},{4,5},{7,6},{6,7},{9,8},{8,9},{11,10... | collective-permute-start | bytes 786440 | tf_op jit(solution)/shard_map/ppermute | solution.py:51

commit v6 on v5

--- a/solution.py
+++ b/solution.py
@@ -17,7 +17,7 @@
 
 YS, XS, ZS, CORES = 8, 4, 8, 2
 AXES = ("dp", "ctx")
-ORDER = ((5, 3, 1, 7, 4, 2, 0, 6), (7, 3, 0, 6, 2, 4, 1, 5))
+KV_ROWS = 2 * PAIR
 AROUND = (0, 1, -1, 2, -2)
 VMEM = pl.BlockSpec(memory_space=pltpu.VMEM)
 HBM = pl.BlockSpec(memory_space=pltpu.HBM)
@@ -31,11 +31,14 @@
     return [(y, x, z, c) for y in range(YS) for x in range(XS) for z in range(ZS) for c in range(CORES)]
 
 
+def color_of(y, x, z):
+    return (2 * x + y + 3 * z) % 8
+
+
 def first_moves():
     pairs = []
     for y, x, z, c in everyone():
-        head = 8 * c + ORDER[c][(2 * x + 3 * y + z) % 8]
-        pairs.append((flat(y, x, head // 2, head % 2), flat(y, x, z, c)))
+        pairs.append((flat(y, x, color_of(y, x, z), c), flat(y, x, z, c)))
     return pairs
 
 
@@ -58,20 +61,20 @@
 
 def kv_rows(rows, key_ref, value_ref, kv_ref, first):
     for base, matrix in ((0, key_ref), (PAIR, value_ref)):
-        kv_ref[base + first : base + first + ROWS] = jnp.dot(
-            rows[...], matrix[...], preferred_element_type=jnp.float32
-        ).astype(jnp.bfloat16)
+        product = jnp.dot(rows[...], matrix[...], preferred_element_type=jnp.float32).astype(jnp.bfloat16)
+        for j in range(2):
+            start = j * KV_ROWS + base + first
+            kv_ref[start : start + ROWS] = product[:, j * HEAD_SIZE : (j + 1) * HEAD_SIZE]
 
 
 def own_kv_kernel(
     lengths_hbm, own_hbm, key_hbm, value_hbm, own_ref, key_ref, value_ref, kv_ref, row_docs_ref, key_docs_ref, lengths, sems
 ):
     y, x, z, c = place()
-    mine = pl.ds(pl.multiple_of(c * HEAD_SIZE, HEAD_SIZE), HEAD_SIZE)
     copies = [
         pltpu.make_async_copy(own_hbm, own_ref, sems.at[0]),
-        pltpu.make_async_copy(key_hbm.at[:, mine], key_ref, sems.at[1]),
-        pltpu.make_async_copy(value_hbm.at[:, mine], value_ref, sems.at[2]),
+        pltpu.make_async_copy(key_hbm, key_ref, sems.at[1]),
+        pltpu.make_async_copy(value_hbm, value_ref, sems.at[2]),
         pltpu.make_async_copy(lengths_hbm, lengths, sems.at[3]),
     ]
     for copy in copies:
@@ -106,14 +109,14 @@
         out_specs=[VMEM] * 6,
         out_shape=[
             jax.ShapeDtypeStruct((ROWS, WIDTH), kind),
-            jax.ShapeDtypeStruct((WIDTH, HEAD_SIZE), kind),
-            jax.ShapeDtypeStruct((WIDTH, HEAD_SIZE), kind),
-            jax.ShapeDtypeStruct((2 * PAIR, HEAD_SIZE), kind),
+            jax.ShapeDtypeStruct((WIDTH, 2 * HEAD_SIZE), kind),
+            jax.ShapeDtypeStruct((WIDTH, 2 * HEAD_SIZE), kind),
+            jax.ShapeDtypeStruct((2 * KV_ROWS, HEAD_SIZE), kind),
             jax.ShapeDtypeStruct((PAIR, 1), jnp.int32),
             jax.ShapeDtypeStruct((1, len(AROUND) * PAIR), jnp.int32),
         ],
         scratch_shapes=[pltpu.SMEM((16,), jnp.int32), pltpu.SemaphoreType.DMA((4,))],
-        compiler_params=pltpu.CompilerParams(vmem_limit_bytes=52 * 2**20),
+        compiler_params=pltpu.CompilerParams(vmem_limit_bytes=50 * 2**20),
         cost_estimate=pl.CostEstimate(flops=2**27, bytes_accessed=2**21, transcendentals=0),
     )(lengths, own, key_matrix, value_matrix)
 
@@ -189,12 +192,16 @@
     )(first, second)
 
 
-def attend(queries, kv, bases, docs, key_docs):
+def attend(queries, kv, bases, half, docs, key_docs):
+    def rows(i, more):
+        start = pl.multiple_of(bases[i] + more + half * KV_ROWS, PAIR)
+        return kv[i][pl.ds(start, PAIR)]
+
     factor = math.log2(math.e) / math.sqrt(HEAD_SIZE)
     scores = []
     for i in range(5):
         product = lax.dot_general(
-            queries, kv[i][bases[i] : bases[i] + PAIR], (((1,), (1,)), ((), ())), preferred_element_type=jnp.float32
+            queries, rows(i, 0), (((1,), (1,)), ((), ())), preferred_element_type=jnp.float32
         )
         allowed = docs == key_docs[:, i * PAIR : (i + 1) * PAIR]
         scores.append(jnp.where(allowed, product, NEG))
@@ -204,7 +211,7 @@
         part = jnp.exp2((scores[i] - highest) * factor)
         summed = summed + jnp.sum(part, axis=1, keepdims=True)
         mixed = mixed + jnp.dot(
-            part.astype(jnp.bfloat16), kv[i][bases[i] + PAIR : bases[i] + 2 * PAIR], preferred_element_type=jnp.float32
+            part.astype(jnp.bfloat16), rows(i, PAIR), preferred_element_type=jnp.float32
         )
     return (mixed / summed).astype(jnp.bfloat16)
 
@@ -225,19 +232,16 @@
             axis=0,
         )
         for i, shift in enumerate(shifts[first : first + 2]):
-            color = (2 * x + 3 * y + z + shift) % 8
-            slot = 0
-            for k in range(8):
-                slot = slot + jnp.where(color == k, jnp.where(c == 0, ORDER[0][k], ORDER[1][k]), 0)
-            result = attend(queries[:, i * HEAD_SIZE : (i + 1) * HEAD_SIZE], kv, bases, docs, key_docs)
-            columns = pl.ds(pl.multiple_of(slot * HEAD_SIZE, HEAD_SIZE), HEAD_SIZE)
+            color = (color_of(y, x, z) + shift + 8) % 8
+            result = attend(queries[:, i * HEAD_SIZE : (i + 1) * HEAD_SIZE], kv, bases, color // 4, docs, key_docs)
+            columns = pl.ds(pl.multiple_of(color * HEAD_SIZE, HEAD_SIZE), HEAD_SIZE)
             keep_ref[:, columns] = result[:ROWS]
             send_ref[:, columns] = result[ROWS:]
 
 
 def some_heads(arrivals, own, other, kv, row_docs, key_docs, keep, send):
     inputs = [own, other, *(w for _, w in arrivals), *kv, row_docs, key_docs, keep, send]
-    bases = [array.shape[0] - 2 * PAIR for array in kv]
+    bases = [array.shape[0] - 2 * KV_ROWS for array in kv]
     shape = jax.ShapeDtypeStruct(keep.shape, keep.dtype)
     return pl.pallas_call(
         functools.partial(heads_kernel, tuple(shift for shift, _ in arrivals), bases),
@@ -252,8 +256,11 @@
 
 def join_kernel(mine_ref, other_ref, out_ref):
     y, x, z, c = place()
-    out_ref[:, pl.ds(pl.multiple_of(c * HALF, HALF), HALF)] = mine_ref[...]
-    out_ref[:, pl.ds(pl.multiple_of((1 - c) * HALF, HALF), HALF)] = other_ref[...]
+    for k in range(8):
+        columns = slice(k * HEAD_SIZE, (k + 1) * HEAD_SIZE)
+        for core, ref in ((c, mine_ref), (1 - c, other_ref)):
+            start = pl.multiple_of((2 * k + core) * HEAD_SIZE, HEAD_SIZE)
+            out_ref[:, pl.ds(start, HEAD_SIZE)] = ref[:, columns]
 
 
 def join(keep, arrived):
@@ -283,7 +290,7 @@
     front = lax.ppermute(weight, AXES, moves(lambda c: (1, 0, 0)))
     back = lax.ppermute(weight, AXES, moves(lambda c: (-1, 0, 0)))
     across = lax.ppermute(choose(right, left), AXES, moves(lambda c: (0, 1, 0) if c == 0 else (0, -1, 0)))
-    arrivals = [(0, weight), (2, right), (-2, left), (1, above), (-1, below), (3, front), (-3, back), (4, across)]
+    arrivals = [(0, weight), (2, right), (-2, left), (3, above), (-3, below), (1, front), (-1, back), (4, across)]
     kv_all = [kv, *near, above, below]
 
     keep = jnp.zeros((ROWS, HALF), jnp.bfloat16)

time: 76.5 us -> 88.9 us (1.16)
  the two profiles are of different devices: /device:TPU:17 before, /device:TPU:1 now
where the time goes in v6:
time: 88.9 us; the launch traced here: 88.3 us
  starting transfers between devices  47.5 us (53%)
  waiting for transfers between devices  28.6 us (32%)
  Pallas kernels  10.4 us (12%)
  local copies, waits for them, and re-layouts  1.74 us (2%)
    ppermute x2, waiting for transfers between devices, body(): lax.ppermute(kv, AXES, moves(lambda c, d=d: (0, 0, d)))  15.8 us
    ppermute x2, starting transfers between devices, swap_cores(): lax.ppermute(value, AXES, [(flat(y, x, z, 1 - c), flat(y, x, z, c)) for y...  13 us
    ppermute x1, starting transfers between devices, body(): right = lax.ppermute(weight, AXES, moves(lambda c: (0, 1, 0)))  8.74 us
    ppermute x2, starting transfers between devices, body(): lax.ppermute(kv, AXES, moves(lambda c, d=d: (0, 0, d)))  7.69 us
    pallas_call x3, Pallas kernels, some_heads(): pl.pallas_call(functools.partial(heads_kernel, tuple((shift for shift, _...  6.78 us
    ppermute x1, waiting for transfers between devices, body(): above = lax.ppermute(down, AXES, moves(lambda c: (0, 0, 1)))  5.69 us
    ppermute x1, starting transfers between devices, body(): above = lax.ppermute(down, AXES, moves(lambda c: (0, 0, 1)))  5.32 us
    ppermute x1, waiting for transfers between devices, body(): below = lax.ppermute(up, AXES, moves(lambda c: (0, 0, -1)))  5.05 us
  transfers between devices with their start and end apart: 12, of which 6 were waited for; matrix products, arithmetic and copies ran while one was open for 0% of the time, Pallas kernels for 9%

profile of v6, /device:TPU:1, one launch (start us, length us, event | category | flops | bytes accessed | tf_op | source)
XLA Modules:
  0.0 88.3 jit_solution(4220621075211791245)
XLA Ops:
  0.0 8.8 %collective-permute-start = (bf16[128,2048]{1,0:T(8,128)(2,1)}, bf16[128,2048]{1,0:T(8,128)(2,1)S(1)}, u32[]{:S(2)}, u32[]{:S(2)}) collective-permute-start(bf16[128,2048]{1,0:T(8,128)(2,1)} %own_hbm.1), channel_id=1, source_target_pairs={{1,0},{0,1},{3,2},{2,3},{5,4},{4,5},{7,6},{6,7},{9,8},{8,9},{11,10... | collective-permute-start | bytes 1572872 | tf_op jit(solution)/shard_map/ppermute | solution.py:54
  8.8 1.7 %collective-permute-start.1 = (bf16[2048,128]{1,0:T(8,128)(2,1)}, bf16[2048,128]{1,0:T(8,128)(2,1)S(1)}, u32[]{:S(2)}, u32[]{:S(2)}) collective-permute-start(bf16[2048,128]{1,0:T(8,128)(2,1)} %param.6), channel_id=1, source_target_pairs={{0,0},{1,1},{6,2},{7,3},{12,4},{13,5},{2,6},{3,7},{8,8},{9,9},{14,... | collective-permute-start | bytes 1572872 | tf_op jit(solution)/shard_map/ppermute | solution.py:278
  10.5 0.0 copy-start
  10.5 1.0 %copy-done = bf16[128,2048]{1,0:T(8,128)(2,1)S(1)} copy-done((bf16[128,2048]{1,0:T(8,128)(2,1)S(1)}, bf16[128,2048]{1,0:T(8,128)(2,1)}, u32[]{:S(2)}) %copy-start) | copy-done | bytes 524312
  11.5 0.0 copy-start.1
  11.5 0.7 copy-done.1
  12.2 2.1 %shard_map.55 = (bf16[128,2048]{1,0:T(8,128)(2,1)S(1)}, bf16[2048,256]{1,0:T(8,128)(2,1)S(1)}, bf16[2048,256]{1,0:T(8,128)(2,1)S(1)}, bf16[1024,128]{1,0:T(8,128...) custom-call(s32[16]{0:T(128)S(1)} %copy-done.1, bf16[128,2048]{1,0:T(8,128)(2,1)S(1)} %copy-done, ...), custom_call_target="tpu_custom_call" | custom-call | flops 134217728 | bytes 2097152 | tf_op jit(solution)/shard_map/pallas_call | solution.py:106
  14.2 0.0 collective-permute-done.other_ref
  14.3 0.5 shard_map.56.refs_4_.refs_2_
  14.7 5.8 %collective-permute-start.2 = (bf16[1024,128]{1,0:T(8,128)(2,1)S(1)}, bf16[1024,128]{1,0:T(8,128)(2,1)S(1)}, u32[]{:S(2)}, u32[]{:S(2)}) collective-permute-start(bf16[1024,128]{1,0:T(8,128)(2,1)S(1)} %shard_map.56.refs_4_.refs_2_), channel_id=1, source_target_pairs={{2,0},{3,1},{4,2},{5,3},{6,4},{7,5},{8,6},{9,7},{10,8},{11,9},{12,... | collective-permute-start | bytes 786440 | tf_op jit(solution)/shard_map/ppermute | solution.py:282
  20.5 1.9 %collective-permute-start.3 = (bf16[1024,128]{1,0:T(8,128)(2,1)S(1)}, bf16[1024,128]{1,0:T(8,128)(2,1)S(1)}, u32[]{:S(2)}, u32[]{:S(2)}) collective-permute-start(bf16[1024,128]{1,0:T(8,128)(2,1)S(1)} %shard_map.56.refs_4_.refs_2_), channel_id=1, source_target_pairs={{14,0},{15,1},{0,2},{1,3},{2,4},{3,5},{4,6},{5,7},{6,8},{7,9},{8,1... | collective-permute-start | bytes 786440 | tf_op jit(solution)/shard_map/ppermute | solution.py:282
  22.4 0.0 collective-permute-done.1.refs_0_
  22.4 3.4 %collective-permute-done.2.refs_1_.above_ref.refs_5_.refs_3_ = bf16[1024,128]{1,0:T(8,128)(2,1)S(1)} collective-permute-done((bf16[1024,128]{1,0:T(8,128)(2,1)S(1)}, bf16[1024,128]{1,0:T(8,128)(2,1)S(1)}, u32[]{:S(2)}, u32[]{:S(2)}) %collective-permute-start.2) | collective-permute-done | bytes 262176 | tf_op jit(solution)/shard_map/ppermute | solution.py:282
  25.9 12.4 %collective-permute-done.3.refs_2_.below_ref.refs_6_.refs_4_ = bf16[1024,128]{1,0:T(8,128)(2,1)S(1)} collective-permute-done((bf16[1024,128]{1,0:T(8,128)(2,1)S(1)}, bf16[1024,128]{1,0:T(8,128)(2,1)S(1)}, u32[]{:S(2)}, u32[]{:S(2)}) %collective-permute-start.3) | collective-permute-done | bytes 262176 | tf_op jit(solution)/shard_map/ppermute | solution.py:282
  38.3 8.7 %collective-permute-start.5 = (bf16[2048,128]{1,0:T(8,128)(2,1)S(1)}, bf16[2048,128]{1,0:T(8,128)(2,1)S(1)}, u32[]{:S(2)}, u32[]{:S(2)}) collective-permute-start(bf16[2048,128]{1,0:T(8,128)(2,1)S(1)} %shard_map.57.weight_ref.refs_0_), channel_id=1, source_target_pairs={{16,0},{17,1},{18,2},{19,3},{20,4},{21,5},{22,6},{23,7},{24,8},{25... | collective-permute-start | bytes 1572872 | tf_op jit(solution)/shard_map/ppermute | solution.py:285
  47.0 1.9 %collective-permute-start.6 = (bf16[2048,128]{1,0:T(8,128)(2,1)S(1)}, bf16[2048,128]{1,0:T(8,128)(2,1)S(1)}, u32[]{:S(2)}, u32[]{:S(2)}) collective-permute-start(bf16[2048,128]{1,0:T(8,128)(2,1)S(1)} %shard_map.57.weight_ref.refs_0_), channel_id=1, source_target_pairs={{48,0},{49,1},{50,2},{51,3},{52,4},{53,5},{54,6},{55,7},{56,8},{57... | collective-permute-start | bytes 1572872 | tf_op jit(solution)/shard_map/ppermute | solution.py:286
  49.0 0.1 shard_map.59
  49.1 5.3 %collective-permute-start.8 = (bf16[3072,128]{1,0:T(8,128)(2,1)S(1)}, bf16[3072,128]{1,0:T(8,128)(2,1)S(1)}, u32[]{:S(2)}, u32[]{:S(2)}) collective-permute-start(bf16[3072,128]{1,0:T(8,128)(2,1)S(1)} %get-tuple-element.23), channel_id=1, source_target_pairs={{2,0},{3,1},{4,2},{5,3},{6,4},{7,5},{8,6},{9,7},{10,8},{11,9},{12,... | collective-permute-start | bytes 2359304 | tf_op jit(solution)/shard_map/ppermute | solution.py:288
  54.4 1.9 %collective-permute-start.9 = (bf16[3072,128]{1,0:T(8,128)(2,1)S(1)}, bf16[3072,128]{1,0:T(8,128)(2,1)S(1)}, u32[]{:S(2)}, u32[]{:S(2)}) collective-permute-start(bf16[3072,128]{1,0:T(8,128)(2,1)S(1)} %get-tuple-element.24), channel_id=1, source_target_pairs={{14,0},{15,1},{0,2},{1,3},{2,4},{3,5},{4,6},{5,7},{6,8},{7,9},{8,1... | collective-permute-start | bytes 2359304 | tf_op jit(solution)/shard_map/ppermute | solution.py:289
  56.3 1.9 %collective-permute-start.10 = (bf16[2048,128]{1,0:T(8,128)(2,1)S(1)}, bf16[2048,128]{1,0:T(8,128)(2,1)S(1)}, u32[]{:S(2)}, u32[]{:S(2)}) collective-permute-start(bf16[2048,128]{1,0:T(8,128)(2,1)S(1)} %shard_map.57.weight_ref.refs_0_), channel_id=1, source_target_pairs={{64,0},{65,1},{66,2},{67,3},{68,4},{69,5},{70,6},{71,7},{72,8},{73... | collective-permute-start | bytes 1572872 | tf_op jit(solution)/shard_map/ppermute | solution.py:290
  58.2 0.0 collective-permute-done.5.first_ref.refs_1_
  58.3 3.4 %collective-permute-start.4 = (bf16[2048,128]{1,0:T(8,128)(2,1)S(1)}, bf16[2048,128]{1,0:T(8,128)(2,1)S(1)}, u32[]{:S(2)}, u32[]{:S(2)}) collective-permute-start(bf16[2048,128]{1,0:T(8,128)(2,1)S(1)} %shard_map.57.weight_ref.refs_0_), channel_id=1, source_target_pairs={{448,0},{449,1},{450,2},{451,3},{452,4},{453,5},{454,6},{455,7},{4... | collective-permute-start | bytes 1572872 | tf_op jit(solution)/shard_map/ppermute | solution.py:291
  61.6 0.8 collective-permute-done.6.second_ref.refs_2_
  62.5 1.9 %collective-permute-start.7 = (bf16[2048,128]{1,0:T(8,128)(2,1)S(1)}, bf16[2048,128]{1,0:T(8,128)(2,1)S(1)}, u32[]{:S(2)}, u32[]{:S(2)}) collective-permute-start(bf16[2048,128]{1,0:T(8,128)(2,1)S(1)} %shard_map.58), channel_id=1, source_target_pairs={{16,0},{49,1},{18,2},{51,3},{20,4},{53,5},{22,6},{55,7},{24,8},{57... | collective-permute-start | bytes 1572872 | tf_op jit(solution)/shard_map/ppermute | solution.py:292
  64.4 5.7 %collective-permute-done.8.refs_3_.refs_7_.refs_5_ = bf16[3072,128]{1,0:T(8,128)(2,1)S(1)} collective-permute-done((bf16[3072,128]{1,0:T(8,128)(2,1)S(1)}, bf16[3072,128]{1,0:T(8,128)(2,1)S(1)}, u32[]{:S(2)}, u32[]{:S(2)}) %collective-permute-start.8) | collective-permute-done | bytes 786464 | tf_op jit(solution)/shard_map/ppermute | solution.py:288
  70.1 5.0 %collective-permute-done.9.refs_8_.refs_0_.refs_6_ = bf16[3072,128]{1,0:T(8,128)(2,1)S(1)} collective-permute-done((bf16[3072,128]{1,0:T(8,128)(2,1)S(1)}, bf16[3072,128]{1,0:T(8,128)(2,1)S(1)}, u32[]{:S(2)}, u32[]{:S(2)}) %collective-permute-start.9) | collective-permute-done | bytes 786464 | tf_op jit(solution)/shard_map/ppermute | solution.py:289
  75.2 3.3 %shard_map.60 = (bf16[128,1024]{1,0:T(8,128)(2,1)S(1)}, bf16[128,1024]{1,0:T(8,128)(2,1)S(1)}) custom-call(bf16[128,2048]{1,0:T(8,128)(2,1)S(1)} %get-tuple-element.19.own_ref, bf16[128,2048]{1,0:T(8,128)(2,1)S(1)} %collective-permute-done.other_ref, ...), custom_call_target="tpu_custom_call", output_to_operand_aliasing={{0}: (13, {}), {1}: (14, {})} | custom-call | flops 268435456 | bytes 2097152 | tf_op jit(solution)/shard_map/pallas_call | solution.py:246
  78.6 0.0 collective-permute-done.10.refs_1_
  78.6 1.7 %shard_map.61 = (bf16[128,1024]{1,0:T(8,128)(2,1)S(1)}, bf16[128,1024]{1,0:T(8,128)(2,1)S(1)}) custom-call(bf16[128,2048]{1,0:T(8,128)(2,1)S(1)} %get-tuple-element.19.own_ref, bf16[128,2048]{1,0:T(8,128)(2,1)S(1)} %collective-permute-done.other_ref, ...), custom_call_target="tpu_custom_call", output_to_operand_aliasing={{0}: (11, {}), {1}: (12, {})} | custom-call | flops 268435456 | bytes 2097152 | tf_op jit(solution)/shard_map/pallas_call | solution.py:246
  80.3 0.0 collective-permute-done.4.refs_0_
  80.3 0.0 collective-permute-done.7.refs_1_
  80.3 1.7 %shard_map.62 = (bf16[128,1024]{1,0:T(8,128)(2,1)S(1)}, bf16[128,1024]{1,0:T(8,128)(2,1)S(1)}) custom-call(bf16[128,2048]{1,0:T(8,128)(2,1)S(1)} %get-tuple-element.19.own_ref, bf16[128,2048]{1,0:T(8,128)(2,1)S(1)} %collective-permute-done.other_ref, ...), custom_call_target="tpu_custom_call", output_to_operand_aliasing={{0}: (11, {}), {1}: (12, {})} | custom-call | flops 268435456 | bytes 2097152 | tf_op jit(solution)/shard_map/pallas_call | solution.py:246
  82.1 4.2 %collective-permute-start.11 = (bf16[128,1024]{1,0:T(8,128)(2,1)S(1)}, bf16[128,1024]{1,0:T(8,128)(2,1)S(1)}, u32[]{:S(2)}, u32[]{:S(2)}) collective-permute-start(bf16[128,1024]{1,0:T(8,128)(2,1)S(1)} %get-tuple-element.32), channel_id=1, source_target_pairs={{1,0},{0,1},{3,2},{2,3},{5,4},{4,5},{7,6},{6,7},{9,8},{8,9},{11,10... | collective-permute-start | bytes 786440 | tf_op jit(solution)/shard_map/ppermute | solution.py:54
  86.3 1.1 %collective-permute-done.11.other_ref = bf16[128,1024]{1,0:T(8,128)(2,1)S(1)} collective-permute-done((bf16[128,1024]{1,0:T(8,128)(2,1)S(1)}, bf16[128,1024]{1,0:T(8,128)(2,1)S(1)}, u32[]{:S(2)}, u32[]{:S(2)}) %collective-permute-start.11) | collective-permute-done | bytes 262176 | tf_op jit(solution)/shard_map/ppermute | solution.py:54
  87.4 0.9 %shard_map.63 = bf16[128,2048]{1,0:T(8,128)(2,1)} custom-call(bf16[128,1024]{1,0:T(8,128)(2,1)S(1)} %get-tuple-element.31.mine_ref, bf16[128,1024]{1,0:T(8,128)(2,1)S(1)} %collective-permute-done.11.other_ref), custom_call_target="tpu_custom_call" | custom-call | tf_op jit(solution)/shard_map/pallas_call | solution.py:267
  (4 shorter events, 0.1 us)
Async XLA Ops:
  0.0 14.2 %collective-permute-start = (bf16[128,2048]{1,0:T(8,128)(2,1)}, bf16[128,2048]{1,0:T(8,128)(2,1)S(1)}, u32[]{:S(2)}, u32[]{:S(2)}) collective-permute-start(bf16[128,2048]{1,0:T(8,128)(2,1)} %own_hbm.1), channel_id=1, source_target_pairs={{1,0},{0,1},{3,2},{2,3},{5,4},{4,5},{7,6},{6,7},{9,8},{8,9},{11,10... | collective-permute-start | bytes 1572872 | tf_op jit(solution)/shard_map/ppermute | solution.py:54
  8.8 13.7 %collective-permute-start.1 = (bf16[2048,128]{1,0:T(8,128)(2,1)}, bf16[2048,128]{1,0:T(8,128)(2,1)S(1)}, u32[]{:S(2)}, u32[]{:S(2)}) collective-permute-start(bf16[2048,128]{1,0:T(8,128)(2,1)} %param.6), channel_id=1, source_target_pairs={{0,0},{1,1},{6,2},{7,3},{12,4},{13,5},{2,6},{3,7},{8,8},{9,9},{14,... | collective-permute-start | bytes 1572872 | tf_op jit(solution)/shard_map/ppermute | solution.py:278
  10.5 1.0 %copy-start = (bf16[128,2048]{1,0:T(8,128)(2,1)S(1)}, bf16[128,2048]{1,0:T(8,128)(2,1)}, u32[]{:S(2)}) copy-start(bf16[128,2048]{1,0:T(8,128)(2,1)} %own_hbm.1) | copy-start | bytes 1572868
  11.5 0.7 copy-start.1
  14.7 11.2 %collective-permute-start.2 = (bf16[1024,128]{1,0:T(8,128)(2,1)S(1)}, bf16[1024,128]{1,0:T(8,128)(2,1)S(1)}, u32[]{:S(2)}, u32[]{:S(2)}) collective-permute-start(bf16[1024,128]{1,0:T(8,128)(2,1)S(1)} %shard_map.56.refs_4_.refs_2_), channel_id=1, source_target_pairs={{2,0},{3,1},{4,2},{5,3},{6,4},{7,5},{8,6},{9,7},{10,8},{11,9},{12,... | collective-permute-start | bytes 786440 | tf_op jit(solution)/shard_map/ppermute | solution.py:282
  20.5 17.8 %collective-permute-start.3 = (bf16[1024,128]{1,0:T(8,128)(2,1)S(1)}, bf16[1024,128]{1,0:T(8,128)(2,1)S(1)}, u32[]{:S(2)}, u32[]{:S(2)}) collective-permute-start(bf16[1024,128]{1,0:T(8,128)(2,1)S(1)} %shard_map.56.refs_4_.refs_2_), channel_id=1, source_target_pairs={{14,0},{15,1},{0,2},{1,3},{2,4},{3,5},{4,6},{5,7},{6,8},{7,9},{8,1... | collective-permute-start | bytes 786440 | tf_op jit(solution)/shard_map/ppermute | solution.py:282
  38.3 20.0 %collective-permute-start.5 = (bf16[2048,128]{1,0:T(8,128)(2,1)S(1)}, bf16[2048,128]{1,0:T(8,128)(2,1)S(1)}, u32[]{:S(2)}, u32[]{:S(2)}) collective-permute-start(bf16[2048,128]{1,0:T(8,128)(2,1)S(1)} %shard_map.57.weight_ref.refs_0_), channel_id=1, source_target_pairs={{16,0},{17,1},{18,2},{19,3},{20,4},{21,5},{22,6},{23,7},{24,8},{25... | collective-permute-start | bytes 1572872 | tf_op jit(solution)/shard_map/ppermute | solution.py:285
  47.0 15.4 %collective-permute-start.6 = (bf16[2048,128]{1,0:T(8,128)(2,1)S(1)}, bf16[2048,128]{1,0:T(8,128)(2,1)S(1)}, u32[]{:S(2)}, u32[]{:S(2)}) collective-permute-start(bf16[2048,128]{1,0:T(8,128)(2,1)S(1)} %shard_map.57.weight_ref.refs_0_), channel_id=1, source_target_pairs={{48,0},{49,1},{50,2},{51,3},{52,4},{53,5},{54,6},{55,7},{56,8},{57... | collective-permute-start | bytes 1572872 | tf_op jit(solution)/shard_map/ppermute | solution.py:286
  49.1 21.1 %collective-permute-start.8 = (bf16[3072,128]{1,0:T(8,128)(2,1)S(1)}, bf16[3072,128]{1,0:T(8,128)(2,1)S(1)}, u32[]{:S(2)}, u32[]{:S(2)}) collective-permute-start(bf16[3072,128]{1,0:T(8,128)(2,1)S(1)} %get-tuple-element.23), channel_id=1, source_target_pairs={{2,0},{3,1},{4,2},{5,3},{6,4},{7,5},{8,6},{9,7},{10,8},{11,9},{12,... | collective-permute-start | bytes 2359304 | tf_op jit(solution)/shard_map/ppermute | solution.py:288
  54.4 20.8 %collective-permute-start.9 = (bf16[3072,128]{1,0:T(8,128)(2,1)S(1)}, bf16[3072,128]{1,0:T(8,128)(2,1)S(1)}, u32[]{:S(2)}, u32[]{:S(2)}) collective-permute-start(bf16[3072,128]{1,0:T(8,128)(2,1)S(1)} %get-tuple-element.24), channel_id=1, source_target_pairs={{14,0},{15,1},{0,2},{1,3},{2,4},{3,5},{4,6},{5,7},{6,8},{7,9},{8,1... | collective-permute-start | bytes 2359304 | tf_op jit(solution)/shard_map/ppermute | solution.py:289
  56.3 22.2 %collective-permute-start.10 = (bf16[2048,128]{1,0:T(8,128)(2,1)S(1)}, bf16[2048,128]{1,0:T(8,128)(2,1)S(1)}, u32[]{:S(2)}, u32[]{:S(2)}) collective-permute-start(bf16[2048,128]{1,0:T(8,128)(2,1)S(1)} %shard_map.57.weight_ref.refs_0_), channel_id=1, source_target_pairs={{64,0},{65,1},{66,2},{67,3},{68,4},{69,5},{70,6},{71,7},{72,8},{73... | collective-permute-start | bytes 1572872 | tf_op jit(solution)/shard_map/ppermute | solution.py:290
  58.3 22.1 %collective-permute-start.4 = (bf16[2048,128]{1,0:T(8,128)(2,1)S(1)}, bf16[2048,128]{1,0:T(8,128)(2,1)S(1)}, u32[]{:S(2)}, u32[]{:S(2)}) collective-permute-start(bf16[2048,128]{1,0:T(8,128)(2,1)S(1)} %shard_map.57.weight_ref.refs_0_), channel_id=1, source_target_pairs={{448,0},{449,1},{450,2},{451,3},{452,4},{453,5},{454,6},{455,7},{4... | collective-permute-start | bytes 1572872 | tf_op jit(solution)/shard_map/ppermute | solution.py:291
  62.5 17.8 %collective-permute-start.7 = (bf16[2048,128]{1,0:T(8,128)(2,1)S(1)}, bf16[2048,128]{1,0:T(8,128)(2,1)S(1)}, u32[]{:S(2)}, u32[]{:S(2)}) collective-permute-start(bf16[2048,128]{1,0:T(8,128)(2,1)S(1)} %shard_map.58), channel_id=1, source_target_pairs={{16,0},{49,1},{18,2},{51,3},{20,4},{53,5},{22,6},{55,7},{24,8},{57... | collective-permute-start | bytes 1572872 | tf_op jit(solution)/shard_map/ppermute | solution.py:292
  82.1 5.3 %collective-permute-start.11 = (bf16[128,1024]{1,0:T(8,128)(2,1)S(1)}, bf16[128,1024]{1,0:T(8,128)(2,1)S(1)}, u32[]{:S(2)}, u32[]{:S(2)}) collective-permute-start(bf16[128,1024]{1,0:T(8,128)(2,1)S(1)} %get-tuple-element.32), channel_id=1, source_target_pairs={{1,0},{0,1},{3,2},{2,3},{5,4},{4,5},{7,6},{6,7},{9,8},{8,9},{11,10... | collective-permute-start | bytes 786440 | tf_op jit(solution)/shard_map/ppermute | solution.py:54

commit v7 on v5

--- a/solution.py
+++ b/solution.py
@@ -164,6 +164,7 @@
         out_specs=[VMEM] * 2,
         out_shape=[packed, packed],
         compiler_params=pltpu.CompilerParams(vmem_limit_bytes=4 * 2**20),
+        cost_estimate=pl.CostEstimate(flops=2**32, bytes_accessed=2**21, transcendentals=0),
     )(weight, above, below)
 
 
@@ -274,7 +275,7 @@
     kv = other_kv(other, key_mine, value_mine, kv)
     near = [lax.ppermute(kv, AXES, moves(lambda c, d=d: (0, 0, d))) for d in (1, -1)]
 
-    weight = gate(weight, *near)
+    weight = gate(weight, kv)
     right = lax.ppermute(weight, AXES, moves(lambda c: (0, 1, 0)))
     left = lax.ppermute(weight, AXES, moves(lambda c: (0, -1, 0)))
     down, up = pack(weight, *near)

time: 76.5 us -> 73 us (0.954)
  the two profiles are of different devices: /device:TPU:17 before, /device:TPU:1 now
where the time goes in v7:
time: 73 us; the launch traced here: 72.6 us
  starting transfers between devices  54.3 us (74%)
  Pallas kernels  9.99 us (14%)
  waiting for transfers between devices  7.38 us (10%)
    ppermute x2, starting transfers between devices, swap_cores(): lax.ppermute(value, AXES, [(flat(y, x, z, 1 - c), flat(y, x, z, c)) for y...  14.4 us
    ppermute x1, starting transfers between devices, body(): above = lax.ppermute(down, AXES, moves(lambda c: (0, 0, 1)))  12.1 us
    ppermute x2, starting transfers between devices, body(): lax.ppermute(kv, AXES, moves(lambda c, d=d: (0, 0, d)))  7.21 us
    pallas_call x3, Pallas kernels, some_heads(): pl.pallas_call(functools.partial(heads_kernel, tuple((shift for shift, _...  6.77 us
    ppermute x1, starting transfers between devices, body(): right = lax.ppermute(weight, AXES, moves(lambda c: (0, 1, 0)))  6.33 us
    ppermute x1, starting transfers between devices, body(): front = lax.ppermute(weight, AXES, moves(lambda c: (1, 0, 0)))  4.57 us
    ppermute x1, waiting for transfers between devices, body(): below = lax.ppermute(up, AXES, moves(lambda c: (0, 0, -1)))  2 us
    ppermute x1, starting transfers between devices, body(): below = lax.ppermute(up, AXES, moves(lambda c: (0, 0, -1)))  1.98 us
  transfers between devices with their start and end apart: 12, of which 6 were waited for; matrix products, arithmetic and copies ran while one was open for 0% of the time, Pallas kernels for 10%

profile of v7, /device:TPU:1, one launch (start us, length us, event | category | flops | bytes accessed | tf_op | source)
XLA Modules:
  0.0 72.6 jit_solution(7533894604342447807)
XLA Ops:
  0.0 8.8 %collective-permute-start = (bf16[128,2048]{1,0:T(8,128)(2,1)}, bf16[128,2048]{1,0:T(8,128)(2,1)S(1)}, u32[]{:S(2)}, u32[]{:S(2)}) collective-permute-start(bf16[128,2048]{1,0:T(8,128)(2,1)} %own_hbm.1), channel_id=1, source_target_pairs={{1,0},{0,1},{3,2},{2,3},{5,4},{4,5},{7,6},{6,7},{9,8},{8,9},{11,10... | collective-permute-start | bytes 1572872 | tf_op jit(solution)/shard_map/ppermute | solution.py:51
  8.8 1.9 %collective-permute-start.1 = (bf16[2048,128]{1,0:T(8,128)(2,1)}, bf16[2048,128]{1,0:T(8,128)(2,1)S(1)}, u32[]{:S(2)}, u32[]{:S(2)}) collective-permute-start(bf16[2048,128]{1,0:T(8,128)(2,1)} %param.6), channel_id=1, source_target_pairs={{5,0},{15,1},{3,2},{11,3},{1,4},{8,5},{7,6},{14,7},{4,8},{10,9},{2... | collective-permute-start | bytes 1572872 | tf_op jit(solution)/shard_map/ppermute | solution.py:272
  10.7 0.0 copy-start
  10.7 0.6 copy-done
  11.4 1.8 %shard_map.55 = (bf16[128,2048]{1,0:T(8,128)(2,1)S(1)}, bf16[2048,128]{1,0:T(8,128)(2,1)S(1)}, bf16[2048,128]{1,0:T(8,128)(2,1)S(1)}, bf16[512,128]{1,0:T(8,128)...) custom-call(s32[16]{0:T(128)S(1)} %copy-done, bf16[128,2048]{1,0:T(8,128)(2,1)} %own_hbm.1, ...), custom_call_target="tpu_custom_call" | custom-call | flops 134217728 | bytes 2097152 | tf_op jit(solution)/shard_map/pallas_call | solution.py:103
  13.2 0.0 collective-permute-done.other_ref
  13.2 0.4 shard_map.56.refs_1_.refs_4_.refs_2_
  13.6 5.3 %collective-permute-start.6 = (bf16[512,128]{1,0:T(8,128)(2,1)S(1)}, bf16[512,128]{1,0:T(8,128)(2,1)S(1)}, u32[]{:S(2)}, u32[]{:S(2)}) collective-permute-start(bf16[512,128]{1,0:T(8,128)(2,1)S(1)} %shard_map.56.refs_1_.refs_4_.refs_2_), channel_id=1, source_target_pairs={{2,0},{3,1},{4,2},{5,3},{6,4},{7,5},{8,6},{9,7},{10,8},{11,9},{12,... | collective-permute-start | bytes 393224 | tf_op jit(solution)/shard_map/ppermute | solution.py:276
  18.9 1.9 %collective-permute-start.7 = (bf16[512,128]{1,0:T(8,128)(2,1)S(1)}, bf16[512,128]{1,0:T(8,128)(2,1)S(1)}, u32[]{:S(2)}, u32[]{:S(2)}) collective-permute-start(bf16[512,128]{1,0:T(8,128)(2,1)S(1)} %shard_map.56.refs_1_.refs_4_.refs_2_), channel_id=1, source_target_pairs={{14,0},{15,1},{0,2},{1,3},{2,4},{3,5},{4,6},{5,7},{6,8},{7,9},{8,1... | collective-permute-start | bytes 393224 | tf_op jit(solution)/shard_map/ppermute | solution.py:276
  20.9 0.1 collective-permute-done.1.refs_0_
  21.0 6.3 %collective-permute-start.3 = (bf16[2048,128]{1,0:T(8,128)(2,1)S(1)}, bf16[2048,128]{1,0:T(8,128)(2,1)S(1)}, u32[]{:S(2)}, u32[]{:S(2)}) collective-permute-start(bf16[2048,128]{1,0:T(8,128)(2,1)S(1)} %shard_map.57.weight_ref.refs_0_), channel_id=1, source_target_pairs={{16,0},{17,1},{18,2},{19,3},{20,4},{21,5},{22,6},{23,7},{24,8},{25... | collective-permute-start | bytes 1572872 | tf_op jit(solution)/shard_map/ppermute | solution.py:279
  27.3 1.9 %collective-permute-start.4 = (bf16[2048,128]{1,0:T(8,128)(2,1)S(1)}, bf16[2048,128]{1,0:T(8,128)(2,1)S(1)}, u32[]{:S(2)}, u32[]{:S(2)}) collective-permute-start(bf16[2048,128]{1,0:T(8,128)(2,1)S(1)} %shard_map.57.weight_ref.refs_0_), channel_id=1, source_target_pairs={{48,0},{49,1},{50,2},{51,3},{52,4},{53,5},{54,6},{55,7},{56,8},{57... | collective-permute-start | bytes 1572872 | tf_op jit(solution)/shard_map/ppermute | solution.py:280
  29.3 0.0 collective-permute-done.6.above_ref.refs_5_.refs_3_
  29.3 0.0 collective-permute-done.7.below_ref.refs_6_.refs_4_
  29.3 0.1 shard_map.59
  29.4 12.1 %collective-permute-start.8 = (bf16[2560,128]{1,0:T(8,128)(2,1)S(1)}, bf16[2560,128]{1,0:T(8,128)(2,1)S(1)}, u32[]{:S(2)}, u32[]{:S(2)}) collective-permute-start(bf16[2560,128]{1,0:T(8,128)(2,1)S(1)} %get-tuple-element.23), channel_id=1, source_target_pairs={{2,0},{3,1},{4,2},{5,3},{6,4},{7,5},{8,6},{9,7},{10,8},{11,9},{12,... | collective-permute-start | bytes 1966088 | tf_op jit(solution)/shard_map/ppermute | solution.py:282
  41.5 2.0 %collective-permute-start.9 = (bf16[2560,128]{1,0:T(8,128)(2,1)S(1)}, bf16[2560,128]{1,0:T(8,128)(2,1)S(1)}, u32[]{:S(2)}, u32[]{:S(2)}) collective-permute-start(bf16[2560,128]{1,0:T(8,128)(2,1)S(1)} %get-tuple-element.24), channel_id=1, source_target_pairs={{14,0},{15,1},{0,2},{1,3},{2,4},{3,5},{4,6},{5,7},{6,8},{7,9},{8,1... | collective-permute-start | bytes 1966088 | tf_op jit(solution)/shard_map/ppermute | solution.py:283
  43.5 4.6 %collective-permute-start.10 = (bf16[2048,128]{1,0:T(8,128)(2,1)S(1)}, bf16[2048,128]{1,0:T(8,128)(2,1)S(1)}, u32[]{:S(2)}, u32[]{:S(2)}) collective-permute-start(bf16[2048,128]{1,0:T(8,128)(2,1)S(1)} %shard_map.57.weight_ref.refs_0_), channel_id=1, source_target_pairs={{64,0},{65,1},{66,2},{67,3},{68,4},{69,5},{70,6},{71,7},{72,8},{73... | collective-permute-start | bytes 1572872 | tf_op jit(solution)/shard_map/ppermute | solution.py:284
  48.1 0.0 collective-permute-done.3.first_ref.refs_1_
  48.1 1.9 %collective-permute-start.2 = (bf16[2048,128]{1,0:T(8,128)(2,1)S(1)}, bf16[2048,128]{1,0:T(8,128)(2,1)S(1)}, u32[]{:S(2)}, u32[]{:S(2)}) collective-permute-start(bf16[2048,128]{1,0:T(8,128)(2,1)S(1)} %shard_map.57.weight_ref.refs_0_), channel_id=1, source_target_pairs={{448,0},{449,1},{450,2},{451,3},{452,4},{453,5},{454,6},{455,7},{4... | collective-permute-start | bytes 1572872 | tf_op jit(solution)/shard_map/ppermute | solution.py:285
  50.0 1.7 %collective-permute-done.4.second_ref.refs_2_ = bf16[2048,128]{1,0:T(8,128)(2,1)S(1)} collective-permute-done((bf16[2048,128]{1,0:T(8,128)(2,1)S(1)}, bf16[2048,128]{1,0:T(8,128)(2,1)S(1)}, u32[]{:S(2)}, u32[]{:S(2)}) %collective-permute-start.4) | collective-permute-done | bytes 524320 | tf_op jit(solution)/shard_map/ppermute | solution.py:280
  51.8 1.9 %collective-permute-start.5 = (bf16[2048,128]{1,0:T(8,128)(2,1)S(1)}, bf16[2048,128]{1,0:T(8,128)(2,1)S(1)}, u32[]{:S(2)}, u32[]{:S(2)}) collective-permute-start(bf16[2048,128]{1,0:T(8,128)(2,1)S(1)} %shard_map.58), channel_id=1, source_target_pairs={{16,0},{49,1},{18,2},{51,3},{20,4},{53,5},{22,6},{55,7},{24,8},{57... | collective-permute-start | bytes 1572872 | tf_op jit(solution)/shard_map/ppermute | solution.py:286
  53.7 1.2 %collective-permute-done.8.refs_3_.refs_7_.refs_5_ = bf16[2560,128]{1,0:T(8,128)(2,1)S(1)} collective-permute-done((bf16[2560,128]{1,0:T(8,128)(2,1)S(1)}, bf16[2560,128]{1,0:T(8,128)(2,1)S(1)}, u32[]{:S(2)}, u32[]{:S(2)}) %collective-permute-start.8) | collective-permute-done | bytes 655392 | tf_op jit(solution)/shard_map/ppermute | solution.py:282
  54.9 2.0 %collective-permute-done.9.refs_8_.refs_0_.refs_6_ = bf16[2560,128]{1,0:T(8,128)(2,1)S(1)} collective-permute-done((bf16[2560,128]{1,0:T(8,128)(2,1)S(1)}, bf16[2560,128]{1,0:T(8,128)(2,1)S(1)}, u32[]{:S(2)}, u32[]{:S(2)}) %collective-permute-start.9) | collective-permute-done | bytes 655392 | tf_op jit(solution)/shard_map/ppermute | solution.py:283
  57.0 3.3 %shard_map.60 = (bf16[128,1024]{1,0:T(8,128)(2,1)S(1)}, bf16[128,1024]{1,0:T(8,128)(2,1)S(1)}) custom-call(bf16[128,2048]{1,0:T(8,128)(2,1)S(1)} %get-tuple-element.19.own_ref, bf16[128,2048]{1,0:T(8,128)(2,1)S(1)} %collective-permute-done.other_ref, ...), custom_call_target="tpu_custom_call", output_to_operand_aliasing={{0}: (13, {}), {1}: (14, {})} | custom-call | flops 268435456 | bytes 2097152 | tf_op jit(solution)/shard_map/pallas_call | solution.py:243
  60.3 0.0 collective-permute-done.10.refs_1_
  60.3 1.7 %shard_map.61 = (bf16[128,1024]{1,0:T(8,128)(2,1)S(1)}, bf16[128,1024]{1,0:T(8,128)(2,1)S(1)}) custom-call(bf16[128,2048]{1,0:T(8,128)(2,1)S(1)} %get-tuple-element.19.own_ref, bf16[128,2048]{1,0:T(8,128)(2,1)S(1)} %collective-permute-done.other_ref, ...), custom_call_target="tpu_custom_call", output_to_operand_aliasing={{0}: (11, {}), {1}: (12, {})} | custom-call | flops 268435456 | bytes 2097152 | tf_op jit(solution)/shard_map/pallas_call | solution.py:243
  62.0 0.0 collective-permute-done.2.refs_0_
  62.1 1.2 %collective-permute-done.5.refs_1_ = bf16[2048,128]{1,0:T(8,128)(2,1)S(1)} collective-permute-done((bf16[2048,128]{1,0:T(8,128)(2,1)S(1)}, bf16[2048,128]{1,0:T(8,128)(2,1)S(1)}, u32[]{:S(2)}, u32[]{:S(2)}) %collective-permute-start.5) | collective-permute-done | bytes 524320 | tf_op jit(solution)/shard_map/ppermute | solution.py:286
  63.2 1.7 %shard_map.62 = (bf16[128,1024]{1,0:T(8,128)(2,1)S(1)}, bf16[128,1024]{1,0:T(8,128)(2,1)S(1)}) custom-call(bf16[128,2048]{1,0:T(8,128)(2,1)S(1)} %get-tuple-element.19.own_ref, bf16[128,2048]{1,0:T(8,128)(2,1)S(1)} %collective-permute-done.other_ref, ...), custom_call_target="tpu_custom_call", output_to_operand_aliasing={{0}: (11, {}), {1}: (12, {})} | custom-call | flops 268435456 | bytes 2097152 | tf_op jit(solution)/shard_map/pallas_call | solution.py:243
  65.0 5.6 %collective-permute-start.11 = (bf16[128,1024]{1,0:T(8,128)(2,1)S(1)}, bf16[128,1024]{1,0:T(8,128)(2,1)S(1)}, u32[]{:S(2)}, u32[]{:S(2)}) collective-permute-start(bf16[128,1024]{1,0:T(8,128)(2,1)S(1)} %get-tuple-element.32), channel_id=1, source_target_pairs={{1,0},{0,1},{3,2},{2,3},{5,4},{4,5},{7,6},{6,7},{9,8},{8,9},{11,10... | collective-permute-start | bytes 786440 | tf_op jit(solution)/shard_map/ppermute | solution.py:51
  70.6 1.1 %collective-permute-done.11.other_ref = bf16[128,1024]{1,0:T(8,128)(2,1)S(1)} collective-permute-done((bf16[128,1024]{1,0:T(8,128)(2,1)S(1)}, bf16[128,1024]{1,0:T(8,128)(2,1)S(1)}, u32[]{:S(2)}, u32[]{:S(2)}) %collective-permute-start.11) | collective-permute-done | bytes 262176 | tf_op jit(solution)/shard_map/ppermute | solution.py:51
  71.7 0.8 %shard_map.63 = bf16[128,2048]{1,0:T(8,128)(2,1)} custom-call(bf16[128,1024]{1,0:T(8,128)(2,1)S(1)} %get-tuple-element.31.mine_ref, bf16[128,1024]{1,0:T(8,128)(2,1)S(1)} %collective-permute-done.11.other_ref), custom_call_target="tpu_custom_call" | custom-call | tf_op jit(solution)/shard_map/pallas_call | solution.py:261
  (4 shorter events, 0.1 us)
Async XLA Ops:
  0.0 13.2 %collective-permute-start = (bf16[128,2048]{1,0:T(8,128)(2,1)}, bf16[128,2048]{1,0:T(8,128)(2,1)S(1)}, u32[]{:S(2)}, u32[]{:S(2)}) collective-permute-start(bf16[128,2048]{1,0:T(8,128)(2,1)} %own_hbm.1), channel_id=1, source_target_pairs={{1,0},{0,1},{3,2},{2,3},{5,4},{4,5},{7,6},{6,7},{9,8},{8,9},{11,10... | collective-permute-start | bytes 1572872 | tf_op jit(solution)/shard_map/ppermute | solution.py:51
  8.8 12.2 %collective-permute-start.1 = (bf16[2048,128]{1,0:T(8,128)(2,1)}, bf16[2048,128]{1,0:T(8,128)(2,1)S(1)}, u32[]{:S(2)}, u32[]{:S(2)}) collective-permute-start(bf16[2048,128]{1,0:T(8,128)(2,1)} %param.6), channel_id=1, source_target_pairs={{5,0},{15,1},{3,2},{11,3},{1,4},{8,5},{7,6},{14,7},{4,8},{10,9},{2... | collective-permute-start | bytes 1572872 | tf_op jit(solution)/shard_map/ppermute | solution.py:272
  10.7 0.7 copy-start
  13.6 15.6 %collective-permute-start.6 = (bf16[512,128]{1,0:T(8,128)(2,1)S(1)}, bf16[512,128]{1,0:T(8,128)(2,1)S(1)}, u32[]{:S(2)}, u32[]{:S(2)}) collective-permute-start(bf16[512,128]{1,0:T(8,128)(2,1)S(1)} %shard_map.56.refs_1_.refs_4_.refs_2_), channel_id=1, source_target_pairs={{2,0},{3,1},{4,2},{5,3},{6,4},{7,5},{8,6},{9,7},{10,8},{11,9},{12,... | collective-permute-start | bytes 393224 | tf_op jit(solution)/shard_map/ppermute | solution.py:276
  18.9 10.3 %collective-permute-start.7 = (bf16[512,128]{1,0:T(8,128)(2,1)S(1)}, bf16[512,128]{1,0:T(8,128)(2,1)S(1)}, u32[]{:S(2)}, u32[]{:S(2)}) collective-permute-start(bf16[512,128]{1,0:T(8,128)(2,1)S(1)} %shard_map.56.refs_1_.refs_4_.refs_2_), channel_id=1, source_target_pairs={{14,0},{15,1},{0,2},{1,3},{2,4},{3,5},{4,6},{5,7},{6,8},{7,9},{8,1... | collective-permute-start | bytes 393224 | tf_op jit(solution)/shard_map/ppermute | solution.py:276
  21.0 27.1 %collective-permute-start.3 = (bf16[2048,128]{1,0:T(8,128)(2,1)S(1)}, bf16[2048,128]{1,0:T(8,128)(2,1)S(1)}, u32[]{:S(2)}, u32[]{:S(2)}) collective-permute-start(bf16[2048,128]{1,0:T(8,128)(2,1)S(1)} %shard_map.57.weight_ref.refs_0_), channel_id=1, source_target_pairs={{16,0},{17,1},{18,2},{19,3},{20,4},{21,5},{22,6},{23,7},{24,8},{25... | collective-permute-start | bytes 1572872 | tf_op jit(solution)/shard_map/ppermute | solution.py:279
  27.3 24.4 %collective-permute-start.4 = (bf16[2048,128]{1,0:T(8,128)(2,1)S(1)}, bf16[2048,128]{1,0:T(8,128)(2,1)S(1)}, u32[]{:S(2)}, u32[]{:S(2)}) collective-permute-start(bf16[2048,128]{1,0:T(8,128)(2,1)S(1)} %shard_map.57.weight_ref.refs_0_), channel_id=1, source_target_pairs={{48,0},{49,1},{50,2},{51,3},{52,4},{53,5},{54,6},{55,7},{56,8},{57... | collective-permute-start | bytes 1572872 | tf_op jit(solution)/shard_map/ppermute | solution.py:280
  29.4 25.5 %collective-permute-start.8 = (bf16[2560,128]{1,0:T(8,128)(2,1)S(1)}, bf16[2560,128]{1,0:T(8,128)(2,1)S(1)}, u32[]{:S(2)}, u32[]{:S(2)}) collective-permute-start(bf16[2560,128]{1,0:T(8,128)(2,1)S(1)} %get-tuple-element.23), channel_id=1, source_target_pairs={{2,0},{3,1},{4,2},{5,3},{6,4},{7,5},{8,6},{9,7},{10,8},{11,9},{12,... | collective-permute-start | bytes 1966088 | tf_op jit(solution)/shard_map/ppermute | solution.py:282
  41.5 15.4 %collective-permute-start.9 = (bf16[2560,128]{1,0:T(8,128)(2,1)S(1)}, bf16[2560,128]{1,0:T(8,128)(2,1)S(1)}, u32[]{:S(2)}, u32[]{:S(2)}) collective-permute-start(bf16[2560,128]{1,0:T(8,128)(2,1)S(1)} %get-tuple-element.24), channel_id=1, source_target_pairs={{14,0},{15,1},{0,2},{1,3},{2,4},{3,5},{4,6},{5,7},{6,8},{7,9},{8,1... | collective-permute-start | bytes 1966088 | tf_op jit(solution)/shard_map/ppermute | solution.py:283
  43.5 16.8 %collective-permute-start.10 = (bf16[2048,128]{1,0:T(8,128)(2,1)S(1)}, bf16[2048,128]{1,0:T(8,128)(2,1)S(1)}, u32[]{:S(2)}, u32[]{:S(2)}) collective-permute-start(bf16[2048,128]{1,0:T(8,128)(2,1)S(1)} %shard_map.57.weight_ref.refs_0_), channel_id=1, source_target_pairs={{64,0},{65,1},{66,2},{67,3},{68,4},{69,5},{70,6},{71,7},{72,8},{73... | collective-permute-start | bytes 1572872 | tf_op jit(solution)/shard_map/ppermute | solution.py:284
  48.1 14.0 %collective-permute-start.2 = (bf16[2048,128]{1,0:T(8,128)(2,1)S(1)}, bf16[2048,128]{1,0:T(8,128)(2,1)S(1)}, u32[]{:S(2)}, u32[]{:S(2)}) collective-permute-start(bf16[2048,128]{1,0:T(8,128)(2,1)S(1)} %shard_map.57.weight_ref.refs_0_), channel_id=1, source_target_pairs={{448,0},{449,1},{450,2},{451,3},{452,4},{453,5},{454,6},{455,7},{4... | collective-permute-start | bytes 1572872 | tf_op jit(solution)/shard_map/ppermute | solution.py:285
  51.8 11.4 %collective-permute-start.5 = (bf16[2048,128]{1,0:T(8,128)(2,1)S(1)}, bf16[2048,128]{1,0:T(8,128)(2,1)S(1)}, u32[]{:S(2)}, u32[]{:S(2)}) collective-permute-start(bf16[2048,128]{1,0:T(8,128)(2,1)S(1)} %shard_map.58), channel_id=1, source_target_pairs={{16,0},{49,1},{18,2},{51,3},{20,4},{53,5},{22,6},{55,7},{24,8},{57... | collective-permute-start | bytes 1572872 | tf_op jit(solution)/shard_map/ppermute | solution.py:286
  65.0 6.8 %collective-permute-start.11 = (bf16[128,1024]{1,0:T(8,128)(2,1)S(1)}, bf16[128,1024]{1,0:T(8,128)(2,1)S(1)}, u32[]{:S(2)}, u32[]{:S(2)}) collective-permute-start(bf16[128,1024]{1,0:T(8,128)(2,1)S(1)} %get-tuple-element.32), channel_id=1, source_target_pairs={{1,0},{0,1},{3,2},{2,3},{5,4},{4,5},{7,6},{6,7},{9,8},{8,9},{11,10... | collective-permute-start | bytes 786440 | tf_op jit(solution)/shard_map/ppermute | solution.py:51

commit v8 on v7

--- a/solution.py
+++ b/solution.py
@@ -190,18 +190,18 @@
     )(first, second)
 
 
-def attend(queries, kv, bases, docs, key_docs):
+def attend(queries, kv, bases, docs, key_docs, blocks):
     factor = math.log2(math.e) / math.sqrt(HEAD_SIZE)
-    scores = []
-    for i in range(5):
+    scores = {}
+    for i in blocks:
         product = lax.dot_general(
             queries, kv[i][bases[i] : bases[i] + PAIR], (((1,), (1,)), ((), ())), preferred_element_type=jnp.float32
         )
         allowed = docs == key_docs[:, i * PAIR : (i + 1) * PAIR]
-        scores.append(jnp.where(allowed, product, NEG))
-    highest = functools.reduce(jnp.maximum, [jnp.max(s, axis=1, keepdims=True) for s in scores])
+        scores[i] = jnp.where(allowed, product, NEG)
+    highest = functools.reduce(jnp.maximum, [jnp.max(s, axis=1, keepdims=True) for s in scores.values()])
     summed, mixed = 0.0, 0.0
-    for i in range(5):
+    for i in blocks:
         part = jnp.exp2((scores[i] - highest) * factor)
         summed = summed + jnp.sum(part, axis=1, keepdims=True)
         mixed = mixed + jnp.dot(
@@ -215,25 +215,48 @@
     kv, (row_docs, key_docs, _, _, keep_ref, send_ref) = refs[:5], refs[5:]
     y, x, z, c = place()
     docs = row_docs[...]
+    queries = []
     for first in range(0, len(shifts), 2):
-        pair = weights[first : first + 2]
-        matrix = jnp.concatenate([w[:WIDTH] for w in pair], axis=1)
-        queries = jnp.concatenate(
-            [
-                jnp.dot(rows[...], matrix, preferred_element_type=jnp.float32).astype(jnp.bfloat16)
-                for rows in (own_ref, other_ref)
-            ],
-            axis=0,
+        matrix = jnp.concatenate([w[:WIDTH] for w in weights[first : first + 2]], axis=1)
+        queries.append(
+            jnp.concatenate(
+                [
+                    jnp.dot(rows[...], matrix, preferred_element_type=jnp.float32).astype(jnp.bfloat16)
+                    for rows in (own_ref, other_ref)
+                ],
+                axis=0,
+            )
         )
-        for i, shift in enumerate(shifts[first : first + 2]):
-            color = (2 * x + 3 * y + z + shift) % 8
-            slot = 0
-            for k in range(8):
-                slot = slot + jnp.where(color == k, jnp.where(c == 0, ORDER[0][k], ORDER[1][k]), 0)
-            result = attend(queries[:, i * HEAD_SIZE : (i + 1) * HEAD_SIZE], kv, bases, docs, key_docs)
-            columns = pl.ds(pl.multiple_of(slot * HEAD_SIZE, HEAD_SIZE), HEAD_SIZE)
-            keep_ref[:, columns] = result[:ROWS]
-            send_ref[:, columns] = result[ROWS:]
+
+    lowest = jnp.minimum(row_docs[0, 0], row_docs[ROWS, 0])
+    highest = jnp.maximum(row_docs[ROWS - 1, 0], row_docs[PAIR - 1, 0])
+
+    def reached(i):
+        first = jnp.minimum(key_docs[0, i * PAIR], key_docs[0, i * PAIR + ROWS])
+        last = jnp.maximum(key_docs[0, i * PAIR + ROWS - 1], key_docs[0, i * PAIR + PAIR - 1])
+        return jnp.logical_and(first <= highest, last >= lowest)
+
+    after, before = reached(3), reached(4)
+    cases = (
+        (jnp.logical_not(jnp.logical_or(after, before)), (0, 1, 2)),
+        (jnp.logical_and(after, jnp.logical_not(before)), (0, 1, 2, 3)),
+        (jnp.logical_and(before, jnp.logical_not(after)), (0, 1, 2, 4)),
+        (jnp.logical_and(after, before), (0, 1, 2, 3, 4)),
+    )
+    for case, blocks in cases:
+
+        @pl.when(case)
+        def _(blocks=blocks):
+            for n, shift in enumerate(shifts):
+                color = (2 * x + 3 * y + z + shift) % 8
+                slot = 0
+                for k in range(8):
+                    slot = slot + jnp.where(color == k, jnp.where(c == 0, ORDER[0][k], ORDER[1][k]), 0)
+                half = queries[n // 2][:, n % 2 * HEAD_SIZE : (n % 2 + 1) * HEAD_SIZE]
+                result = attend(half, kv, bases, docs, key_docs, blocks)
+                columns = pl.ds(pl.multiple_of(slot * HEAD_SIZE, HEAD_SIZE), HEAD_SIZE)
+                keep_ref[:, columns] = result[:ROWS]
+                send_ref[:, columns] = result[ROWS:]
 
 
 def some_heads(arrivals, own, other, kv, row_docs, key_docs, keep, send):

time: 73 us -> 72.1 us (0.988)
  Pallas kernels: 9.99 us -> 9.09 us
    pallas_call x3, Pallas kernels: 6.77 us -> 5.88 us  [some_heads(): pl.pallas_call(functools.partial(heads_kernel, tuple((shift for shift, _...]
    ppermute x2, starting transfers between devices: 14.4 us -> 13.7 us  [swap_cores(): lax.ppermute(value, AXES, [(flat(y, x, z, 1 - c), flat(y, x, z, c)) for y...]
  transfers between devices with their start and end apart: 12 -> 12, of which waited for: 6 -> 7; matrix products, arithmetic and copies ran while one was open for 0% -> 0% of each run, Pallas kernels for 10% -> 9%
where the time goes in v8:
time: 72.1 us; the launch traced here: 71.7 us
  starting transfers between devices  53.6 us (74%)
  Pallas kernels  9.09 us (13%)
  waiting for transfers between devices  8.09 us (11%)
    ppermute x2, starting transfers between devices, swap_cores(): lax.ppermute(value, AXES, [(flat(y, x, z, 1 - c), flat(y, x, z, c)) for y...  13.7 us
    ppermute x1, starting transfers between devices, body(): above = lax.ppermute(down, AXES, moves(lambda c: (0, 0, 1)))  12.1 us
    ppermute x2, starting transfers between devices, body(): lax.ppermute(kv, AXES, moves(lambda c, d=d: (0, 0, d)))  7.21 us
    ppermute x1, starting transfers between devices, body(): right = lax.ppermute(weight, AXES, moves(lambda c: (0, 1, 0)))  6.33 us
    pallas_call x3, Pallas kernels, some_heads(): pl.pallas_call(functools.partial(heads_kernel, tuple((shift for shift, _...  5.88 us
    ppermute x1, starting transfers between devices, body(): front = lax.ppermute(weight, AXES, moves(lambda c: (1, 0, 0)))  4.57 us
    ppermute x1, waiting for transfers between devices, body(): below = lax.ppermute(up, AXES, moves(lambda c: (0, 0, -1)))  2 us
    ppermute x1, starting transfers between devices, body(): below = lax.ppermute(up, AXES, moves(lambda c: (0, 0, -1)))  1.98 us
  transfers between devices with their start and end apart: 12, of which 7 were waited for; matrix products, arithmetic and copies ran while one was open for 0% of the time, Pallas kernels for 9%

profile of v8, /device:TPU:1, one launch (start us, length us, event | category | flops | bytes accessed | tf_op | source)
XLA Modules:
  0.0 71.7 jit_solution(16831215295567214802)
XLA Ops:
  0.0 8.8 %collective-permute-start = (bf16[128,2048]{1,0:T(8,128)(2,1)}, bf16[128,2048]{1,0:T(8,128)(2,1)S(1)}, u32[]{:S(2)}, u32[]{:S(2)}) collective-permute-start(bf16[128,2048]{1,0:T(8,128)(2,1)} %own_hbm.1), channel_id=1, source_target_pairs={{1,0},{0,1},{3,2},{2,3},{5,4},{4,5},{7,6},{6,7},{9,8},{8,9},{11,10... | collective-permute-start | bytes 1572872 | tf_op jit(solution)/shard_map/ppermute | solution.py:51
  8.8 1.9 %collective-permute-start.1 = (bf16[2048,128]{1,0:T(8,128)(2,1)}, bf16[2048,128]{1,0:T(8,128)(2,1)S(1)}, u32[]{:S(2)}, u32[]{:S(2)}) collective-permute-start(bf16[2048,128]{1,0:T(8,128)(2,1)} %param.6), channel_id=1, source_target_pairs={{5,0},{15,1},{3,2},{11,3},{1,4},{8,5},{7,6},{14,7},{4,8},{10,9},{2... | collective-permute-start | bytes 1572872 | tf_op jit(solution)/shard_map/ppermute | solution.py:295
  10.7 0.0 copy-start
  10.7 0.6 copy-done
  11.4 1.8 %shard_map.55 = (bf16[128,2048]{1,0:T(8,128)(2,1)S(1)}, bf16[2048,128]{1,0:T(8,128)(2,1)S(1)}, bf16[2048,128]{1,0:T(8,128)(2,1)S(1)}, bf16[512,128]{1,0:T(8,128)...) custom-call(s32[16]{0:T(128)S(1)} %copy-done, bf16[128,2048]{1,0:T(8,128)(2,1)} %own_hbm.1, ...), custom_call_target="tpu_custom_call" | custom-call | flops 134217728 | bytes 2097152 | tf_op jit(solution)/shard_map/pallas_call | solution.py:103
  13.2 0.0 collective-permute-done.other_ref
  13.2 0.4 shard_map.56.refs_1_.refs_4_.refs_2_
  13.6 5.3 %collective-permute-start.6 = (bf16[512,128]{1,0:T(8,128)(2,1)S(1)}, bf16[512,128]{1,0:T(8,128)(2,1)S(1)}, u32[]{:S(2)}, u32[]{:S(2)}) collective-permute-start(bf16[512,128]{1,0:T(8,128)(2,1)S(1)} %shard_map.56.refs_1_.refs_4_.refs_2_), channel_id=1, source_target_pairs={{2,0},{3,1},{4,2},{5,3},{6,4},{7,5},{8,6},{9,7},{10,8},{11,9},{12,... | collective-permute-start | bytes 393224 | tf_op jit(solution)/shard_map/ppermute | solution.py:299
  18.9 1.9 %collective-permute-start.7 = (bf16[512,128]{1,0:T(8,128)(2,1)S(1)}, bf16[512,128]{1,0:T(8,128)(2,1)S(1)}, u32[]{:S(2)}, u32[]{:S(2)}) collective-permute-start(bf16[512,128]{1,0:T(8,128)(2,1)S(1)} %shard_map.56.refs_1_.refs_4_.refs_2_), channel_id=1, source_target_pairs={{14,0},{15,1},{0,2},{1,3},{2,4},{3,5},{4,6},{5,7},{6,8},{7,9},{8,1... | collective-permute-start | bytes 393224 | tf_op jit(solution)/shard_map/ppermute | solution.py:299
  20.9 0.1 collective-permute-done.1.refs_0_
  21.0 6.3 %collective-permute-start.3 = (bf16[2048,128]{1,0:T(8,128)(2,1)S(1)}, bf16[2048,128]{1,0:T(8,128)(2,1)S(1)}, u32[]{:S(2)}, u32[]{:S(2)}) collective-permute-start(bf16[2048,128]{1,0:T(8,128)(2,1)S(1)} %shard_map.57.weight_ref.refs_0_), channel_id=1, source_target_pairs={{16,0},{17,1},{18,2},{19,3},{20,4},{21,5},{22,6},{23,7},{24,8},{25... | collective-permute-start | bytes 1572872 | tf_op jit(solution)/shard_map/ppermute | solution.py:302
  27.3 1.9 %collective-permute-start.4 = (bf16[2048,128]{1,0:T(8,128)(2,1)S(1)}, bf16[2048,128]{1,0:T(8,128)(2,1)S(1)}, u32[]{:S(2)}, u32[]{:S(2)}) collective-permute-start(bf16[2048,128]{1,0:T(8,128)(2,1)S(1)} %shard_map.57.weight_ref.refs_0_), channel_id=1, source_target_pairs={{48,0},{49,1},{50,2},{51,3},{52,4},{53,5},{54,6},{55,7},{56,8},{57... | collective-permute-start | bytes 1572872 | tf_op jit(solution)/shard_map/ppermute | solution.py:303
  29.3 0.0 collective-permute-done.6.above_ref.refs_5_.refs_3_
  29.3 0.0 collective-permute-done.7.below_ref.refs_6_.refs_4_
  29.3 0.1 shard_map.59
  29.4 12.1 %collective-permute-start.8 = (bf16[2560,128]{1,0:T(8,128)(2,1)S(1)}, bf16[2560,128]{1,0:T(8,128)(2,1)S(1)}, u32[]{:S(2)}, u32[]{:S(2)}) collective-permute-start(bf16[2560,128]{1,0:T(8,128)(2,1)S(1)} %get-tuple-element.23), channel_id=1, source_target_pairs={{2,0},{3,1},{4,2},{5,3},{6,4},{7,5},{8,6},{9,7},{10,8},{11,9},{12,... | collective-permute-start | bytes 1966088 | tf_op jit(solution)/shard_map/ppermute | solution.py:305
  41.5 2.0 %collective-permute-start.9 = (bf16[2560,128]{1,0:T(8,128)(2,1)S(1)}, bf16[2560,128]{1,0:T(8,128)(2,1)S(1)}, u32[]{:S(2)}, u32[]{:S(2)}) collective-permute-start(bf16[2560,128]{1,0:T(8,128)(2,1)S(1)} %get-tuple-element.24), channel_id=1, source_target_pairs={{14,0},{15,1},{0,2},{1,3},{2,4},{3,5},{4,6},{5,7},{6,8},{7,9},{8,1... | collective-permute-start | bytes 1966088 | tf_op jit(solution)/shard_map/ppermute | solution.py:306
  43.5 4.6 %collective-permute-start.10 = (bf16[2048,128]{1,0:T(8,128)(2,1)S(1)}, bf16[2048,128]{1,0:T(8,128)(2,1)S(1)}, u32[]{:S(2)}, u32[]{:S(2)}) collective-permute-start(bf16[2048,128]{1,0:T(8,128)(2,1)S(1)} %shard_map.57.weight_ref.refs_0_), channel_id=1, source_target_pairs={{64,0},{65,1},{66,2},{67,3},{68,4},{69,5},{70,6},{71,7},{72,8},{73... | collective-permute-start | bytes 1572872 | tf_op jit(solution)/shard_map/ppermute | solution.py:307
  48.1 0.0 collective-permute-done.3.first_ref.refs_1_
  48.1 1.9 %collective-permute-start.2 = (bf16[2048,128]{1,0:T(8,128)(2,1)S(1)}, bf16[2048,128]{1,0:T(8,128)(2,1)S(1)}, u32[]{:S(2)}, u32[]{:S(2)}) collective-permute-start(bf16[2048,128]{1,0:T(8,128)(2,1)S(1)} %shard_map.57.weight_ref.refs_0_), channel_id=1, source_target_pairs={{448,0},{449,1},{450,2},{451,3},{452,4},{453,5},{454,6},{455,7},{4... | collective-permute-start | bytes 1572872 | tf_op jit(solution)/shard_map/ppermute | solution.py:308
  50.0 1.7 %collective-permute-done.4.second_ref.refs_2_ = bf16[2048,128]{1,0:T(8,128)(2,1)S(1)} collective-permute-done((bf16[2048,128]{1,0:T(8,128)(2,1)S(1)}, bf16[2048,128]{1,0:T(8,128)(2,1)S(1)}, u32[]{:S(2)}, u32[]{:S(2)}) %collective-permute-start.4) | collective-permute-done | bytes 524320 | tf_op jit(solution)/shard_map/ppermute | solution.py:303
  51.8 1.9 %collective-permute-start.5 = (bf16[2048,128]{1,0:T(8,128)(2,1)S(1)}, bf16[2048,128]{1,0:T(8,128)(2,1)S(1)}, u32[]{:S(2)}, u32[]{:S(2)}) collective-permute-start(bf16[2048,128]{1,0:T(8,128)(2,1)S(1)} %shard_map.58), channel_id=1, source_target_pairs={{16,0},{49,1},{18,2},{51,3},{20,4},{53,5},{22,6},{55,7},{24,8},{57... | collective-permute-start | bytes 1572872 | tf_op jit(solution)/shard_map/ppermute | solution.py:309
  53.7 1.2 %collective-permute-done.8.refs_3_.refs_7_.refs_5_ = bf16[2560,128]{1,0:T(8,128)(2,1)S(1)} collective-permute-done((bf16[2560,128]{1,0:T(8,128)(2,1)S(1)}, bf16[2560,128]{1,0:T(8,128)(2,1)S(1)}, u32[]{:S(2)}, u32[]{:S(2)}) %collective-permute-start.8) | collective-permute-done | bytes 655392 | tf_op jit(solution)/shard_map/ppermute | solution.py:305
  54.9 2.0 %collective-permute-done.9.refs_8_.refs_0_.refs_6_ = bf16[2560,128]{1,0:T(8,128)(2,1)S(1)} collective-permute-done((bf16[2560,128]{1,0:T(8,128)(2,1)S(1)}, bf16[2560,128]{1,0:T(8,128)(2,1)S(1)}, u32[]{:S(2)}, u32[]{:S(2)}) %collective-permute-start.9) | collective-permute-done | bytes 655392 | tf_op jit(solution)/shard_map/ppermute | solution.py:306
  57.0 2.6 %shard_map.60 = (bf16[128,1024]{1,0:T(8,128)(2,1)S(1)}, bf16[128,1024]{1,0:T(8,128)(2,1)S(1)}) custom-call(bf16[128,2048]{1,0:T(8,128)(2,1)S(1)} %get-tuple-element.19.own_ref, bf16[128,2048]{1,0:T(8,128)(2,1)S(1)} %collective-permute-done.other_ref, ...), custom_call_target="tpu_custom_call", output_to_operand_aliasing={{0}: (13, {}), {1}: (14, {})} | custom-call | flops 268435456 | bytes 2097152 | tf_op jit(solution)/shard_map/pallas_call | solution.py:266
  59.6 0.0 collective-permute-done.10.refs_1_
  59.6 1.7 %shard_map.61 = (bf16[128,1024]{1,0:T(8,128)(2,1)S(1)}, bf16[128,1024]{1,0:T(8,128)(2,1)S(1)}) custom-call(bf16[128,2048]{1,0:T(8,128)(2,1)S(1)} %get-tuple-element.19.own_ref, bf16[128,2048]{1,0:T(8,128)(2,1)S(1)} %collective-permute-done.other_ref, ...), custom_call_target="tpu_custom_call", output_to_operand_aliasing={{0}: (11, {}), {1}: (12, {})} | custom-call | flops 268435456 | bytes 2097152 | tf_op jit(solution)/shard_map/pallas_call | solution.py:266
  61.3 0.5 collective-permute-done.2.refs_0_
  61.9 1.3 %collective-permute-done.5.refs_1_ = bf16[2048,128]{1,0:T(8,128)(2,1)S(1)} collective-permute-done((bf16[2048,128]{1,0:T(8,128)(2,1)S(1)}, bf16[2048,128]{1,0:T(8,128)(2,1)S(1)}, u32[]{:S(2)}, u32[]{:S(2)}) %collective-permute-start.5) | collective-permute-done | bytes 524320 | tf_op jit(solution)/shard_map/ppermute | solution.py:309
  63.2 1.5 %shard_map.62 = (bf16[128,1024]{1,0:T(8,128)(2,1)S(1)}, bf16[128,1024]{1,0:T(8,128)(2,1)S(1)}) custom-call(bf16[128,2048]{1,0:T(8,128)(2,1)S(1)} %get-tuple-element.19.own_ref, bf16[128,2048]{1,0:T(8,128)(2,1)S(1)} %collective-permute-done.other_ref, ...), custom_call_target="tpu_custom_call", output_to_operand_aliasing={{0}: (11, {}), {1}: (12, {})} | custom-call | flops 268435456 | bytes 2097152 | tf_op jit(solution)/shard_map/pallas_call | solution.py:266
  64.8 4.9 %collective-permute-start.11 = (bf16[128,1024]{1,0:T(8,128)(2,1)S(1)}, bf16[128,1024]{1,0:T(8,128)(2,1)S(1)}, u32[]{:S(2)}, u32[]{:S(2)}) collective-permute-start(bf16[128,1024]{1,0:T(8,128)(2,1)S(1)} %get-tuple-element.32), channel_id=1, source_target_pairs={{1,0},{0,1},{3,2},{2,3},{5,4},{4,5},{7,6},{6,7},{9,8},{8,9},{11,10... | collective-permute-start | bytes 786440 | tf_op jit(solution)/shard_map/ppermute | solution.py:51
  69.7 1.1 %collective-permute-done.11.other_ref = bf16[128,1024]{1,0:T(8,128)(2,1)S(1)} collective-permute-done((bf16[128,1024]{1,0:T(8,128)(2,1)S(1)}, bf16[128,1024]{1,0:T(8,128)(2,1)S(1)}, u32[]{:S(2)}, u32[]{:S(2)}) %collective-permute-start.11) | collective-permute-done | bytes 262176 | tf_op jit(solution)/shard_map/ppermute | solution.py:51
  70.8 0.8 %shard_map.63 = bf16[128,2048]{1,0:T(8,128)(2,1)} custom-call(bf16[128,1024]{1,0:T(8,128)(2,1)S(1)} %get-tuple-element.31.mine_ref, bf16[128,1024]{1,0:T(8,128)(2,1)S(1)} %collective-permute-done.11.other_ref), custom_call_target="tpu_custom_call" | custom-call | tf_op jit(solution)/shard_map/pallas_call | solution.py:284
  (4 shorter events, 0.1 us)
Async XLA Ops:
  0.0 13.2 %collective-permute-start = (bf16[128,2048]{1,0:T(8,128)(2,1)}, bf16[128,2048]{1,0:T(8,128)(2,1)S(1)}, u32[]{:S(2)}, u32[]{:S(2)}) collective-permute-start(bf16[128,2048]{1,0:T(8,128)(2,1)} %own_hbm.1), channel_id=1, source_target_pairs={{1,0},{0,1},{3,2},{2,3},{5,4},{4,5},{7,6},{6,7},{9,8},{8,9},{11,10... | collective-permute-start | bytes 1572872 | tf_op jit(solution)/shard_map/ppermute | solution.py:51
  8.8 12.2 %collective-permute-start.1 = (bf16[2048,128]{1,0:T(8,128)(2,1)}, bf16[2048,128]{1,0:T(8,128)(2,1)S(1)}, u32[]{:S(2)}, u32[]{:S(2)}) collective-permute-start(bf16[2048,128]{1,0:T(8,128)(2,1)} %param.6), channel_id=1, source_target_pairs={{5,0},{15,1},{3,2},{11,3},{1,4},{8,5},{7,6},{14,7},{4,8},{10,9},{2... | collective-permute-start | bytes 1572872 | tf_op jit(solution)/shard_map/ppermute | solution.py:295
  10.7 0.7 copy-start
  13.6 15.6 %collective-permute-start.6 = (bf16[512,128]{1,0:T(8,128)(2,1)S(1)}, bf16[512,128]{1,0:T(8,128)(2,1)S(1)}, u32[]{:S(2)}, u32[]{:S(2)}) collective-permute-start(bf16[512,128]{1,0:T(8,128)(2,1)S(1)} %shard_map.56.refs_1_.refs_4_.refs_2_), channel_id=1, source_target_pairs={{2,0},{3,1},{4,2},{5,3},{6,4},{7,5},{8,6},{9,7},{10,8},{11,9},{12,... | collective-permute-start | bytes 393224 | tf_op jit(solution)/shard_map/ppermute | solution.py:299
  18.9 10.3 %collective-permute-start.7 = (bf16[512,128]{1,0:T(8,128)(2,1)S(1)}, bf16[512,128]{1,0:T(8,128)(2,1)S(1)}, u32[]{:S(2)}, u32[]{:S(2)}) collective-permute-start(bf16[512,128]{1,0:T(8,128)(2,1)S(1)} %shard_map.56.refs_1_.refs_4_.refs_2_), channel_id=1, source_target_pairs={{14,0},{15,1},{0,2},{1,3},{2,4},{3,5},{4,6},{5,7},{6,8},{7,9},{8,1... | collective-permute-start | bytes 393224 | tf_op jit(solution)/shard_map/ppermute | solution.py:299
  21.0 27.1 %collective-permute-start.3 = (bf16[2048,128]{1,0:T(8,128)(2,1)S(1)}, bf16[2048,128]{1,0:T(8,128)(2,1)S(1)}, u32[]{:S(2)}, u32[]{:S(2)}) collective-permute-start(bf16[2048,128]{1,0:T(8,128)(2,1)S(1)} %shard_map.57.weight_ref.refs_0_), channel_id=1, source_target_pairs={{16,0},{17,1},{18,2},{19,3},{20,4},{21,5},{22,6},{23,7},{24,8},{25... | collective-permute-start | bytes 1572872 | tf_op jit(solution)/shard_map/ppermute | solution.py:302
  27.3 24.4 %collective-permute-start.4 = (bf16[2048,128]{1,0:T(8,128)(2,1)S(1)}, bf16[2048,128]{1,0:T(8,128)(2,1)S(1)}, u32[]{:S(2)}, u32[]{:S(2)}) collective-permute-start(bf16[2048,128]{1,0:T(8,128)(2,1)S(1)} %shard_map.57.weight_ref.refs_0_), channel_id=1, source_target_pairs={{48,0},{49,1},{50,2},{51,3},{52,4},{53,5},{54,6},{55,7},{56,8},{57... | collective-permute-start | bytes 1572872 | tf_op jit(solution)/shard_map/ppermute | solution.py:303
  29.4 25.5 %collective-permute-start.8 = (bf16[2560,128]{1,0:T(8,128)(2,1)S(1)}, bf16[2560,128]{1,0:T(8,128)(2,1)S(1)}, u32[]{:S(2)}, u32[]{:S(2)}) collective-permute-start(bf16[2560,128]{1,0:T(8,128)(2,1)S(1)} %get-tuple-element.23), channel_id=1, source_target_pairs={{2,0},{3,1},{4,2},{5,3},{6,4},{7,5},{8,6},{9,7},{10,8},{11,9},{12,... | collective-permute-start | bytes 1966088 | tf_op jit(solution)/shard_map/ppermute | solution.py:305
  41.5 15.4 %collective-permute-start.9 = (bf16[2560,128]{1,0:T(8,128)(2,1)S(1)}, bf16[2560,128]{1,0:T(8,128)(2,1)S(1)}, u32[]{:S(2)}, u32[]{:S(2)}) collective-permute-start(bf16[2560,128]{1,0:T(8,128)(2,1)S(1)} %get-tuple-element.24), channel_id=1, source_target_pairs={{14,0},{15,1},{0,2},{1,3},{2,4},{3,5},{4,6},{5,7},{6,8},{7,9},{8,1... | collective-permute-start | bytes 1966088 | tf_op jit(solution)/shard_map/ppermute | solution.py:306
  43.5 16.1 %collective-permute-start.10 = (bf16[2048,128]{1,0:T(8,128)(2,1)S(1)}, bf16[2048,128]{1,0:T(8,128)(2,1)S(1)}, u32[]{:S(2)}, u32[]{:S(2)}) collective-permute-start(bf16[2048,128]{1,0:T(8,128)(2,1)S(1)} %shard_map.57.weight_ref.refs_0_), channel_id=1, source_target_pairs={{64,0},{65,1},{66,2},{67,3},{68,4},{69,5},{70,6},{71,7},{72,8},{73... | collective-permute-start | bytes 1572872 | tf_op jit(solution)/shard_map/ppermute | solution.py:307
  48.1 13.8 %collective-permute-start.2 = (bf16[2048,128]{1,0:T(8,128)(2,1)S(1)}, bf16[2048,128]{1,0:T(8,128)(2,1)S(1)}, u32[]{:S(2)}, u32[]{:S(2)}) collective-permute-start(bf16[2048,128]{1,0:T(8,128)(2,1)S(1)} %shard_map.57.weight_ref.refs_0_), channel_id=1, source_target_pairs={{448,0},{449,1},{450,2},{451,3},{452,4},{453,5},{454,6},{455,7},{4... | collective-permute-start | bytes 1572872 | tf_op jit(solution)/shard_map/ppermute | solution.py:308
  51.8 11.4 %collective-permute-start.5 = (bf16[2048,128]{1,0:T(8,128)(2,1)S(1)}, bf16[2048,128]{1,0:T(8,128)(2,1)S(1)}, u32[]{:S(2)}, u32[]{:S(2)}) collective-permute-start(bf16[2048,128]{1,0:T(8,128)(2,1)S(1)} %shard_map.58), channel_id=1, source_target_pairs={{16,0},{49,1},{18,2},{51,3},{20,4},{53,5},{22,6},{55,7},{24,8},{57... | collective-permute-start | bytes 1572872 | tf_op jit(solution)/shard_map/ppermute | solution.py:309
  64.8 6.0 %collective-permute-start.11 = (bf16[128,1024]{1,0:T(8,128)(2,1)S(1)}, bf16[128,1024]{1,0:T(8,128)(2,1)S(1)}, u32[]{:S(2)}, u32[]{:S(2)}) collective-permute-start(bf16[128,1024]{1,0:T(8,128)(2,1)S(1)} %get-tuple-element.32), channel_id=1, source_target_pairs={{1,0},{0,1},{3,2},{2,3},{5,4},{4,5},{7,6},{6,7},{9,8},{8,9},{11,10... | collective-permute-start | bytes 786440 | tf_op jit(solution)/shard_map/ppermute | solution.py:51

commit v9 on v8

--- a/solution.py
+++ b/solution.py
@@ -274,21 +274,28 @@
     )(*inputs)
 
 
-def join_kernel(mine_ref, other_ref, out_ref):
+def put_kernel(side, value_ref, *refs):
+    out_ref, sem = refs[-2:]
     y, x, z, c = place()
-    out_ref[:, pl.ds(pl.multiple_of(c * HALF, HALF), HALF)] = mine_ref[...]
-    out_ref[:, pl.ds(pl.multiple_of((1 - c) * HALF, HALF), HALF)] = other_ref[...]
-
-
-def join(keep, arrived):
-    return pl.pallas_call(
-        join_kernel,
-        grid=(1,),
-        in_specs=[pl.BlockSpec((ROWS, HALF), lambda i: (0, 0))] * 2,
-        out_specs=pl.BlockSpec((ROWS, 2 * HALF), lambda i: (0, 0)),
-        out_shape=jax.ShapeDtypeStruct((ROWS, 2 * HALF), keep.dtype),
-        compiler_params=pltpu.CompilerParams(vmem_limit_bytes=8 * 2**20),
-    )(keep, arrived)
+    core = c if side == 0 else 1 - c
+    columns = pl.ds(pl.multiple_of(core * HALF, HALF), HALF)
+    copy = pltpu.make_async_copy(value_ref, out_ref.at[:, columns], sem)
+    copy.start()
+    copy.wait()
+
+
+def put(side, value, result=None):
+    inputs = [value] if result is None else [value, result]
+    return pl.pallas_call(
+        functools.partial(put_kernel, side),
+        in_specs=[VMEM, HBM][: len(inputs)],
+        out_specs=HBM,
+        out_shape=jax.ShapeDtypeStruct((ROWS, 2 * HALF), value.dtype),
+        scratch_shapes=[pltpu.SemaphoreType.DMA],
+        input_output_aliases={} if result is None else {1: 0},
+        compiler_params=pltpu.CompilerParams(vmem_limit_bytes=2**20),
+        cost_estimate=pl.CostEstimate(flops=2**24, bytes_accessed=2**18, transcendentals=0),
+    )(*inputs)
 
 
 def body(tokens, query_weight, key_matrix, value_matrix, doc_lengths):
@@ -312,9 +319,9 @@
 
     keep = jnp.zeros((ROWS, HALF), jnp.bfloat16)
     send = jnp.zeros((ROWS, HALF), jnp.bfloat16)
-    for some in (arrivals[:4], arrivals[4:6], arrivals[6:]):
+    for some in (arrivals[:4], arrivals[4:7], arrivals[7:]):
         keep, send = some_heads(some, own, other, kv_all, row_docs, key_docs, keep, send)
-    return join(keep, swap_cores(send))
+    return put(1, swap_cores(send), put(0, keep))
 
 
 def solution(mesh):

time: 72.1 us -> 72.4 us (level)
  Pallas kernels: 9.09 us -> 9.92 us
    ppermute x1, waiting for transfers between devices: 0.01 us -> 1.94 us  [body(): front = lax.ppermute(weight, AXES, moves(lambda c: (1, 0, 0)))]
    ppermute x1, waiting for transfers between devices: 1.35 us -> 0.01 us  [body(): lax.ppermute(choose(right, left), AXES, moves(lambda c: (0, 1, 0) if c ==...]
    ppermute x2, waiting for transfers between devices: 1.14 us -> 0.41 us  [swap_cores(): lax.ppermute(value, AXES, [(flat(y, x, z, 1 - c), flat(y, x, z, c)) for y...]
  transfers between devices with their start and end apart: 12 -> 12, of which waited for: 7 -> 6; matrix products, arithmetic and copies ran while one was open for 0% -> 0% of each run, Pallas kernels for 9% -> 11%
where the time goes in v9:
time: 72.4 us; the launch traced here: 71.9 us
  starting transfers between devices  53.5 us (74%)
  Pallas kernels  9.92 us (14%)
  waiting for transfers between devices  7.41 us (10%)
    ppermute x2, starting transfers between devices, swap_cores(): lax.ppermute(value, AXES, [(flat(y, x, z, 1 - c), flat(y, x, z, c)) for y...  13.6 us
    ppermute x1, starting transfers between devices, body(): above = lax.ppermute(down, AXES, moves(lambda c: (0, 0, 1)))  12.1 us
    ppermute x2, starting transfers between devices, body(): lax.ppermute(kv, AXES, moves(lambda c, d=d: (0, 0, d)))  7.21 us
    ppermute x1, starting transfers between devices, body(): right = lax.ppermute(weight, AXES, moves(lambda c: (0, 1, 0)))  6.33 us
    pallas_call x3, Pallas kernels, some_heads(): pl.pallas_call(functools.partial(heads_kernel, tuple((shift for shift, _...  6.11 us
    ppermute x1, starting transfers between devices, body(): front = lax.ppermute(weight, AXES, moves(lambda c: (1, 0, 0)))  4.06 us
    ppermute x1, starting transfers between devices, body(): back = lax.ppermute(weight, AXES, moves(lambda c: (-1, 0, 0)))  2.43 us
    ppermute x1, waiting for transfers between devices, body(): below = lax.ppermute(up, AXES, moves(lambda c: (0, 0, -1)))  2 us
  transfers between devices with their start and end apart: 12, of which 6 were waited for; matrix products, arithmetic and copies ran while one was open for 0% of the time, Pallas kernels for 11%

profile of v9, /device:TPU:1, one launch (start us, length us, event | category | flops | bytes accessed | tf_op | source)
XLA Modules:
  0.0 71.9 jit_solution(2355293470298766994)
XLA Ops:
  0.0 8.8 %collective-permute-start = (bf16[128,2048]{1,0:T(8,128)(2,1)}, bf16[128,2048]{1,0:T(8,128)(2,1)S(1)}, u32[]{:S(2)}, u32[]{:S(2)}) collective-permute-start(bf16[128,2048]{1,0:T(8,128)(2,1)} %own_hbm.1), channel_id=1, source_target_pairs={{1,0},{0,1},{3,2},{2,3},{5,4},{4,5},{7,6},{6,7},{9,8},{8,9},{11,10... | collective-permute-start | bytes 1572872 | tf_op jit(solution)/shard_map/ppermute | solution.py:51
  8.8 1.9 %collective-permute-start.1 = (bf16[2048,128]{1,0:T(8,128)(2,1)}, bf16[2048,128]{1,0:T(8,128)(2,1)S(1)}, u32[]{:S(2)}, u32[]{:S(2)}) collective-permute-start(bf16[2048,128]{1,0:T(8,128)(2,1)} %param.6), channel_id=1, source_target_pairs={{5,0},{15,1},{3,2},{11,3},{1,4},{8,5},{7,6},{14,7},{4,8},{10,9},{2... | collective-permute-start | bytes 1572872 | tf_op jit(solution)/shard_map/ppermute | solution.py:302
  10.7 0.0 copy-start
  10.7 0.6 copy-done
  11.4 1.8 %shard_map.55 = (bf16[128,2048]{1,0:T(8,128)(2,1)S(1)}, bf16[2048,128]{1,0:T(8,128)(2,1)S(1)}, bf16[2048,128]{1,0:T(8,128)(2,1)S(1)}, bf16[512,128]{1,0:T(8,128)...) custom-call(s32[16]{0:T(128)S(1)} %copy-done, bf16[128,2048]{1,0:T(8,128)(2,1)} %own_hbm.1, ...), custom_call_target="tpu_custom_call" | custom-call | flops 134217728 | bytes 2097152 | tf_op jit(solution)/shard_map/pallas_call | solution.py:103
  13.2 0.0 collective-permute-done.other_ref
  13.2 0.4 shard_map.56.refs_1_.refs_4_.refs_3_
  13.6 5.3 %collective-permute-start.5 = (bf16[512,128]{1,0:T(8,128)(2,1)S(1)}, bf16[512,128]{1,0:T(8,128)(2,1)S(1)}, u32[]{:S(2)}, u32[]{:S(2)}) collective-permute-start(bf16[512,128]{1,0:T(8,128)(2,1)S(1)} %shard_map.56.refs_1_.refs_4_.refs_3_), channel_id=1, source_target_pairs={{2,0},{3,1},{4,2},{5,3},{6,4},{7,5},{8,6},{9,7},{10,8},{11,9},{12,... | collective-permute-start | bytes 393224 | tf_op jit(solution)/shard_map/ppermute | solution.py:306
  18.9 1.9 %collective-permute-start.6 = (bf16[512,128]{1,0:T(8,128)(2,1)S(1)}, bf16[512,128]{1,0:T(8,128)(2,1)S(1)}, u32[]{:S(2)}, u32[]{:S(2)}) collective-permute-start(bf16[512,128]{1,0:T(8,128)(2,1)S(1)} %shard_map.56.refs_1_.refs_4_.refs_3_), channel_id=1, source_target_pairs={{14,0},{15,1},{0,2},{1,3},{2,4},{3,5},{4,6},{5,7},{6,8},{7,9},{8,1... | collective-permute-start | bytes 393224 | tf_op jit(solution)/shard_map/ppermute | solution.py:306
  20.9 0.1 collective-permute-done.1.refs_0_
  21.0 6.3 %collective-permute-start.2 = (bf16[2048,128]{1,0:T(8,128)(2,1)S(1)}, bf16[2048,128]{1,0:T(8,128)(2,1)S(1)}, u32[]{:S(2)}, u32[]{:S(2)}) collective-permute-start(bf16[2048,128]{1,0:T(8,128)(2,1)S(1)} %shard_map.57.weight_ref.refs_0_), channel_id=1, source_target_pairs={{16,0},{17,1},{18,2},{19,3},{20,4},{21,5},{22,6},{23,7},{24,8},{25... | collective-permute-start | bytes 1572872 | tf_op jit(solution)/shard_map/ppermute | solution.py:309
  27.3 1.9 %collective-permute-start.3 = (bf16[2048,128]{1,0:T(8,128)(2,1)S(1)}, bf16[2048,128]{1,0:T(8,128)(2,1)S(1)}, u32[]{:S(2)}, u32[]{:S(2)}) collective-permute-start(bf16[2048,128]{1,0:T(8,128)(2,1)S(1)} %shard_map.57.weight_ref.refs_0_), channel_id=1, source_target_pairs={{48,0},{49,1},{50,2},{51,3},{52,4},{53,5},{54,6},{55,7},{56,8},{57... | collective-permute-start | bytes 1572872 | tf_op jit(solution)/shard_map/ppermute | solution.py:310
  29.3 0.0 collective-permute-done.5.above_ref.refs_5_.refs_4_.refs_2_
  29.3 0.0 collective-permute-done.6.below_ref.refs_6_.refs_5_.refs_3_
  29.3 0.1 shard_map.59
  29.4 12.1 %collective-permute-start.7 = (bf16[2560,128]{1,0:T(8,128)(2,1)S(1)}, bf16[2560,128]{1,0:T(8,128)(2,1)S(1)}, u32[]{:S(2)}, u32[]{:S(2)}) collective-permute-start(bf16[2560,128]{1,0:T(8,128)(2,1)S(1)} %get-tuple-element.23), channel_id=1, source_target_pairs={{2,0},{3,1},{4,2},{5,3},{6,4},{7,5},{8,6},{9,7},{10,8},{11,9},{12,... | collective-permute-start | bytes 1966088 | tf_op jit(solution)/shard_map/ppermute | solution.py:312
  41.5 2.0 %collective-permute-start.8 = (bf16[2560,128]{1,0:T(8,128)(2,1)S(1)}, bf16[2560,128]{1,0:T(8,128)(2,1)S(1)}, u32[]{:S(2)}, u32[]{:S(2)}) collective-permute-start(bf16[2560,128]{1,0:T(8,128)(2,1)S(1)} %get-tuple-element.24), channel_id=1, source_target_pairs={{14,0},{15,1},{0,2},{1,3},{2,4},{3,5},{4,6},{5,7},{6,8},{7,9},{8,1... | collective-permute-start | bytes 1966088 | tf_op jit(solution)/shard_map/ppermute | solution.py:313
  43.5 2.4 %collective-permute-start.10 = (bf16[2048,128]{1,0:T(8,128)(2,1)S(1)}, bf16[2048,128]{1,0:T(8,128)(2,1)S(1)}, u32[]{:S(2)}, u32[]{:S(2)}) collective-permute-start(bf16[2048,128]{1,0:T(8,128)(2,1)S(1)} %shard_map.57.weight_ref.refs_0_), channel_id=1, source_target_pairs={{448,0},{449,1},{450,2},{451,3},{452,4},{453,5},{454,6},{455,7},{4... | collective-permute-start | bytes 1572872 | tf_op jit(solution)/shard_map/ppermute | solution.py:315
  45.9 0.0 collective-permute-done.2.first_ref.refs_1_
  46.0 4.1 %collective-permute-start.9 = (bf16[2048,128]{1,0:T(8,128)(2,1)S(1)}, bf16[2048,128]{1,0:T(8,128)(2,1)S(1)}, u32[]{:S(2)}, u32[]{:S(2)}) collective-permute-start(bf16[2048,128]{1,0:T(8,128)(2,1)S(1)} %shard_map.57.weight_ref.refs_0_), channel_id=1, source_target_pairs={{64,0},{65,1},{66,2},{67,3},{68,4},{69,5},{70,6},{71,7},{72,8},{73... | collective-permute-start | bytes 1572872 | tf_op jit(solution)/shard_map/ppermute | solution.py:314
  50.0 1.7 %collective-permute-done.3.second_ref.refs_2_ = bf16[2048,128]{1,0:T(8,128)(2,1)S(1)} collective-permute-done((bf16[2048,128]{1,0:T(8,128)(2,1)S(1)}, bf16[2048,128]{1,0:T(8,128)(2,1)S(1)}, u32[]{:S(2)}, u32[]{:S(2)}) %collective-permute-start.3) | collective-permute-done | bytes 524320 | tf_op jit(solution)/shard_map/ppermute | solution.py:310
  51.8 1.9 %collective-permute-start.4 = (bf16[2048,128]{1,0:T(8,128)(2,1)S(1)}, bf16[2048,128]{1,0:T(8,128)(2,1)S(1)}, u32[]{:S(2)}, u32[]{:S(2)}) collective-permute-start(bf16[2048,128]{1,0:T(8,128)(2,1)S(1)} %shard_map.58), channel_id=1, source_target_pairs={{16,0},{49,1},{18,2},{51,3},{20,4},{53,5},{22,6},{55,7},{24,8},{57... | collective-permute-start | bytes 1572872 | tf_op jit(solution)/shard_map/ppermute | solution.py:316
  53.7 1.2 %collective-permute-done.7.refs_3_.refs_7_.refs_6_.refs_4_ = bf16[2560,128]{1,0:T(8,128)(2,1)S(1)} collective-permute-done((bf16[2560,128]{1,0:T(8,128)(2,1)S(1)}, bf16[2560,128]{1,0:T(8,128)(2,1)S(1)}, u32[]{:S(2)}, u32[]{:S(2)}) %collective-permute-start.7) | collective-permute-done | bytes 655392 | tf_op jit(solution)/shard_map/ppermute | solution.py:312
  54.9 2.0 %collective-permute-done.8.refs_8_.refs_0_.refs_7_.refs_5_ = bf16[2560,128]{1,0:T(8,128)(2,1)S(1)} collective-permute-done((bf16[2560,128]{1,0:T(8,128)(2,1)S(1)}, bf16[2560,128]{1,0:T(8,128)(2,1)S(1)}, u32[]{:S(2)}, u32[]{:S(2)}) %collective-permute-start.8) | collective-permute-done | bytes 655392 | tf_op jit(solution)/shard_map/ppermute | solution.py:313
  57.0 2.8 %shard_map.60 = (bf16[128,1024]{1,0:T(8,128)(2,1)S(1)}, bf16[128,1024]{1,0:T(8,128)(2,1)S(1)}) custom-call(bf16[128,2048]{1,0:T(8,128)(2,1)S(1)} %get-tuple-element.19.own_ref, bf16[128,2048]{1,0:T(8,128)(2,1)S(1)} %collective-permute-done.other_ref, ...), custom_call_target="tpu_custom_call", output_to_operand_aliasing={{0}: (13, {}), {1}: (14, {})} | custom-call | flops 268435456 | bytes 2097152 | tf_op jit(solution)/shard_map/pallas_call | solution.py:266
  59.8 0.0 collective-permute-done.10.refs_2_
  59.8 1.9 %collective-permute-done.9.refs_1_ = bf16[2048,128]{1,0:T(8,128)(2,1)S(1)} collective-permute-done((bf16[2048,128]{1,0:T(8,128)(2,1)S(1)}, bf16[2048,128]{1,0:T(8,128)(2,1)S(1)}, u32[]{:S(2)}, u32[]{:S(2)}) %collective-permute-start.9) | collective-permute-done | bytes 524320 | tf_op jit(solution)/shard_map/ppermute | solution.py:314
  61.7 2.2 %shard_map.61 = (bf16[128,1024]{1,0:T(8,128)(2,1)S(1)}, bf16[128,1024]{1,0:T(8,128)(2,1)S(1)}) custom-call(bf16[128,2048]{1,0:T(8,128)(2,1)S(1)} %get-tuple-element.19.own_ref, bf16[128,2048]{1,0:T(8,128)(2,1)S(1)} %collective-permute-done.other_ref, ...), custom_call_target="tpu_custom_call", output_to_operand_aliasing={{0}: (12, {}), {1}: (13, {})} | custom-call | flops 268435456 | bytes 2097152 | tf_op jit(solution)/shard_map/pallas_call | solution.py:266
  63.9 0.0 collective-permute-done.4.refs_0_
  64.0 1.1 %shard_map.62 = (bf16[128,1024]{1,0:T(8,128)(2,1)S(1)}, bf16[128,1024]{1,0:T(8,128)(2,1)S(1)}) custom-call(bf16[128,2048]{1,0:T(8,128)(2,1)S(1)} %get-tuple-element.19.own_ref, bf16[128,2048]{1,0:T(8,128)(2,1)S(1)} %collective-permute-done.other_ref, ...), custom_call_target="tpu_custom_call", output_to_operand_aliasing={{0}: (10, {}), {1}: (11, {})} | custom-call | flops 268435456 | bytes 2097152 | tf_op jit(solution)/shard_map/pallas_call | solution.py:266
  65.1 4.8 %collective-permute-start.11 = (bf16[128,1024]{1,0:T(8,128)(2,1)S(1)}, bf16[128,1024]{1,0:T(8,128)(2,1)S(1)}, u32[]{:S(2)}, u32[]{:S(2)}) collective-permute-start(bf16[128,1024]{1,0:T(8,128)(2,1)S(1)} %get-tuple-element.31), channel_id=1, source_target_pairs={{1,0},{0,1},{3,2},{2,3},{5,4},{4,5},{7,6},{6,7},{9,8},{8,9},{11,10... | collective-permute-start | bytes 786440 | tf_op jit(solution)/shard_map/ppermute | solution.py:51
  69.9 0.7 %shard_map.63.refs_0_ = bf16[128,2048]{1,0:T(8,128)(2,1)} custom-call(bf16[128,1024]{1,0:T(8,128)(2,1)S(1)} %get-tuple-element.32.value_ref), custom_call_target="tpu_custom_call" | custom-call | flops 16777216 | bytes 262144 | tf_op jit(solution)/shard_map/pallas_call | solution.py:289
  70.6 0.4 collective-permute-done.11.value_ref
  71.1 0.7 shard_map.64
  (4 shorter events, 0.1 us)
Async XLA Ops:
  0.0 13.2 %collective-permute-start = (bf16[128,2048]{1,0:T(8,128)(2,1)}, bf16[128,2048]{1,0:T(8,128)(2,1)S(1)}, u32[]{:S(2)}, u32[]{:S(2)}) collective-permute-start(bf16[128,2048]{1,0:T(8,128)(2,1)} %own_hbm.1), channel_id=1, source_target_pairs={{1,0},{0,1},{3,2},{2,3},{5,4},{4,5},{7,6},{6,7},{9,8},{8,9},{11,10... | collective-permute-start | bytes 1572872 | tf_op jit(solution)/shard_map/ppermute | solution.py:51
  8.8 12.2 %collective-permute-start.1 = (bf16[2048,128]{1,0:T(8,128)(2,1)}, bf16[2048,128]{1,0:T(8,128)(2,1)S(1)}, u32[]{:S(2)}, u32[]{:S(2)}) collective-permute-start(bf16[2048,128]{1,0:T(8,128)(2,1)} %param.6), channel_id=1, source_target_pairs={{5,0},{15,1},{3,2},{11,3},{1,4},{8,5},{7,6},{14,7},{4,8},{10,9},{2... | collective-permute-start | bytes 1572872 | tf_op jit(solution)/shard_map/ppermute | solution.py:302
  10.7 0.7 copy-start
  13.6 15.6 %collective-permute-start.5 = (bf16[512,128]{1,0:T(8,128)(2,1)S(1)}, bf16[512,128]{1,0:T(8,128)(2,1)S(1)}, u32[]{:S(2)}, u32[]{:S(2)}) collective-permute-start(bf16[512,128]{1,0:T(8,128)(2,1)S(1)} %shard_map.56.refs_1_.refs_4_.refs_3_), channel_id=1, source_target_pairs={{2,0},{3,1},{4,2},{5,3},{6,4},{7,5},{8,6},{9,7},{10,8},{11,9},{12,... | collective-permute-start | bytes 393224 | tf_op jit(solution)/shard_map/ppermute | solution.py:306
  18.9 10.3 %collective-permute-start.6 = (bf16[512,128]{1,0:T(8,128)(2,1)S(1)}, bf16[512,128]{1,0:T(8,128)(2,1)S(1)}, u32[]{:S(2)}, u32[]{:S(2)}) collective-permute-start(bf16[512,128]{1,0:T(8,128)(2,1)S(1)} %shard_map.56.refs_1_.refs_4_.refs_3_), channel_id=1, source_target_pairs={{14,0},{15,1},{0,2},{1,3},{2,4},{3,5},{4,6},{5,7},{6,8},{7,9},{8,1... | collective-permute-start | bytes 393224 | tf_op jit(solution)/shard_map/ppermute | solution.py:306
  21.0 25.0 %collective-permute-start.2 = (bf16[2048,128]{1,0:T(8,128)(2,1)S(1)}, bf16[2048,128]{1,0:T(8,128)(2,1)S(1)}, u32[]{:S(2)}, u32[]{:S(2)}) collective-permute-start(bf16[2048,128]{1,0:T(8,128)(2,1)S(1)} %shard_map.57.weight_ref.refs_0_), channel_id=1, source_target_pairs={{16,0},{17,1},{18,2},{19,3},{20,4},{21,5},{22,6},{23,7},{24,8},{25... | collective-permute-start | bytes 1572872 | tf_op jit(solution)/shard_map/ppermute | solution.py:309
  27.3 24.4 %collective-permute-start.3 = (bf16[2048,128]{1,0:T(8,128)(2,1)S(1)}, bf16[2048,128]{1,0:T(8,128)(2,1)S(1)}, u32[]{:S(2)}, u32[]{:S(2)}) collective-permute-start(bf16[2048,128]{1,0:T(8,128)(2,1)S(1)} %shard_map.57.weight_ref.refs_0_), channel_id=1, source_target_pairs={{48,0},{49,1},{50,2},{51,3},{52,4},{53,5},{54,6},{55,7},{56,8},{57... | collective-permute-start | bytes 1572872 | tf_op jit(solution)/shard_map/ppermute | solution.py:310
  29.4 25.5 %collective-permute-start.7 = (bf16[2560,128]{1,0:T(8,128)(2,1)S(1)}, bf16[2560,128]{1,0:T(8,128)(2,1)S(1)}, u32[]{:S(2)}, u32[]{:S(2)}) collective-permute-start(bf16[2560,128]{1,0:T(8,128)(2,1)S(1)} %get-tuple-element.23), channel_id=1, source_target_pairs={{2,0},{3,1},{4,2},{5,3},{6,4},{7,5},{8,6},{9,7},{10,8},{11,9},{12,... | collective-permute-start | bytes 1966088 | tf_op jit(solution)/shard_map/ppermute | solution.py:312
  41.5 15.4 %collective-permute-start.8 = (bf16[2560,128]{1,0:T(8,128)(2,1)S(1)}, bf16[2560,128]{1,0:T(8,128)(2,1)S(1)}, u32[]{:S(2)}, u32[]{:S(2)}) collective-permute-start(bf16[2560,128]{1,0:T(8,128)(2,1)S(1)} %get-tuple-element.24), channel_id=1, source_target_pairs={{14,0},{15,1},{0,2},{1,3},{2,4},{3,5},{4,6},{5,7},{6,8},{7,9},{8,1... | collective-permute-start | bytes 1966088 | tf_op jit(solution)/shard_map/ppermute | solution.py:313
  43.5 16.3 %collective-permute-start.10 = (bf16[2048,128]{1,0:T(8,128)(2,1)S(1)}, bf16[2048,128]{1,0:T(8,128)(2,1)S(1)}, u32[]{:S(2)}, u32[]{:S(2)}) collective-permute-start(bf16[2048,128]{1,0:T(8,128)(2,1)S(1)} %shard_map.57.weight_ref.refs_0_), channel_id=1, source_target_pairs={{448,0},{449,1},{450,2},{451,3},{452,4},{453,5},{454,6},{455,7},{4... | collective-permute-start | bytes 1572872 | tf_op jit(solution)/shard_map/ppermute | solution.py:315
  46.0 15.8 %collective-permute-start.9 = (bf16[2048,128]{1,0:T(8,128)(2,1)S(1)}, bf16[2048,128]{1,0:T(8,128)(2,1)S(1)}, u32[]{:S(2)}, u32[]{:S(2)}) collective-permute-start(bf16[2048,128]{1,0:T(8,128)(2,1)S(1)} %shard_map.57.weight_ref.refs_0_), channel_id=1, source_target_pairs={{64,0},{65,1},{66,2},{67,3},{68,4},{69,5},{70,6},{71,7},{72,8},{73... | collective-permute-start | bytes 1572872 | tf_op jit(solution)/shard_map/ppermute | solution.py:314
  51.8 12.1 %collective-permute-start.4 = (bf16[2048,128]{1,0:T(8,128)(2,1)S(1)}, bf16[2048,128]{1,0:T(8,128)(2,1)S(1)}, u32[]{:S(2)}, u32[]{:S(2)}) collective-permute-start(bf16[2048,128]{1,0:T(8,128)(2,1)S(1)} %shard_map.58), channel_id=1, source_target_pairs={{16,0},{49,1},{18,2},{51,3},{20,4},{53,5},{22,6},{55,7},{24,8},{57... | collective-permute-start | bytes 1572872 | tf_op jit(solution)/shard_map/ppermute | solution.py:316
  65.1 6.0 %collective-permute-start.11 = (bf16[128,1024]{1,0:T(8,128)(2,1)S(1)}, bf16[128,1024]{1,0:T(8,128)(2,1)S(1)}, u32[]{:S(2)}, u32[]{:S(2)}) collective-permute-start(bf16[128,1024]{1,0:T(8,128)(2,1)S(1)} %get-tuple-element.31), channel_id=1, source_target_pairs={{1,0},{0,1},{3,2},{2,3},{5,4},{4,5},{7,6},{6,7},{9,8},{8,9},{11,10... | collective-permute-start | bytes 786440 | tf_op jit(solution)/shard_map/ppermute | solution.py:51

commit v10 on v9

--- a/solution.py
+++ b/solution.py
@@ -17,7 +17,7 @@
 
 YS, XS, ZS, CORES = 8, 4, 8, 2
 AXES = ("dp", "ctx")
-ORDER = ((5, 3, 1, 7, 4, 2, 0, 6), (7, 3, 0, 6, 2, 4, 1, 5))
+ORDER = ((0, 6, 4, 2, 1, 7, 5, 3), (1, 7, 5, 3, 0, 6, 4, 2))
 AROUND = (0, 1, -1, 2, -2)
 VMEM = pl.BlockSpec(memory_space=pltpu.VMEM)
 HBM = pl.BlockSpec(memory_space=pltpu.HBM)
@@ -319,7 +319,7 @@
 
     keep = jnp.zeros((ROWS, HALF), jnp.bfloat16)
     send = jnp.zeros((ROWS, HALF), jnp.bfloat16)
-    for some in (arrivals[:4], arrivals[4:7], arrivals[7:]):
+    for some in (arrivals[:4], arrivals[4:6], arrivals[6:]):
         keep, send = some_heads(some, own, other, kv_all, row_docs, key_docs, keep, send)
     return put(1, swap_cores(send), put(0, keep))
 

time: 72.4 us -> 73.8 us (1.019)
  waiting for transfers between devices: 7.41 us -> 20.2 us
  starting transfers between devices: 53.5 us -> 42.3 us
    ppermute x1, waiting for transfers between devices: 0.12 us -> 13.3 us  [body(): weight = lax.ppermute(query_weight, AXES, first_moves())]
    ppermute x1, starting transfers between devices: 12.1 us -> 2.24 us  [body(): above = lax.ppermute(down, AXES, moves(lambda c: (0, 0, 1)))]
    ppermute x1, starting transfers between devices: 6.33 us -> 1.96 us  [body(): right = lax.ppermute(weight, AXES, moves(lambda c: (0, 1, 0)))]
    ppermute x1, starting transfers between devices: 1.92 us -> 5.16 us  [body(): weight = lax.ppermute(query_weight, AXES, first_moves())]
    ppermute x1, starting transfers between devices: 4.06 us -> 1.92 us  [body(): front = lax.ppermute(weight, AXES, moves(lambda c: (1, 0, 0)))]
    ppermute x1, waiting for transfers between devices: 1.18 us -> 3.17 us  [body(): above = lax.ppermute(down, AXES, moves(lambda c: (0, 0, 1)))]
    ppermute x1, waiting for transfers between devices: 1.94 us -> 0.01 us  [body(): front = lax.ppermute(weight, AXES, moves(lambda c: (1, 0, 0)))]
    ppermute x2, starting transfers between devices: 7.21 us -> 5.28 us  [body(): lax.ppermute(kv, AXES, moves(lambda c, d=d: (0, 0, d)))]
  transfers between devices with their start and end apart: 12 -> 12, of which waited for: 6 -> 6; matrix products, arithmetic and copies ran while one was open for 0% -> 0% of each run, Pallas kernels for 11% -> 10%
where the time goes in v10:
time: 73.8 us; the launch traced here: 73.3 us
  starting transfers between devices  42.3 us (57%)
  waiting for transfers between devices  20.2 us (27%)
  Pallas kernels  9.71 us (13%)
    ppermute x2, starting transfers between devices, swap_cores(): lax.ppermute(value, AXES, [(flat(y, x, z, 1 - c), flat(y, x, z, c)) for y...  13.9 us
    ppermute x1, waiting for transfers between devices, body(): weight = lax.ppermute(query_weight, AXES, first_moves())  13.3 us
    pallas_call x3, Pallas kernels, some_heads(): pl.pallas_call(functools.partial(heads_kernel, tuple((shift for shift, _...  5.88 us
    ppermute x2, starting transfers between devices, body(): lax.ppermute(kv, AXES, moves(lambda c, d=d: (0, 0, d)))  5.28 us
    ppermute x1, starting transfers between devices, body(): weight = lax.ppermute(query_weight, AXES, first_moves())  5.16 us
    ppermute x1, starting transfers between devices, body(): lax.ppermute(choose(right, left), AXES, moves(lambda c: (0, 1, 0) if c ==...  3.52 us
    ppermute x1, starting transfers between devices, body(): left = lax.ppermute(weight, AXES, moves(lambda c: (0, -1, 0)))  3.31 us
    ppermute x1, waiting for transfers between devices, body(): above = lax.ppermute(down, AXES, moves(lambda c: (0, 0, 1)))  3.17 us
  transfers between devices with their start and end apart: 12, of which 6 were waited for; matrix products, arithmetic and copies ran while one was open for 0% of the time, Pallas kernels for 10%

profile of v10, /device:TPU:1, one launch (start us, length us, event | category | flops | bytes accessed | tf_op | source)
XLA Modules:
  0.0 73.3 jit_solution(12272922595901843553)
XLA Ops:
  0.0 8.8 %collective-permute-start = (bf16[128,2048]{1,0:T(8,128)(2,1)}, bf16[128,2048]{1,0:T(8,128)(2,1)S(1)}, u32[]{:S(2)}, u32[]{:S(2)}) collective-permute-start(bf16[128,2048]{1,0:T(8,128)(2,1)} %own_hbm.1), channel_id=1, source_target_pairs={{1,0},{0,1},{3,2},{2,3},{5,4},{4,5},{7,6},{6,7},{9,8},{8,9},{11,10... | collective-permute-start | bytes 1572872 | tf_op jit(solution)/shard_map/ppermute | solution.py:51
  8.8 5.2 %collective-permute-start.1 = (bf16[2048,128]{1,0:T(8,128)(2,1)}, bf16[2048,128]{1,0:T(8,128)(2,1)S(1)}, u32[]{:S(2)}, u32[]{:S(2)}) collective-permute-start(bf16[2048,128]{1,0:T(8,128)(2,1)} %param.6), channel_id=1, source_target_pairs={{0,0},{9,1},{6,2},{15,3},{4,4},{13,5},{2,6},{11,7},{1,8},{8,9},{7,... | collective-permute-start | bytes 1572872 | tf_op jit(solution)/shard_map/ppermute | solution.py:302
  13.9 0.0 copy-start
  14.0 0.6 copy-done
  14.6 1.8 %shard_map.55 = (bf16[128,2048]{1,0:T(8,128)(2,1)S(1)}, bf16[2048,128]{1,0:T(8,128)(2,1)S(1)}, bf16[2048,128]{1,0:T(8,128)(2,1)S(1)}, bf16[512,128]{1,0:T(8,128)...) custom-call(s32[16]{0:T(128)S(1)} %copy-done, bf16[128,2048]{1,0:T(8,128)(2,1)} %own_hbm.1, ...), custom_call_target="tpu_custom_call" | custom-call | flops 134217728 | bytes 2097152 | tf_op jit(solution)/shard_map/pallas_call | solution.py:103
  16.4 0.0 collective-permute-done.other_ref
  16.4 0.4 shard_map.56.refs_1_.refs_4_.refs_2_
  16.9 2.1 %collective-permute-start.6 = (bf16[512,128]{1,0:T(8,128)(2,1)S(1)}, bf16[512,128]{1,0:T(8,128)(2,1)S(1)}, u32[]{:S(2)}, u32[]{:S(2)}) collective-permute-start(bf16[512,128]{1,0:T(8,128)(2,1)S(1)} %shard_map.56.refs_1_.refs_4_.refs_2_), channel_id=1, source_target_pairs={{2,0},{3,1},{4,2},{5,3},{6,4},{7,5},{8,6},{9,7},{10,8},{11,9},{12,... | collective-permute-start | bytes 393224 | tf_op jit(solution)/shard_map/ppermute | solution.py:306
  18.9 3.2 %collective-permute-start.7 = (bf16[512,128]{1,0:T(8,128)(2,1)S(1)}, bf16[512,128]{1,0:T(8,128)(2,1)S(1)}, u32[]{:S(2)}, u32[]{:S(2)}) collective-permute-start(bf16[512,128]{1,0:T(8,128)(2,1)S(1)} %shard_map.56.refs_1_.refs_4_.refs_2_), channel_id=1, source_target_pairs={{14,0},{15,1},{0,2},{1,3},{2,4},{3,5},{4,6},{5,7},{6,8},{7,9},{8,1... | collective-permute-start | bytes 393224 | tf_op jit(solution)/shard_map/ppermute | solution.py:306
  22.2 13.3 %collective-permute-done.1.refs_0_ = bf16[2048,128]{1,0:T(8,128)(2,1)S(1)} collective-permute-done((bf16[2048,128]{1,0:T(8,128)(2,1)}, bf16[2048,128]{1,0:T(8,128)(2,1)S(1)}, u32[]{:S(2)}, u32[]{:S(2)}) %collective-permute-start.1) | collective-permute-done | bytes 524320 | tf_op jit(solution)/shard_map/ppermute | solution.py:302
  35.5 2.0 %collective-permute-start.3 = (bf16[2048,128]{1,0:T(8,128)(2,1)S(1)}, bf16[2048,128]{1,0:T(8,128)(2,1)S(1)}, u32[]{:S(2)}, u32[]{:S(2)}) collective-permute-start(bf16[2048,128]{1,0:T(8,128)(2,1)S(1)} %shard_map.57.weight_ref.refs_0_), channel_id=1, source_target_pairs={{16,0},{17,1},{18,2},{19,3},{20,4},{21,5},{22,6},{23,7},{24,8},{25... | collective-permute-start | bytes 1572872 | tf_op jit(solution)/shard_map/ppermute | solution.py:309
  37.4 3.3 %collective-permute-start.4 = (bf16[2048,128]{1,0:T(8,128)(2,1)S(1)}, bf16[2048,128]{1,0:T(8,128)(2,1)S(1)}, u32[]{:S(2)}, u32[]{:S(2)}) collective-permute-start(bf16[2048,128]{1,0:T(8,128)(2,1)S(1)} %shard_map.57.weight_ref.refs_0_), channel_id=1, source_target_pairs={{48,0},{49,1},{50,2},{51,3},{52,4},{53,5},{54,6},{55,7},{56,8},{57... | collective-permute-start | bytes 1572872 | tf_op jit(solution)/shard_map/ppermute | solution.py:310
  40.8 0.0 collective-permute-done.6.above_ref.refs_5_.refs_3_
  40.8 0.0 collective-permute-done.7.below_ref.refs_6_.refs_4_
  40.8 0.1 shard_map.59
  40.9 2.2 %collective-permute-start.8 = (bf16[2560,128]{1,0:T(8,128)(2,1)S(1)}, bf16[2560,128]{1,0:T(8,128)(2,1)S(1)}, u32[]{:S(2)}, u32[]{:S(2)}) collective-permute-start(bf16[2560,128]{1,0:T(8,128)(2,1)S(1)} %get-tuple-element.23), channel_id=1, source_target_pairs={{2,0},{3,1},{4,2},{5,3},{6,4},{7,5},{8,6},{9,7},{10,8},{11,9},{12,... | collective-permute-start | bytes 1966088 | tf_op jit(solution)/shard_map/ppermute | solution.py:312
  43.1 3.0 %collective-permute-start.9 = (bf16[2560,128]{1,0:T(8,128)(2,1)S(1)}, bf16[2560,128]{1,0:T(8,128)(2,1)S(1)}, u32[]{:S(2)}, u32[]{:S(2)}) collective-permute-start(bf16[2560,128]{1,0:T(8,128)(2,1)S(1)} %get-tuple-element.24), channel_id=1, source_target_pairs={{14,0},{15,1},{0,2},{1,3},{2,4},{3,5},{4,6},{5,7},{6,8},{7,9},{8,1... | collective-permute-start | bytes 1966088 | tf_op jit(solution)/shard_map/ppermute | solution.py:313
  46.2 1.9 %collective-permute-start.10 = (bf16[2048,128]{1,0:T(8,128)(2,1)S(1)}, bf16[2048,128]{1,0:T(8,128)(2,1)S(1)}, u32[]{:S(2)}, u32[]{:S(2)}) collective-permute-start(bf16[2048,128]{1,0:T(8,128)(2,1)S(1)} %shard_map.57.weight_ref.refs_0_), channel_id=1, source_target_pairs={{64,0},{65,1},{66,2},{67,3},{68,4},{69,5},{70,6},{71,7},{72,8},{73... | collective-permute-start | bytes 1572872 | tf_op jit(solution)/shard_map/ppermute | solution.py:314
  48.1 1.4 %collective-permute-done.3.first_ref.refs_1_ = bf16[2048,128]{1,0:T(8,128)(2,1)S(1)} collective-permute-done((bf16[2048,128]{1,0:T(8,128)(2,1)S(1)}, bf16[2048,128]{1,0:T(8,128)(2,1)S(1)}, u32[]{:S(2)}, u32[]{:S(2)}) %collective-permute-start.3) | collective-permute-done | bytes 524320 | tf_op jit(solution)/shard_map/ppermute | solution.py:309
  49.5 2.0 %collective-permute-start.2 = (bf16[2048,128]{1,0:T(8,128)(2,1)S(1)}, bf16[2048,128]{1,0:T(8,128)(2,1)S(1)}, u32[]{:S(2)}, u32[]{:S(2)}) collective-permute-start(bf16[2048,128]{1,0:T(8,128)(2,1)S(1)} %shard_map.57.weight_ref.refs_0_), channel_id=1, source_target_pairs={{448,0},{449,1},{450,2},{451,3},{452,4},{453,5},{454,6},{455,7},{4... | collective-permute-start | bytes 1572872 | tf_op jit(solution)/shard_map/ppermute | solution.py:315
  51.5 0.0 collective-permute-done.4.second_ref.refs_2_
  51.5 0.1 shard_map.58
  51.6 3.5 %collective-permute-start.5 = (bf16[2048,128]{1,0:T(8,128)(2,1)S(1)}, bf16[2048,128]{1,0:T(8,128)(2,1)S(1)}, u32[]{:S(2)}, u32[]{:S(2)}) collective-permute-start(bf16[2048,128]{1,0:T(8,128)(2,1)S(1)} %shard_map.58), channel_id=1, source_target_pairs={{16,0},{49,1},{18,2},{51,3},{20,4},{53,5},{22,6},{55,7},{24,8},{57... | collective-permute-start | bytes 1572872 | tf_op jit(solution)/shard_map/ppermute | solution.py:316
  55.1 3.2 %collective-permute-done.8.refs_3_.refs_7_.refs_5_ = bf16[2560,128]{1,0:T(8,128)(2,1)S(1)} collective-permute-done((bf16[2560,128]{1,0:T(8,128)(2,1)S(1)}, bf16[2560,128]{1,0:T(8,128)(2,1)S(1)}, u32[]{:S(2)}, u32[]{:S(2)}) %collective-permute-start.8) | collective-permute-done | bytes 655392 | tf_op jit(solution)/shard_map/ppermute | solution.py:312
  58.2 1.8 %collective-permute-done.9.refs_8_.refs_0_.refs_6_ = bf16[2560,128]{1,0:T(8,128)(2,1)S(1)} collective-permute-done((bf16[2560,128]{1,0:T(8,128)(2,1)S(1)}, bf16[2560,128]{1,0:T(8,128)(2,1)S(1)}, u32[]{:S(2)}, u32[]{:S(2)}) %collective-permute-start.9) | collective-permute-done | bytes 655392 | tf_op jit(solution)/shard_map/ppermute | solution.py:313
  60.1 2.6 %shard_map.60 = (bf16[128,1024]{1,0:T(8,128)(2,1)S(1)}, bf16[128,1024]{1,0:T(8,128)(2,1)S(1)}) custom-call(bf16[128,2048]{1,0:T(8,128)(2,1)S(1)} %get-tuple-element.19.own_ref, bf16[128,2048]{1,0:T(8,128)(2,1)S(1)} %collective-permute-done.other_ref, ...), custom_call_target="tpu_custom_call", output_to_operand_aliasing={{0}: (13, {}), {1}: (14, {})} | custom-call | flops 268435456 | bytes 2097152 | tf_op jit(solution)/shard_map/pallas_call | solution.py:266
  62.7 0.0 collective-permute-done.10.refs_1_
  62.8 1.7 %shard_map.61 = (bf16[128,1024]{1,0:T(8,128)(2,1)S(1)}, bf16[128,1024]{1,0:T(8,128)(2,1)S(1)}) custom-call(bf16[128,2048]{1,0:T(8,128)(2,1)S(1)} %get-tuple-element.19.own_ref, bf16[128,2048]{1,0:T(8,128)(2,1)S(1)} %collective-permute-done.other_ref, ...), custom_call_target="tpu_custom_call", output_to_operand_aliasing={{0}: (11, {}), {1}: (12, {})} | custom-call | flops 268435456 | bytes 2097152 | tf_op jit(solution)/shard_map/pallas_call | solution.py:266
  64.5 0.1 collective-permute-done.2.refs_0_
  64.6 0.0 collective-permute-done.5.refs_1_
  64.6 1.5 %shard_map.62 = (bf16[128,1024]{1,0:T(8,128)(2,1)S(1)}, bf16[128,1024]{1,0:T(8,128)(2,1)S(1)}) custom-call(bf16[128,2048]{1,0:T(8,128)(2,1)S(1)} %get-tuple-element.19.own_ref, bf16[128,2048]{1,0:T(8,128)(2,1)S(1)} %collective-permute-done.other_ref, ...), custom_call_target="tpu_custom_call", output_to_operand_aliasing={{0}: (11, {}), {1}: (12, {})} | custom-call | flops 268435456 | bytes 2097152 | tf_op jit(solution)/shard_map/pallas_call | solution.py:266
  66.1 5.1 %collective-permute-start.11 = (bf16[128,1024]{1,0:T(8,128)(2,1)S(1)}, bf16[128,1024]{1,0:T(8,128)(2,1)S(1)}, u32[]{:S(2)}, u32[]{:S(2)}) collective-permute-start(bf16[128,1024]{1,0:T(8,128)(2,1)S(1)} %get-tuple-element.31), channel_id=1, source_target_pairs={{1,0},{0,1},{3,2},{2,3},{5,4},{4,5},{7,6},{6,7},{9,8},{8,9},{11,10... | collective-permute-start | bytes 786440 | tf_op jit(solution)/shard_map/ppermute | solution.py:51
  71.3 0.7 shard_map.63.refs_0_
  72.0 0.4 collective-permute-done.11.value_ref
  72.4 0.7 shard_map.64
  (3 shorter events, 0.0 us)
Async XLA Ops:
  0.0 16.4 %collective-permute-start = (bf16[128,2048]{1,0:T(8,128)(2,1)}, bf16[128,2048]{1,0:T(8,128)(2,1)S(1)}, u32[]{:S(2)}, u32[]{:S(2)}) collective-permute-start(bf16[128,2048]{1,0:T(8,128)(2,1)} %own_hbm.1), channel_id=1, source_target_pairs={{1,0},{0,1},{3,2},{2,3},{5,4},{4,5},{7,6},{6,7},{9,8},{8,9},{11,10... | collective-permute-start | bytes 1572872 | tf_op jit(solution)/shard_map/ppermute | solution.py:51
  8.8 26.7 %collective-permute-start.1 = (bf16[2048,128]{1,0:T(8,128)(2,1)}, bf16[2048,128]{1,0:T(8,128)(2,1)S(1)}, u32[]{:S(2)}, u32[]{:S(2)}) collective-permute-start(bf16[2048,128]{1,0:T(8,128)(2,1)} %param.6), channel_id=1, source_target_pairs={{0,0},{9,1},{6,2},{15,3},{4,4},{13,5},{2,6},{11,7},{1,8},{8,9},{7,... | collective-permute-start | bytes 1572872 | tf_op jit(solution)/shard_map/ppermute | solution.py:302
  13.9 0.7 copy-start
  16.9 23.9 %collective-permute-start.6 = (bf16[512,128]{1,0:T(8,128)(2,1)S(1)}, bf16[512,128]{1,0:T(8,128)(2,1)S(1)}, u32[]{:S(2)}, u32[]{:S(2)}) collective-permute-start(bf16[512,128]{1,0:T(8,128)(2,1)S(1)} %shard_map.56.refs_1_.refs_4_.refs_2_), channel_id=1, source_target_pairs={{2,0},{3,1},{4,2},{5,3},{6,4},{7,5},{8,6},{9,7},{10,8},{11,9},{12,... | collective-permute-start | bytes 393224 | tf_op jit(solution)/shard_map/ppermute | solution.py:306
  18.9 21.8 %collective-permute-start.7 = (bf16[512,128]{1,0:T(8,128)(2,1)S(1)}, bf16[512,128]{1,0:T(8,128)(2,1)S(1)}, u32[]{:S(2)}, u32[]{:S(2)}) collective-permute-start(bf16[512,128]{1,0:T(8,128)(2,1)S(1)} %shard_map.56.refs_1_.refs_4_.refs_2_), channel_id=1, source_target_pairs={{14,0},{15,1},{0,2},{1,3},{2,4},{3,5},{4,6},{5,7},{6,8},{7,9},{8,1... | collective-permute-start | bytes 393224 | tf_op jit(solution)/shard_map/ppermute | solution.py:306
  35.5 14.0 %collective-permute-start.3 = (bf16[2048,128]{1,0:T(8,128)(2,1)S(1)}, bf16[2048,128]{1,0:T(8,128)(2,1)S(1)}, u32[]{:S(2)}, u32[]{:S(2)}) collective-permute-start(bf16[2048,128]{1,0:T(8,128)(2,1)S(1)} %shard_map.57.weight_ref.refs_0_), channel_id=1, source_target_pairs={{16,0},{17,1},{18,2},{19,3},{20,4},{21,5},{22,6},{23,7},{24,8},{25... | collective-permute-start | bytes 1572872 | tf_op jit(solution)/shard_map/ppermute | solution.py:309
  37.4 14.0 %collective-permute-start.4 = (bf16[2048,128]{1,0:T(8,128)(2,1)S(1)}, bf16[2048,128]{1,0:T(8,128)(2,1)S(1)}, u32[]{:S(2)}, u32[]{:S(2)}) collective-permute-start(bf16[2048,128]{1,0:T(8,128)(2,1)S(1)} %shard_map.57.weight_ref.refs_0_), channel_id=1, source_target_pairs={{48,0},{49,1},{50,2},{51,3},{52,4},{53,5},{54,6},{55,7},{56,8},{57... | collective-permute-start | bytes 1572872 | tf_op jit(solution)/shard_map/ppermute | solution.py:310
  40.9 17.4 %collective-permute-start.8 = (bf16[2560,128]{1,0:T(8,128)(2,1)S(1)}, bf16[2560,128]{1,0:T(8,128)(2,1)S(1)}, u32[]{:S(2)}, u32[]{:S(2)}) collective-permute-start(bf16[2560,128]{1,0:T(8,128)(2,1)S(1)} %get-tuple-element.23), channel_id=1, source_target_pairs={{2,0},{3,1},{4,2},{5,3},{6,4},{7,5},{8,6},{9,7},{10,8},{11,9},{12,... | collective-permute-start | bytes 1966088 | tf_op jit(solution)/shard_map/ppermute | solution.py:312
  43.1 16.9 %collective-permute-start.9 = (bf16[2560,128]{1,0:T(8,128)(2,1)S(1)}, bf16[2560,128]{1,0:T(8,128)(2,1)S(1)}, u32[]{:S(2)}, u32[]{:S(2)}) collective-permute-start(bf16[2560,128]{1,0:T(8,128)(2,1)S(1)} %get-tuple-element.24), channel_id=1, source_target_pairs={{14,0},{15,1},{0,2},{1,3},{2,4},{3,5},{4,6},{5,7},{6,8},{7,9},{8,1... | collective-permute-start | bytes 1966088 | tf_op jit(solution)/shard_map/ppermute | solution.py:313
  46.2 16.6 %collective-permute-start.10 = (bf16[2048,128]{1,0:T(8,128)(2,1)S(1)}, bf16[2048,128]{1,0:T(8,128)(2,1)S(1)}, u32[]{:S(2)}, u32[]{:S(2)}) collective-permute-start(bf16[2048,128]{1,0:T(8,128)(2,1)S(1)} %shard_map.57.weight_ref.refs_0_), channel_id=1, source_target_pairs={{64,0},{65,1},{66,2},{67,3},{68,4},{69,5},{70,6},{71,7},{72,8},{73... | collective-permute-start | bytes 1572872 | tf_op jit(solution)/shard_map/ppermute | solution.py:314
  49.5 15.1 %collective-permute-start.2 = (bf16[2048,128]{1,0:T(8,128)(2,1)S(1)}, bf16[2048,128]{1,0:T(8,128)(2,1)S(1)}, u32[]{:S(2)}, u32[]{:S(2)}) collective-permute-start(bf16[2048,128]{1,0:T(8,128)(2,1)S(1)} %shard_map.57.weight_ref.refs_0_), channel_id=1, source_target_pairs={{448,0},{449,1},{450,2},{451,3},{452,4},{453,5},{454,6},{455,7},{4... | collective-permute-start | bytes 1572872 | tf_op jit(solution)/shard_map/ppermute | solution.py:315
  51.6 13.0 %collective-permute-start.5 = (bf16[2048,128]{1,0:T(8,128)(2,1)S(1)}, bf16[2048,128]{1,0:T(8,128)(2,1)S(1)}, u32[]{:S(2)}, u32[]{:S(2)}) collective-permute-start(bf16[2048,128]{1,0:T(8,128)(2,1)S(1)} %shard_map.58), channel_id=1, source_target_pairs={{16,0},{49,1},{18,2},{51,3},{20,4},{53,5},{22,6},{55,7},{24,8},{57... | collective-permute-start | bytes 1572872 | tf_op jit(solution)/shard_map/ppermute | solution.py:316
  66.1 6.3 %collective-permute-start.11 = (bf16[128,1024]{1,0:T(8,128)(2,1)S(1)}, bf16[128,1024]{1,0:T(8,128)(2,1)S(1)}, u32[]{:S(2)}, u32[]{:S(2)}) collective-permute-start(bf16[128,1024]{1,0:T(8,128)(2,1)S(1)} %get-tuple-element.31), channel_id=1, source_target_pairs={{1,0},{0,1},{3,2},{2,3},{5,4},{4,5},{7,6},{6,7},{9,8},{8,9},{11,10... | collective-permute-start | bytes 786440 | tf_op jit(solution)/shard_map/ppermute | solution.py:51

commit v11 on v10

--- a/solution.py
+++ b/solution.py
@@ -17,7 +17,7 @@
 
 YS, XS, ZS, CORES = 8, 4, 8, 2
 AXES = ("dp", "ctx")
-ORDER = ((0, 6, 4, 2, 1, 7, 5, 3), (1, 7, 5, 3, 0, 6, 4, 2))
+ORDER = ((5, 3, 1, 7, 4, 2, 0, 6), (7, 3, 0, 6, 2, 4, 1, 5))
 AROUND = (0, 1, -1, 2, -2)
 VMEM = pl.BlockSpec(memory_space=pltpu.VMEM)
 HBM = pl.BlockSpec(memory_space=pltpu.HBM)

time: 73.8 us -> 72.1 us (0.977)
  waiting for transfers between devices: 20.2 us -> 7.36 us
  starting transfers between devices: 42.3 us -> 53.6 us
    ppermute x1, waiting for transfers between devices: 13.3 us -> 0.12 us  [body(): weight = lax.ppermute(query_weight, AXES, first_moves())]
    ppermute x1, starting transfers between devices: 2.24 us -> 12.1 us  [body(): above = lax.ppermute(down, AXES, moves(lambda c: (0, 0, 1)))]
    ppermute x1, starting transfers between devices: 1.96 us -> 6.33 us  [body(): right = lax.ppermute(weight, AXES, moves(lambda c: (0, 1, 0)))]
    ppermute x1, starting transfers between devices: 5.16 us -> 1.92 us  [body(): weight = lax.ppermute(query_weight, AXES, first_moves())]
    ppermute x1, starting transfers between devices: 1.92 us -> 4.57 us  [body(): front = lax.ppermute(weight, AXES, moves(lambda c: (1, 0, 0)))]
    ppermute x1, waiting for transfers between devices: 3.17 us -> 1.18 us  [body(): above = lax.ppermute(down, AXES, moves(lambda c: (0, 0, 1)))]
    ppermute x2, starting transfers between devices: 5.28 us -> 7.21 us  [body(): lax.ppermute(kv, AXES, moves(lambda c, d=d: (0, 0, d)))]
    ppermute x1, waiting for transfers between devices: 0.01 us -> 1.75 us  [body(): left = lax.ppermute(weight, AXES, moves(lambda c: (0, -1, 0)))]
  transfers between devices with their start and end apart: 12 -> 12, of which waited for: 6 -> 7; matrix products, arithmetic and copies ran while one was open for 0% -> 0% of each run, Pallas kernels for 10% -> 10%
where the time goes in v11:
time: 72.1 us; the launch traced here: 71.7 us
  starting transfers between devices  53.6 us (74%)
  Pallas kernels  9.68 us (13%)
  waiting for transfers between devices  7.36 us (10%)
    ppermute x2, starting transfers between devices, swap_cores(): lax.ppermute(value, AXES, [(flat(y, x, z, 1 - c), flat(y, x, z, c)) for y...  13.7 us
    ppermute x1, starting transfers between devices, body(): above = lax.ppermute(down, AXES, moves(lambda c: (0, 0, 1)))  12.1 us
    ppermute x2, starting transfers between devices, body(): lax.ppermute(kv, AXES, moves(lambda c, d=d: (0, 0, d)))  7.21 us
    ppermute x1, starting transfers between devices, body(): right = lax.ppermute(weight, AXES, moves(lambda c: (0, 1, 0)))  6.33 us
    pallas_call x3, Pallas kernels, some_heads(): pl.pallas_call(functools.partial(heads_kernel, tuple((shift for shift, _...  5.88 us
    ppermute x1, starting transfers between devices, body(): front = lax.ppermute(weight, AXES, moves(lambda c: (1, 0, 0)))  4.57 us
    ppermute x1, waiting for transfers between devices, body(): below = lax.ppermute(up, AXES, moves(lambda c: (0, 0, -1)))  2 us
    ppermute x1, starting transfers between devices, body(): below = lax.ppermute(up, AXES, moves(lambda c: (0, 0, -1)))  1.98 us
  transfers between devices with their start and end apart: 12, of which 7 were waited for; matrix products, arithmetic and copies ran while one was open for 0% of the time, Pallas kernels for 10%

profile of v11, /device:TPU:1, one launch (start us, length us, event | category | flops | bytes accessed | tf_op | source)
XLA Modules:
  0.0 71.7 jit_solution(1679433832079302869)
XLA Ops:
  0.0 8.8 %collective-permute-start = (bf16[128,2048]{1,0:T(8,128)(2,1)}, bf16[128,2048]{1,0:T(8,128)(2,1)S(1)}, u32[]{:S(2)}, u32[]{:S(2)}) collective-permute-start(bf16[128,2048]{1,0:T(8,128)(2,1)} %own_hbm.1), channel_id=1, source_target_pairs={{1,0},{0,1},{3,2},{2,3},{5,4},{4,5},{7,6},{6,7},{9,8},{8,9},{11,10... | collective-permute-start | bytes 1572872 | tf_op jit(solution)/shard_map/ppermute | solution.py:51
  8.8 1.9 %collective-permute-start.1 = (bf16[2048,128]{1,0:T(8,128)(2,1)}, bf16[2048,128]{1,0:T(8,128)(2,1)S(1)}, u32[]{:S(2)}, u32[]{:S(2)}) collective-permute-start(bf16[2048,128]{1,0:T(8,128)(2,1)} %param.6), channel_id=1, source_target_pairs={{5,0},{15,1},{3,2},{11,3},{1,4},{8,5},{7,6},{14,7},{4,8},{10,9},{2... | collective-permute-start | bytes 1572872 | tf_op jit(solution)/shard_map/ppermute | solution.py:302
  10.7 0.0 copy-start
  10.7 0.6 copy-done
  11.4 1.8 %shard_map.55 = (bf16[128,2048]{1,0:T(8,128)(2,1)S(1)}, bf16[2048,128]{1,0:T(8,128)(2,1)S(1)}, bf16[2048,128]{1,0:T(8,128)(2,1)S(1)}, bf16[512,128]{1,0:T(8,128)...) custom-call(s32[16]{0:T(128)S(1)} %copy-done, bf16[128,2048]{1,0:T(8,128)(2,1)} %own_hbm.1, ...), custom_call_target="tpu_custom_call" | custom-call | flops 134217728 | bytes 2097152 | tf_op jit(solution)/shard_map/pallas_call | solution.py:103
  13.2 0.0 collective-permute-done.other_ref
  13.2 0.4 shard_map.56.refs_1_.refs_4_.refs_2_
  13.6 5.3 %collective-permute-start.6 = (bf16[512,128]{1,0:T(8,128)(2,1)S(1)}, bf16[512,128]{1,0:T(8,128)(2,1)S(1)}, u32[]{:S(2)}, u32[]{:S(2)}) collective-permute-start(bf16[512,128]{1,0:T(8,128)(2,1)S(1)} %shard_map.56.refs_1_.refs_4_.refs_2_), channel_id=1, source_target_pairs={{2,0},{3,1},{4,2},{5,3},{6,4},{7,5},{8,6},{9,7},{10,8},{11,9},{12,... | collective-permute-start | bytes 393224 | tf_op jit(solution)/shard_map/ppermute | solution.py:306
  18.9 1.9 %collective-permute-start.7 = (bf16[512,128]{1,0:T(8,128)(2,1)S(1)}, bf16[512,128]{1,0:T(8,128)(2,1)S(1)}, u32[]{:S(2)}, u32[]{:S(2)}) collective-permute-start(bf16[512,128]{1,0:T(8,128)(2,1)S(1)} %shard_map.56.refs_1_.refs_4_.refs_2_), channel_id=1, source_target_pairs={{14,0},{15,1},{0,2},{1,3},{2,4},{3,5},{4,6},{5,7},{6,8},{7,9},{8,1... | collective-permute-start | bytes 393224 | tf_op jit(solution)/shard_map/ppermute | solution.py:306
  20.9 0.1 collective-permute-done.1.refs_0_
  21.0 6.3 %collective-permute-start.3 = (bf16[2048,128]{1,0:T(8,128)(2,1)S(1)}, bf16[2048,128]{1,0:T(8,128)(2,1)S(1)}, u32[]{:S(2)}, u32[]{:S(2)}) collective-permute-start(bf16[2048,128]{1,0:T(8,128)(2,1)S(1)} %shard_map.57.weight_ref.refs_0_), channel_id=1, source_target_pairs={{16,0},{17,1},{18,2},{19,3},{20,4},{21,5},{22,6},{23,7},{24,8},{25... | collective-permute-start | bytes 1572872 | tf_op jit(solution)/shard_map/ppermute | solution.py:309
  27.3 1.9 %collective-permute-start.4 = (bf16[2048,128]{1,0:T(8,128)(2,1)S(1)}, bf16[2048,128]{1,0:T(8,128)(2,1)S(1)}, u32[]{:S(2)}, u32[]{:S(2)}) collective-permute-start(bf16[2048,128]{1,0:T(8,128)(2,1)S(1)} %shard_map.57.weight_ref.refs_0_), channel_id=1, source_target_pairs={{48,0},{49,1},{50,2},{51,3},{52,4},{53,5},{54,6},{55,7},{56,8},{57... | collective-permute-start | bytes 1572872 | tf_op jit(solution)/shard_map/ppermute | solution.py:310
  29.3 0.0 collective-permute-done.6.above_ref.refs_5_.refs_3_
  29.3 0.0 collective-permute-done.7.below_ref.refs_6_.refs_4_
  29.3 0.1 shard_map.59
  29.4 12.1 %collective-permute-start.8 = (bf16[2560,128]{1,0:T(8,128)(2,1)S(1)}, bf16[2560,128]{1,0:T(8,128)(2,1)S(1)}, u32[]{:S(2)}, u32[]{:S(2)}) collective-permute-start(bf16[2560,128]{1,0:T(8,128)(2,1)S(1)} %get-tuple-element.23), channel_id=1, source_target_pairs={{2,0},{3,1},{4,2},{5,3},{6,4},{7,5},{8,6},{9,7},{10,8},{11,9},{12,... | collective-permute-start | bytes 1966088 | tf_op jit(solution)/shard_map/ppermute | solution.py:312
  41.5 2.0 %collective-permute-start.9 = (bf16[2560,128]{1,0:T(8,128)(2,1)S(1)}, bf16[2560,128]{1,0:T(8,128)(2,1)S(1)}, u32[]{:S(2)}, u32[]{:S(2)}) collective-permute-start(bf16[2560,128]{1,0:T(8,128)(2,1)S(1)} %get-tuple-element.24), channel_id=1, source_target_pairs={{14,0},{15,1},{0,2},{1,3},{2,4},{3,5},{4,6},{5,7},{6,8},{7,9},{8,1... | collective-permute-start | bytes 1966088 | tf_op jit(solution)/shard_map/ppermute | solution.py:313
  43.5 4.6 %collective-permute-start.10 = (bf16[2048,128]{1,0:T(8,128)(2,1)S(1)}, bf16[2048,128]{1,0:T(8,128)(2,1)S(1)}, u32[]{:S(2)}, u32[]{:S(2)}) collective-permute-start(bf16[2048,128]{1,0:T(8,128)(2,1)S(1)} %shard_map.57.weight_ref.refs_0_), channel_id=1, source_target_pairs={{64,0},{65,1},{66,2},{67,3},{68,4},{69,5},{70,6},{71,7},{72,8},{73... | collective-permute-start | bytes 1572872 | tf_op jit(solution)/shard_map/ppermute | solution.py:314
  48.1 0.0 collective-permute-done.3.first_ref.refs_1_
  48.1 1.9 %collective-permute-start.2 = (bf16[2048,128]{1,0:T(8,128)(2,1)S(1)}, bf16[2048,128]{1,0:T(8,128)(2,1)S(1)}, u32[]{:S(2)}, u32[]{:S(2)}) collective-permute-start(bf16[2048,128]{1,0:T(8,128)(2,1)S(1)} %shard_map.57.weight_ref.refs_0_), channel_id=1, source_target_pairs={{448,0},{449,1},{450,2},{451,3},{452,4},{453,5},{454,6},{455,7},{4... | collective-permute-start | bytes 1572872 | tf_op jit(solution)/shard_map/ppermute | solution.py:315
  50.0 1.7 %collective-permute-done.4.second_ref.refs_2_ = bf16[2048,128]{1,0:T(8,128)(2,1)S(1)} collective-permute-done((bf16[2048,128]{1,0:T(8,128)(2,1)S(1)}, bf16[2048,128]{1,0:T(8,128)(2,1)S(1)}, u32[]{:S(2)}, u32[]{:S(2)}) %collective-permute-start.4) | collective-permute-done | bytes 524320 | tf_op jit(solution)/shard_map/ppermute | solution.py:310
  51.8 1.9 %collective-permute-start.5 = (bf16[2048,128]{1,0:T(8,128)(2,1)S(1)}, bf16[2048,128]{1,0:T(8,128)(2,1)S(1)}, u32[]{:S(2)}, u32[]{:S(2)}) collective-permute-start(bf16[2048,128]{1,0:T(8,128)(2,1)S(1)} %shard_map.58), channel_id=1, source_target_pairs={{16,0},{49,1},{18,2},{51,3},{20,4},{53,5},{22,6},{55,7},{24,8},{57... | collective-permute-start | bytes 1572872 | tf_op jit(solution)/shard_map/ppermute | solution.py:316
  53.7 1.2 %collective-permute-done.8.refs_3_.refs_7_.refs_5_ = bf16[2560,128]{1,0:T(8,128)(2,1)S(1)} collective-permute-done((bf16[2560,128]{1,0:T(8,128)(2,1)S(1)}, bf16[2560,128]{1,0:T(8,128)(2,1)S(1)}, u32[]{:S(2)}, u32[]{:S(2)}) %collective-permute-start.8) | collective-permute-done | bytes 655392 | tf_op jit(solution)/shard_map/ppermute | solution.py:312
  54.9 2.0 %collective-permute-done.9.refs_8_.refs_0_.refs_6_ = bf16[2560,128]{1,0:T(8,128)(2,1)S(1)} collective-permute-done((bf16[2560,128]{1,0:T(8,128)(2,1)S(1)}, bf16[2560,128]{1,0:T(8,128)(2,1)S(1)}, u32[]{:S(2)}, u32[]{:S(2)}) %collective-permute-start.9) | collective-permute-done | bytes 655392 | tf_op jit(solution)/shard_map/ppermute | solution.py:313
  57.0 2.6 %shard_map.60 = (bf16[128,1024]{1,0:T(8,128)(2,1)S(1)}, bf16[128,1024]{1,0:T(8,128)(2,1)S(1)}) custom-call(bf16[128,2048]{1,0:T(8,128)(2,1)S(1)} %get-tuple-element.19.own_ref, bf16[128,2048]{1,0:T(8,128)(2,1)S(1)} %collective-permute-done.other_ref, ...), custom_call_target="tpu_custom_call", output_to_operand_aliasing={{0}: (13, {}), {1}: (14, {})} | custom-call | flops 268435456 | bytes 2097152 | tf_op jit(solution)/shard_map/pallas_call | solution.py:266
  59.6 0.0 collective-permute-done.10.refs_1_
  59.6 1.7 %shard_map.61 = (bf16[128,1024]{1,0:T(8,128)(2,1)S(1)}, bf16[128,1024]{1,0:T(8,128)(2,1)S(1)}) custom-call(bf16[128,2048]{1,0:T(8,128)(2,1)S(1)} %get-tuple-element.19.own_ref, bf16[128,2048]{1,0:T(8,128)(2,1)S(1)} %collective-permute-done.other_ref, ...), custom_call_target="tpu_custom_call", output_to_operand_aliasing={{0}: (11, {}), {1}: (12, {})} | custom-call | flops 268435456 | bytes 2097152 | tf_op jit(solution)/shard_map/pallas_call | solution.py:266
  61.3 0.5 collective-permute-done.2.refs_0_
  61.9 1.3 %collective-permute-done.5.refs_1_ = bf16[2048,128]{1,0:T(8,128)(2,1)S(1)} collective-permute-done((bf16[2048,128]{1,0:T(8,128)(2,1)S(1)}, bf16[2048,128]{1,0:T(8,128)(2,1)S(1)}, u32[]{:S(2)}, u32[]{:S(2)}) %collective-permute-start.5) | collective-permute-done | bytes 524320 | tf_op jit(solution)/shard_map/ppermute | solution.py:316
  63.2 1.5 %shard_map.62 = (bf16[128,1024]{1,0:T(8,128)(2,1)S(1)}, bf16[128,1024]{1,0:T(8,128)(2,1)S(1)}) custom-call(bf16[128,2048]{1,0:T(8,128)(2,1)S(1)} %get-tuple-element.19.own_ref, bf16[128,2048]{1,0:T(8,128)(2,1)S(1)} %collective-permute-done.other_ref, ...), custom_call_target="tpu_custom_call", output_to_operand_aliasing={{0}: (11, {}), {1}: (12, {})} | custom-call | flops 268435456 | bytes 2097152 | tf_op jit(solution)/shard_map/pallas_call | solution.py:266
  64.8 4.9 %collective-permute-start.11 = (bf16[128,1024]{1,0:T(8,128)(2,1)S(1)}, bf16[128,1024]{1,0:T(8,128)(2,1)S(1)}, u32[]{:S(2)}, u32[]{:S(2)}) collective-permute-start(bf16[128,1024]{1,0:T(8,128)(2,1)S(1)} %get-tuple-element.31), channel_id=1, source_target_pairs={{1,0},{0,1},{3,2},{2,3},{5,4},{4,5},{7,6},{6,7},{9,8},{8,9},{11,10... | collective-permute-start | bytes 786440 | tf_op jit(solution)/shard_map/ppermute | solution.py:51
  69.7 0.7 %shard_map.63.refs_0_ = bf16[128,2048]{1,0:T(8,128)(2,1)} custom-call(bf16[128,1024]{1,0:T(8,128)(2,1)S(1)} %get-tuple-element.32.value_ref), custom_call_target="tpu_custom_call" | custom-call | flops 16777216 | bytes 262144 | tf_op jit(solution)/shard_map/pallas_call | solution.py:289
  70.4 0.4 collective-permute-done.11.value_ref
  70.8 0.7 shard_map.64
  (4 shorter events, 0.1 us)
Async XLA Ops:
  0.0 13.2 %collective-permute-start = (bf16[128,2048]{1,0:T(8,128)(2,1)}, bf16[128,2048]{1,0:T(8,128)(2,1)S(1)}, u32[]{:S(2)}, u32[]{:S(2)}) collective-permute-start(bf16[128,2048]{1,0:T(8,128)(2,1)} %own_hbm.1), channel_id=1, source_target_pairs={{1,0},{0,1},{3,2},{2,3},{5,4},{4,5},{7,6},{6,7},{9,8},{8,9},{11,10... | collective-permute-start | bytes 1572872 | tf_op jit(solution)/shard_map/ppermute | solution.py:51
  8.8 12.2 %collective-permute-start.1 = (bf16[2048,128]{1,0:T(8,128)(2,1)}, bf16[2048,128]{1,0:T(8,128)(2,1)S(1)}, u32[]{:S(2)}, u32[]{:S(2)}) collective-permute-start(bf16[2048,128]{1,0:T(8,128)(2,1)} %param.6), channel_id=1, source_target_pairs={{5,0},{15,1},{3,2},{11,3},{1,4},{8,5},{7,6},{14,7},{4,8},{10,9},{2... | collective-permute-start | bytes 1572872 | tf_op jit(solution)/shard_map/ppermute | solution.py:302
  10.7 0.7 copy-start
  13.6 15.6 %collective-permute-start.6 = (bf16[512,128]{1,0:T(8,128)(2,1)S(1)}, bf16[512,128]{1,0:T(8,128)(2,1)S(1)}, u32[]{:S(2)}, u32[]{:S(2)}) collective-permute-start(bf16[512,128]{1,0:T(8,128)(2,1)S(1)} %shard_map.56.refs_1_.refs_4_.refs_2_), channel_id=1, source_target_pairs={{2,0},{3,1},{4,2},{5,3},{6,4},{7,5},{8,6},{9,7},{10,8},{11,9},{12,... | collective-permute-start | bytes 393224 | tf_op jit(solution)/shard_map/ppermute | solution.py:306
  18.9 10.3 %collective-permute-start.7 = (bf16[512,128]{1,0:T(8,128)(2,1)S(1)}, bf16[512,128]{1,0:T(8,128)(2,1)S(1)}, u32[]{:S(2)}, u32[]{:S(2)}) collective-permute-start(bf16[512,128]{1,0:T(8,128)(2,1)S(1)} %shard_map.56.refs_1_.refs_4_.refs_2_), channel_id=1, source_target_pairs={{14,0},{15,1},{0,2},{1,3},{2,4},{3,5},{4,6},{5,7},{6,8},{7,9},{8,1... | collective-permute-start | bytes 393224 | tf_op jit(solution)/shard_map/ppermute | solution.py:306
  21.0 27.1 %collective-permute-start.3 = (bf16[2048,128]{1,0:T(8,128)(2,1)S(1)}, bf16[2048,128]{1,0:T(8,128)(2,1)S(1)}, u32[]{:S(2)}, u32[]{:S(2)}) collective-permute-start(bf16[2048,128]{1,0:T(8,128)(2,1)S(1)} %shard_map.57.weight_ref.refs_0_), channel_id=1, source_target_pairs={{16,0},{17,1},{18,2},{19,3},{20,4},{21,5},{22,6},{23,7},{24,8},{25... | collective-permute-start | bytes 1572872 | tf_op jit(solution)/shard_map/ppermute | solution.py:309
  27.3 24.4 %collective-permute-start.4 = (bf16[2048,128]{1,0:T(8,128)(2,1)S(1)}, bf16[2048,128]{1,0:T(8,128)(2,1)S(1)}, u32[]{:S(2)}, u32[]{:S(2)}) collective-permute-start(bf16[2048,128]{1,0:T(8,128)(2,1)S(1)} %shard_map.57.weight_ref.refs_0_), channel_id=1, source_target_pairs={{48,0},{49,1},{50,2},{51,3},{52,4},{53,5},{54,6},{55,7},{56,8},{57... | collective-permute-start | bytes 1572872 | tf_op jit(solution)/shard_map/ppermute | solution.py:310
  29.4 25.5 %collective-permute-start.8 = (bf16[2560,128]{1,0:T(8,128)(2,1)S(1)}, bf16[2560,128]{1,0:T(8,128)(2,1)S(1)}, u32[]{:S(2)}, u32[]{:S(2)}) collective-permute-start(bf16[2560,128]{1,0:T(8,128)(2,1)S(1)} %get-tuple-element.23), channel_id=1, source_target_pairs={{2,0},{3,1},{4,2},{5,3},{6,4},{7,5},{8,6},{9,7},{10,8},{11,9},{12,... | collective-permute-start | bytes 1966088 | tf_op jit(solution)/shard_map/ppermute | solution.py:312
  41.5 15.4 %collective-permute-start.9 = (bf16[2560,128]{1,0:T(8,128)(2,1)S(1)}, bf16[2560,128]{1,0:T(8,128)(2,1)S(1)}, u32[]{:S(2)}, u32[]{:S(2)}) collective-permute-start(bf16[2560,128]{1,0:T(8,128)(2,1)S(1)} %get-tuple-element.24), channel_id=1, source_target_pairs={{14,0},{15,1},{0,2},{1,3},{2,4},{3,5},{4,6},{5,7},{6,8},{7,9},{8,1... | collective-permute-start | bytes 1966088 | tf_op jit(solution)/shard_map/ppermute | solution.py:313
  43.5 16.1 %collective-permute-start.10 = (bf16[2048,128]{1,0:T(8,128)(2,1)S(1)}, bf16[2048,128]{1,0:T(8,128)(2,1)S(1)}, u32[]{:S(2)}, u32[]{:S(2)}) collective-permute-start(bf16[2048,128]{1,0:T(8,128)(2,1)S(1)} %shard_map.57.weight_ref.refs_0_), channel_id=1, source_target_pairs={{64,0},{65,1},{66,2},{67,3},{68,4},{69,5},{70,6},{71,7},{72,8},{73... | collective-permute-start | bytes 1572872 | tf_op jit(solution)/shard_map/ppermute | solution.py:314
  48.1 13.8 %collective-permute-start.2 = (bf16[2048,128]{1,0:T(8,128)(2,1)S(1)}, bf16[2048,128]{1,0:T(8,128)(2,1)S(1)}, u32[]{:S(2)}, u32[]{:S(2)}) collective-permute-start(bf16[2048,128]{1,0:T(8,128)(2,1)S(1)} %shard_map.57.weight_ref.refs_0_), channel_id=1, source_target_pairs={{448,0},{449,1},{450,2},{451,3},{452,4},{453,5},{454,6},{455,7},{4... | collective-permute-start | bytes 1572872 | tf_op jit(solution)/shard_map/ppermute | solution.py:315
  51.8 11.4 %collective-permute-start.5 = (bf16[2048,128]{1,0:T(8,128)(2,1)S(1)}, bf16[2048,128]{1,0:T(8,128)(2,1)S(1)}, u32[]{:S(2)}, u32[]{:S(2)}) collective-permute-start(bf16[2048,128]{1,0:T(8,128)(2,1)S(1)} %shard_map.58), channel_id=1, source_target_pairs={{16,0},{49,1},{18,2},{51,3},{20,4},{53,5},{22,6},{55,7},{24,8},{57... | collective-permute-start | bytes 1572872 | tf_op jit(solution)/shard_map/ppermute | solution.py:316
  64.8 6.0 %collective-permute-start.11 = (bf16[128,1024]{1,0:T(8,128)(2,1)S(1)}, bf16[128,1024]{1,0:T(8,128)(2,1)S(1)}, u32[]{:S(2)}, u32[]{:S(2)}) collective-permute-start(bf16[128,1024]{1,0:T(8,128)(2,1)S(1)} %get-tuple-element.31), channel_id=1, source_target_pairs={{1,0},{0,1},{3,2},{2,3},{5,4},{4,5},{7,6},{6,7},{9,8},{8,9},{11,10... | collective-permute-start | bytes 786440 | tf_op jit(solution)/shard_map/ppermute | solution.py:51
